TPU v7x, 128 devices: a whole 4x4x4 slice. The times are simulated.
128 devices in a mesh: sector: 32 (over y, z, core), blk: 4 (over x).
Axes of the slice: x: 4, y: 4, z: 4, core: 2. Of those that a mesh axis runs over, the one named last changes fastest.
Arguments:
- visible_feats: bfloat16 [262144, 256], P(('sector', 'blk')), may hold values from -6 to 6
- grid_pos: bfloat16 [256, 32, 40, 256], P('sector', 'blk'), may hold values from -6 to 6
- vis_cells: int32 [262144], P(('sector', 'blk')), may hold values from 0 to 2559, as said below
- vis_count: int32 [128], P(('sector', 'blk')), may hold values from 512 to 2048, as said below
- owner: int32 [262144], P(('sector', 'blk')), may hold values from 0 to 127, as said below
- slot: int32 [262144], P(('sector', 'blk')), may hold values from 0 to 1023, as said below
- window: int32 [128, 1024], P(('sector', 'blk')), may hold values from 0 to 3, never falling along the last dimension, each value on 1 to 512 neighbouring positions
- enc_gain1: float32 [256], replicated, may hold values from 0.1 to 1.9
- attn_in: bfloat16 [256, 768], replicated, may hold values from -2 to 2
- attn_out: bfloat16 [256, 256], replicated, may hold values from -0.375 to 0.375
- enc_gain2: float32 [256], replicated, may hold values from 0.1 to 1.9
- mlp_in: bfloat16 [256, 1024], replicated, may hold values from -0.375 to 0.375
- mlp_out: bfloat16 [1024, 256], replicated, may hold values from -0.1875 to 0.1875
- mask_token: float32 [256], replicated, may hold values from -4 to 4
- dec_gain: float32 [256], replicated, may hold values from 0.1 to 1.9
- conv_weight: bfloat16 [27, 256, 256], replicated, may hold values from -0.078125 to 0.078125
- conv_bias: float32 [256], replicated, may hold values from -3 to 3
Outputs:
- decoded: bfloat16 [256, 32, 40, 256], P('sector', 'blk')
Inputs may be any that keep to these rules, and one draw needn't show every extreme that they name: `vis_cells`: the first vis_count entries of a device are distinct cells of its block; later entries are ignored. `vis_count`: counts sum to 131072; 2048 is reached on some device in every draw. On each device the owners of the live entries never fall along the list; each device sends each owner 1 to 18 live entries, and 18 is reached by some pair in every draw. Later entries are ignored. `slot`: the live entries of all devices sent to one owner take each of its 1024 slots exactly once. Later entries are ignored.
All inputs are finite; a program needn't handle non-finite values.
Results may differ from a plain program's by a relative error of at most 0.0062.
Values may be sent and summed in bfloat16 or wider, within the bound.
No kernel may reach another device: no remote copies, remote signals or barrier semaphores. Data moves between devices by JAX's collectives and lax.ppermute only.
A program may use at most 128 MiB of HBM per device.

v0:
```python
import functools

import jax
import jax.numpy as jnp
from jax import lax
from jax.experimental import pallas as pl
from jax.experimental.pallas import tpu as pltpu
from jax.sharding import PartitionSpec as P

HEAD_DIM = 32
EPSILON = 1e-05
F32 = jnp.float32
BF16 = jnp.bfloat16
I32 = jnp.int32
CAP = 18
MSG = 40
VMEM_LIMIT = 48 * 2**20


def iota(shape, dim):
    return lax.broadcasted_iota(I32, shape, dim)


def one_hot(mask):
    return jnp.where(mask, 1.0, 0.0).astype(BF16)


def dot(a, b):
    return jnp.dot(a, b, preferred_element_type=F32)


def dot_nt(a, b):
    return lax.dot_general(a, b, (((1,), (1,)), ((), ())), preferred_element_type=F32)


def eye_mask(n):
    return iota((n, n), 0) == iota((n, n), 1)


def layer_norm(values, gain_vec):
    center = values - jnp.mean(values, axis=-1, keepdims=True)
    spread = jnp.mean(center * center, axis=-1, keepdims=True)
    return center * lax.rsqrt(spread + EPSILON) * gain_vec


def gelu(x):
    return 0.5 * x * (1.0 + jnp.tanh(0.7978845608028654 * (x + 0.044715 * (x * x * x))))


def send_kernel(
    count_ref, cells_ref, owner_ref, slot_ref, vis_ref, pos_ref,
    msg_ref, starts_ref,
    left_scr, right_scr, meta_scr, starts_smem, sem,
):
    entries = cells_ref.shape[1]
    owners = msg_ref.shape[0]
    cell_total = pos_ref.shape[0]
    entry = iota((1, entries), 1)
    live = entry < count_ref[0]
    owner = jnp.where(live, owner_ref[...], owners)
    owner_id = iota((owners, entries), 0)
    start_col = jnp.sum(jnp.where(owner < owner_id, 1.0, 0.0), axis=1, keepdims=True)
    start_row = jnp.sum(jnp.where(eye_mask(owners), start_col, 0.0), axis=0, keepdims=True)
    starts_ref[...] = start_row.astype(I32)
    copy = pltpu.make_async_copy(starts_ref, starts_smem, sem)
    copy.start()
    belongs = owner == owner_id
    first = jnp.sum(jnp.where(belongs, start_col, 0.0), axis=0, keepdims=True)
    within = jnp.where(live, entry - first.astype(I32), 64)
    cells = cells_ref[...]
    slots = slot_ref[...]
    parts = jnp.concatenate(
        [cells >> 6, cells & 63, slots >> 5, slots & 31, within, within, within, within], axis=0
    ).astype(F32).astype(BF16)
    eye = one_hot(eye_mask(128))
    lane = iota((128, 128), 1)
    cell_cols = []
    meta_parts = []
    for b in range(entries // 128):
        turned = dot_nt(eye, parts[:, b * 128 : (b + 1) * 128])
        cell_cols.append((turned[:, 0:1] * 64.0 + turned[:, 1:2]).astype(I32))
        place = turned[:, 4:5].astype(I32)
        meta_parts.append(
            jnp.where(
                lane == place,
                turned[:, 2:3] + 1.0,
                jnp.where(lane == place + 32, turned[:, 3:4], 0.0),
            ).astype(BF16)
        )
    meta_scr[...] = dot(one_hot(belongs), jnp.concatenate(meta_parts, axis=0))
    step = 512
    for b in range(entries // step):
        col = jnp.concatenate(cell_cols[b * step // 128 : (b + 1) * step // 128], axis=0)
        pick = one_hot(iota((step, cell_total), 1) == col)
        rows = vis_ref[b * step : (b + 1) * step, :].astype(F32) + dot(pick, pos_ref[...])
        rows = rows.astype(BF16).astype(F32)
        left_scr[b * step : (b + 1) * step, :] = rows[:, 0:128]
        right_scr[b * step : (b + 1) * step, :] = rows[:, 128:256]
    left_scr[entries:, :] = jnp.zeros((left_scr.shape[0] - entries, 128), F32)
    right_scr[entries:, :] = jnp.zeros((right_scr.shape[0] - entries, 128), F32)
    copy.wait()
    sub = iota((8, 128), 0)

    def emit(o, carry):
        start = starts_smem[0, o]
        msg_ref[o, 0:16, :] = left_scr[pl.ds(start, 16), :].astype(BF16)
        msg_ref[o, 16:32, :] = right_scr[pl.ds(start, 16), :].astype(BF16)
        left = left_scr[pl.ds(start + 16, 8), :]
        right = pltpu.roll(right_scr[pl.ds(start + 16, 8), :], 2, 0)
        last = jnp.where(sub < 2, left, jnp.where(sub < 4, right, meta_scr[pl.ds(o, 1), :]))
        msg_ref[o, 32:40, :] = last.astype(BF16)
        return carry

    lax.fori_loop(0, owners, emit, 0, unroll=4)


def send_rows(vis_count, cells, owner, slot, vis, pos, owners):
    entries = vis.shape[0]
    vmem = pl.BlockSpec(memory_space=pltpu.VMEM)
    smem = pl.BlockSpec(memory_space=pltpu.SMEM)
    return pl.pallas_call(
        send_kernel,
        out_shape=(
            jax.ShapeDtypeStruct((owners, MSG, 128), BF16),
            jax.ShapeDtypeStruct((1, owners), I32),
        ),
        in_specs=[smem, vmem, vmem, vmem, vmem, vmem],
        out_specs=(vmem, vmem),
        scratch_shapes=[
            pltpu.VMEM((entries + 24, 128), F32),
            pltpu.VMEM((entries + 24, 128), F32),
            pltpu.VMEM((owners, 128), F32),
            pltpu.SMEM((1, owners), I32),
            pltpu.SemaphoreType.DMA,
        ],
        compiler_params=pltpu.CompilerParams(vmem_limit_bytes=VMEM_LIMIT),
        name="send_rows",
    )(vis_count, cells, owner, slot, vis, pos)


def owner_kernel(
    span_ref, msg_ref, window_ref, gain1_ref, attn_in_ref, attn_out_ref, gain2_ref,
    mlp_in_ref, mlp_out_ref,
    back_ref,
    tail_scr, q_scr, k_scr, v_scr, att_scr,
):
    owners = msg_ref.shape[0]
    rows = window_ref.shape[1]
    channels = attn_out_ref.shape[0]
    head_count = channels // HEAD_DIM
    full = 16 * owners
    tail_scr[...] = msg_ref[:, 32:40, :].astype(F32).reshape(owners * 8, 128)

    def tail(j):
        return tail_scr[pl.ds(j, owners, stride=8), :]

    meta = tail(4).astype(BF16)
    place = iota((128, full), 0)
    inner = iota((128, full), 1) & 15
    spread = (
        jnp.where(place == inner, 32.0, 0.0) + jnp.where(place == inner + 32, 1.0, 0.0)
    ).astype(BF16)
    wide = dot(meta, spread)
    of_sender = (iota((owners, full), 1) >> 4) == iota((owners, full), 0)
    slot_full = jnp.sum(jnp.where(of_sender, wide, 0.0), axis=0, keepdims=True) - 32.0
    eye = eye_mask(owners)
    meta32 = meta.astype(F32)
    tail_cols = [meta32[:, j : j + 1] * 32.0 + meta32[:, j + 32 : j + 33] - 32.0 for j in (16, 17)]
    tail_slots = [jnp.sum(jnp.where(eye, c, 0.0), axis=0, keepdims=True) for c in tail_cols]
    slot_row = jnp.concatenate([slot_full] + tail_slots, axis=1).astype(I32)
    left = msg_ref[:, 0:16, :].reshape(full, 128)
    right = msg_ref[:, 16:32, :].reshape(full, 128)
    main = jnp.concatenate([left, right], axis=1)
    rest = jnp.concatenate(
        [
            jnp.concatenate([tail(0), tail(2)], axis=1),
            jnp.concatenate([tail(1), tail(3)], axis=1),
        ],
        axis=0,
    ).astype(BF16)
    step = 256
    for b in range(rows // step):
        sel = one_hot(slot_row == iota((step, slot_row.shape[1]), 0) + b * step)
        x = dot(sel[:, :full], main) + dot(sel[:, full:], rest)
        att_scr[b * step : (b + 1) * step, :] = x
        normed = layer_norm(x, gain1_ref[...]).astype(BF16)
        projected = dot(normed, attn_in_ref[...]).astype(BF16)
        q_scr[b * step : (b + 1) * step, :] = projected[:, :channels]
        k_scr[b * step : (b + 1) * step, :] = projected[:, channels : 2 * channels]
        v_scr[b * step : (b + 1) * step, :] = projected[:, 2 * channels :]
    q_step = 128
    win_row = window_ref[...].astype(F32)
    head_of_lane = iota((q_step, channels), 1) // HEAD_DIM
    eye_q = eye_mask(q_step)

    def attend(qi, key_count, key_start):
        q_rows = pl.ds(pl.multiple_of(qi * q_step, q_step), q_step)
        k_rows = pl.ds(key_start, key_count)
        q = q_scr[q_rows, :]
        keys = k_scr[k_rows, :]
        vals = v_scr[k_rows, :]
        q_win = window_ref[:, q_rows].astype(F32)
        q_win = jnp.sum(jnp.where(eye_q, q_win, 0.0), axis=1, keepdims=True)
        k_win = window_ref[:, k_rows].astype(F32)
        bias = jnp.where(q_win == k_win, 0.0, -jnp.inf)
        total = jnp.zeros((q_step, channels), F32)
        for h in range(head_count):
            q_h = jnp.where(head_of_lane == h, q.astype(F32), 0.0).astype(BF16)
            s = dot_nt(q_h, keys) * HEAD_DIM ** (-0.5) + bias
            e = jnp.exp(s - jnp.max(s, axis=1, keepdims=True))
            norm = 1.0 / jnp.sum(e, axis=1, keepdims=True)
            o = dot(e.astype(BF16), vals) * norm
            total = jnp.where(head_of_lane == h, o, total)
        x = att_scr[q_rows, :] + dot(total.astype(BF16), attn_out_ref[...])
        att_scr[q_rows, :] = x

    def q_block(qi, carry):
        low = span_ref[0, qi]
        count = span_ref[1, qi]
        for n in range(1, rows // 256 + 1):

            @pl.when(count == n)
            def _():
                attend(qi, 256 * n, pl.multiple_of(low, 128))

        return carry

    lax.fori_loop(0, rows // q_step, q_block, 0)
    step = 256
    for b in range(rows // step):
        part = slice(b * step, (b + 1) * step)
        x = att_scr[part, :]
        normed = layer_norm(x, gain2_ref[...]).astype(BF16)
        hidden = gelu(dot(normed, mlp_in_ref[...])).astype(BF16)
        q_scr[part, :] = (x + dot(hidden, mlp_out_ref[...])).astype(BF16)
    slot_f = slot_row.astype(F32)
    eye128 = eye_mask(128)
    step = 512
    for b in range(full // step + 1):
        size = step if b < full // step else 2 * owners
        cols = []
        for i in range(size // 128):
            at = b * step + i * 128
            cols.append(
                jnp.sum(jnp.where(eye128, slot_f[:, at : at + 128], 0.0), axis=1, keepdims=True)
            )
        col = jnp.concatenate(cols, axis=0).astype(I32)
        pick = one_hot(iota((size, rows), 1) == col)
        out = dot(pick, q_scr[...])
        if b < full // step:
            o = b * step // 16
            n = step // 16
            out = out.astype(BF16)
            back_ref[o : o + n, 0:16, :] = out[:, 0:128].reshape(n, 16, 128)
            back_ref[o : o + n, 16:32, :] = out[:, 128:256].reshape(n, 16, 128)
        else:
            for j in range(2):
                tail_scr[pl.ds(j, owners, stride=8), :] = out[j * owners : (j + 1) * owners, 0:128]
                tail_scr[pl.ds(j + 2, owners, stride=8), :] = out[
                    j * owners : (j + 1) * owners, 128:256
                ]
            back_ref[:, 32:40, :] = tail_scr[...].astype(BF16).reshape(owners, 8, 128)


def owner_encode(span, msg, window, gain1, attn_in, attn_out, gain2, mlp_in, mlp_out):
    owners = msg.shape[0]
    rows = window.shape[1]
    channels = attn_out.shape[0]
    vmem = pl.BlockSpec(memory_space=pltpu.VMEM)
    smem = pl.BlockSpec(memory_space=pltpu.SMEM)
    return pl.pallas_call(
        owner_kernel,
        out_shape=jax.ShapeDtypeStruct((owners, MSG, 128), BF16),
        in_specs=[smem] + [vmem] * 8,
        out_specs=vmem,
        scratch_shapes=[
            pltpu.VMEM((owners * 8, 128), F32),
            pltpu.VMEM((rows, channels), BF16),
            pltpu.VMEM((rows, channels), BF16),
            pltpu.VMEM((rows, channels), BF16),
            pltpu.VMEM((rows, channels), F32),
        ],
        compiler_params=pltpu.CompilerParams(vmem_limit_bytes=VMEM_LIMIT),
        name="owner_encode",
    )(span, msg, window, gain1, attn_in, attn_out, gain2, mlp_in, mlp_out)


def place_kernel(
    count_ref, starts_ref, back_ref, cells_ref, pos_ref, token_ref, gain_ref,
    dec_ref, normed_ref,
    left_scr, right_scr,
):
    owners = back_ref.shape[0]
    entries = cells_ref.shape[1]
    cell_total = pos_ref.shape[0]
    count = count_ref[0]
    left_scr[...] = jnp.zeros(left_scr.shape, F32)
    right_scr[...] = jnp.zeros(right_scr.shape, F32)

    def take(o, carry):
        start = starts_ref[0, o]
        block = back_ref[o].astype(F32)
        left_scr[pl.ds(start, 16), :] = block[0:16]
        right_scr[pl.ds(start, 16), :] = block[16:32]
        left_scr[pl.ds(start + 16, 2), :] = block[32:34]
        right_scr[pl.ds(start + 16, 2), :] = block[34:36]
        return carry

    lax.fori_loop(0, owners, take, 0, unroll=4)
    rows = jnp.concatenate([left_scr[0:entries, :], right_scr[0:entries, :]], axis=1).astype(BF16)
    cells = jnp.where(iota((1, entries), 1) < count, cells_ref[...], -1)
    step = 512
    for b in range(cell_total // step):
        part = slice(b * step, (b + 1) * step)
        hit = jnp.where(cells == iota((step, entries), 0) + b * step, 1.0, 0.0)
        filled = dot(hit.astype(BF16), rows)
        seen = jnp.sum(hit, axis=1, keepdims=True)
        filled = jnp.where(seen > 0.5, filled, token_ref[...])
        dec = (filled + pos_ref[part, :].astype(F32)).astype(BF16)
        dec_ref[part, :] = dec
        normed_ref[part, :] = layer_norm(dec.astype(F32), gain_ref[...]).astype(BF16)


def place_rows(vis_count, starts, back, cells, pos, token, gain):
    vmem = pl.BlockSpec(memory_space=pltpu.VMEM)
    smem = pl.BlockSpec(memory_space=pltpu.SMEM)
    return pl.pallas_call(
        place_kernel,
        out_shape=(
            jax.ShapeDtypeStruct(pos.shape, BF16),
            jax.ShapeDtypeStruct(pos.shape, BF16),
        ),
        in_specs=[smem, smem] + [vmem] * 5,
        out_specs=(vmem, vmem),
        scratch_shapes=[pltpu.VMEM((cells.shape[1] + 24, 128), F32)] * 2,
        compiler_params=pltpu.CompilerParams(vmem_limit_bytes=VMEM_LIMIT),
        name="place_rows",
    )(vis_count, starts, back, cells, pos, token, gain)


def conv_kernel(
    dims, normed_ref, dec_ref, az_low_ref, az_high_ref, rad_low_ref, rad_high_ref, corner_ref,
    weight_ref, bias_ref,
    out_ref,
    wide_scr,
):
    az, rad, height = dims
    channels = bias_ref.shape[1]
    plane = rad * height
    pitch = (rad + 2) * height

    def put(at, rows):
        n = rows.shape[0]
        h = iota((n, 1), 0) % height
        values = rows.astype(F32)
        wide_scr[at : at + n, channels : 2 * channels] = rows
        below = jnp.where(h == 0, 0.0, pltpu.roll(values, 1, 0))
        wide_scr[at : at + n, 0:channels] = below.astype(BF16)
        above = jnp.where(h == height - 1, 0.0, pltpu.roll(values, n - 1, 0))
        wide_scr[at : at + n, 2 * channels :] = above.astype(BF16)

    for a in range(az + 2):
        base = a * pitch
        if a == 0:
            row, lo, hi = az_low_ref[...], corner_ref[0], corner_ref[1]
        elif a == az + 1:
            row, lo, hi = az_high_ref[...], corner_ref[2], corner_ref[3]
        else:
            i = a - 1
            row = normed_ref[i * plane : (i + 1) * plane, :]
            lo = rad_low_ref[i * height : (i + 1) * height, :]
            hi = rad_high_ref[i * height : (i + 1) * height, :]
        put(base, lo)
        put(base + height, row)
        put(base + height + plane, hi)
    for a in range(az):
        total = jnp.broadcast_to(bias_ref[...], (plane, channels))
        for da in range(3):
            for dr in range(3):
                at = (a + da) * pitch + dr * height
                total = total + dot(wide_scr[at : at + plane, :], weight_ref[da * 3 + dr])
        part = slice(a * plane, (a + 1) * plane)
        out_ref[part, :] = (dec_ref[part, :].astype(F32) + gelu(total)).astype(BF16)


def conv_block(dims, normed, dec, az_low, az_high, rad_low, rad_high, corners, weight, bias):
    az, rad, height = dims
    channels = normed.shape[1]
    vmem = pl.BlockSpec(memory_space=pltpu.VMEM)
    return pl.pallas_call(
        functools.partial(conv_kernel, dims),
        out_shape=jax.ShapeDtypeStruct(normed.shape, BF16),
        in_specs=[vmem] * 9,
        out_specs=vmem,
        scratch_shapes=[pltpu.VMEM(((az + 2) * (rad + 2) * height, 3 * channels), BF16)],
        compiler_params=pltpu.CompilerParams(vmem_limit_bytes=VMEM_LIMIT),
        name="conv_block",
    )(normed, dec, az_low, az_high, rad_low, rad_high, corners, weight, bias)


def key_spans(window_ids, q_step):
    rows = window_ids.shape[0]
    blocks = window_ids.reshape(rows // q_step, q_step)
    low = jnp.sum(window_ids[None, :] < blocks[:, 0:1], axis=1, dtype=I32)
    high = jnp.sum(window_ids[None, :] <= blocks[:, q_step - 1 :], axis=1, dtype=I32)
    low = low // 128 * 128
    count = (high - low + 255) // 256
    low = jnp.minimum(low, rows - 256 * count)
    return jnp.stack([low, count])


def exchange(values):
    return lax.all_to_all(values, ("sector", "blk"), split_axis=0, concat_axis=0, tiled=True)


def body(
    visible_feats, grid_pos, vis_cells, vis_count, owner, slot, window, enc_gain1, attn_in,
    attn_out, enc_gain2, mlp_in, mlp_out, mask_token, dec_gain, conv_weight, conv_bias,
):
    n_sector = lax.axis_size("sector")
    n_blk = lax.axis_size("blk")
    owners = n_sector * n_blk
    az, rad, height, channels = grid_pos.shape
    cell_total = az * rad * height
    pos = grid_pos.reshape(cell_total, channels)
    cells = vis_cells.reshape(1, -1)
    message, starts = send_rows(
        vis_count, cells, owner.reshape(1, -1), slot.reshape(1, -1), visible_feats, pos, owners
    )
    message = exchange(message)
    back = owner_encode(
        key_spans(window[0], 128), message, window, enc_gain1.reshape(1, -1), attn_in, attn_out,
        enc_gain2.reshape(1, -1), mlp_in, mlp_out,
    )
    back = exchange(back)
    dec, normed = place_rows(
        vis_count, starts, back, cells, pos, mask_token.reshape(1, -1), dec_gain.reshape(1, -1)
    )
    cube = normed.reshape(az, rad, height, channels)
    up = [(i, (i + 1) % n_sector) for i in range(n_sector)]
    down = [(t, s) for s, t in up]
    outward = [(i, i + 1) for i in range(n_blk - 1)]
    inward = [(t, s) for s, t in outward]

    def both(first, second):
        return [(s * n_blk + r, s2 * n_blk + r2) for s, s2 in first for r, r2 in second]

    def flat(values):
        return values.reshape(-1, channels)

    az_low = lax.ppermute(flat(cube[az - 1]), "sector", up)
    az_high = lax.ppermute(flat(cube[0]), "sector", down)
    rad_low = lax.ppermute(flat(cube[:, rad - 1]), "blk", outward)
    rad_high = lax.ppermute(flat(cube[:, 0]), "blk", inward)
    every = ("sector", "blk")
    corners = jnp.stack(
        [
            lax.ppermute(cube[az - 1, rad - 1], every, both(up, outward)),
            lax.ppermute(cube[az - 1, 0], every, both(up, inward)),
            lax.ppermute(cube[0, rad - 1], every, both(down, outward)),
            lax.ppermute(cube[0, 0], every, both(down, inward)),
        ]
    )
    decoded = conv_block(
        (az, rad, height), normed, dec, az_low, az_high, rad_low, rad_high, corners,
        conv_weight.reshape(9, 3 * channels, channels), conv_bias.reshape(1, -1),
    )
    return decoded.reshape(az, rad, height, channels)


def solution(mesh):
    lists = P(("sector", "blk"))
    return jax.shard_map(
        body,
        mesh=mesh,
        in_specs=(
            P(("sector", "blk"), None),
            P("sector", "blk", None, None),
            lists,
            lists,
            lists,
            lists,
            P(("sector", "blk"), None),
        )
        + (P(),) * 10,
        out_specs=P("sector", "blk", None, None),
        check_vma=False,
    )
```

profile of v0, /device:TPU:0, one launch (start us, length us, event | category | flops | bytes accessed | tf_op | source)
XLA Modules:
  0.0 157.7 jit_solution(10024968656666218373)
XLA Ops:
  0.7 0.0 copy-start
  0.7 1.3 copy-done
  2.0 1.2 copy-done.2
  3.2 0.7 copy-done.8
  3.9 0.7 copy-done.10
  4.6 0.7 copy-done.11
  5.3 6.2 %send_rows.1 = (bf16[128,40,128]{2,1,0:T(8,128)(2,1)}, s32[1,128]{1,0:T(1,128)S(1)}) custom-call(s32[1]{0:T(128)S(6)} %copy.24.count_ref, s32[1,2048]{1,0:T(1,128)S(1)} %bitcast.60, s32[1,2048]{1,0:T(1,128)S(1)} %bitcast.62, s32[1,2048]{1,0:T(1,128)S(1)} %bitcast.63, bf16[2048,256]{1,0:T(8,128)(2,1)S(1)} %copy-done.2, bf16[2560,256]{1,0:T(8,128)(2,1)S(1)} %bitcast.54), custom_call_target="tpu_custom_call" | custom-call | tf_op jit(solution)/shard_map/send_rows/pallas_call | solution.py:121
  11.5 0.0 copy-start.4
  11.5 0.0 copy-start.5
  11.6 0.0 copy-start.13
  11.6 11.3 %all-to-all-start = ((bf16[128,40,128]{2,1,0:T(8,128)(2,1)}), bf16[128,40,128]{2,1,0:T(8,128)(2,1)S(1)}, u32[]{:S(2)}, u32[]{:S(2)}) async-start(bf16[128,40,128]{2,1,0:T(8,128)(2,1)} %get-tuple-element.10), calls=%async_computation | async-start | bytes 2621440 | tf_op jit(solution)/shard_map/all_to_all | solution.py:413
  22.9 0.1 fusion.4
  23.0 0.1 copy.23
  23.1 0.1 copy.22
  23.2 0.2 convert_reduce_fusion.1
  23.5 21.0 %all-to-all-done.msg_ref = bf16[128,40,128]{2,1,0:T(8,128)(2,1)S(1)} async-done(((bf16[128,40,128]{2,1,0:T(8,128)(2,1)}), bf16[128,40,128]{2,1,0:T(8,128)(2,1)S(1)}, u32[]{:S(2)}, u32[]{:S(2)}) %all-to-all-start) | async-done | bytes 1310752 | tf_op jit(solution)/shard_map/all_to_all | solution.py:413
  44.5 31.2 %owner_encode.1 = bf16[128,40,128]{2,1,0:T(8,128)(2,1)S(1)} custom-call(s32[2,8]{1,0:T(2,128)S(1)} %pad_add_fusion.span_ref, bf16[128,40,128]{2,1,0:T(8,128)(2,1)S(1)} %all-to-all-done.msg_ref, s32[1,1024]{1,0:T(1,128)S(1)} %copy-done.7, f32[1,256]{1,0:T(1,128)S(1)} %bitcast.64, bf16[256,768]{1,0:T(8,128)(2,1)S(1)} %copy-done.5, ...), custom_call_target="tpu_custom_call" | custom-call | tf_op jit(solution)/shard_map/owner_encode/pallas_call | solution.py:271
  75.8 0.0 copy-start.14
  75.8 0.0 copy-start.15
  75.8 28.6 %all_to_all.10.back_ref = bf16[128,40,128]{2,1,0:T(8,128)(2,1)S(1)} all-to-all(bf16[128,40,128]{2,1,0:T(8,128)(2,1)S(1)} %owner_encode.1), channel_id=1, replica_groups=mesh['sector'=32,'blk'=4] {'sector','blk'}, dimensions={0} | all-to-all | bytes 2621440 | tf_op jit(solution)/shard_map/all_to_all | solution.py:413
  104.4 6.5 %place_rows.1 = (bf16[2560,256]{1,0:T(8,128)(2,1)S(1)}, bf16[2560,256]{1,0:T(8,128)(2,1)S(1)}) custom-call(s32[1]{0:T(128)S(6)} %copy.24.count_ref, s32[1,128]{1,0:T(1,128)S(1)} %get-tuple-element.9.starts_ref, bf16[128,40,128]{2,1,0:T(8,128)(2,1)S(1)} %all_to_all.10.back_ref, s32[1,2048]{1,0:T(1,128)S(1)} %bitcast.61, bf16[2560,256]{1,0:T(8,128)(2,1)S(1)} %bitcast.55, ...), custom_call_target="tpu_custom_call" | custom-call | tf_op jit(solution)/shard_map/place_rows/pallas_call | solution.py:327
  110.9 2.4 %collective-permute-start.4 = (bf16[40,256]{1,0:T(8,128)(2,1)S(1)}, bf16[40,256]{1,0:T(8,128)(2,1)S(1)}, u32[]{:S(2)}, u32[]{:S(2)}) collective-permute-start(bf16[40,256]{1,0:T(8,128)(2,1)S(1)} %get-tuple-element.15), channel_id=1, source_target_pairs={{0,5},{1,6},{2,7},{4,9},{5,10},{6,11},{8,13},{9,14},{10,15},{12,17... | collective-permute-start | bytes 61448 | tf_op jit(solution)/shard_map/ppermute | solution.py:458
  113.3 1.3 collective-permute-start.7
  114.6 8.6 %collective-permute-start.2 = (bf16[320,256]{1,0:T(8,128)(2,1)S(1)}, bf16[320,256]{1,0:T(8,128)(2,1)S(1)}, u32[]{:S(2)}, u32[]{:S(2)}) collective-permute-start(bf16[320,256]{1,0:T(8,128)(2,1)S(1)} %bitcast.71), channel_id=1, source_target_pairs={{0,1},{1,2},{2,3},{4,5},{5,6},{6,7},{8,9},{9,10},{10,11},{12,13},{... | collective-permute-start | bytes 491528 | tf_op jit(solution)/shard_map/ppermute | solution.py:453
  123.3 1.3 collective-permute-start.3
  124.6 0.1 collective-permute-start.1
  124.7 0.5 collective-permute-start
  125.1 8.6 %collective-permute-start.6 = (bf16[40,256]{1,0:T(8,128)(2,1)S(1)}, bf16[40,256]{1,0:T(8,128)(2,1)S(1)}, u32[]{:S(2)}, u32[]{:S(2)}) collective-permute-start(bf16[40,256]{1,0:T(8,128)(2,1)S(1)} %get-tuple-element.17), channel_id=1, source_target_pairs={{4,1},{5,2},{6,3},{8,5},{9,6},{10,7},{12,9},{13,10},{14,11},{16,13... | collective-permute-start | bytes 61448 | tf_op jit(solution)/shard_map/ppermute | solution.py:460
  133.8 1.5 collective-permute-done.6
  135.2 1.5 collective-permute-start.5
  136.8 7.8 %collective-permute-done.5 = bf16[40,256]{1,0:T(8,128)(2,1)S(1)} collective-permute-done((bf16[40,256]{1,0:T(8,128)(2,1)S(1)}, bf16[40,256]{1,0:T(8,128)(2,1)S(1)}, u32[]{:S(2)}, u32[]{:S(2)}) %collective-permute-start.5) | collective-permute-done | bytes 20512 | tf_op jit(solution)/shard_map/ppermute | solution.py:459
  144.6 13.1 %conv_block.1 = bf16[2560,256]{1,0:T(8,128)(2,1)} custom-call(bf16[2560,256]{1,0:T(8,128)(2,1)S(1)} %get-tuple-element.11.normed_ref, bf16[2560,256]{1,0:T(8,128)(2,1)S(1)} %get-tuple-element.12.dec_ref, bf16[320,256]{1,0:T(8,128)(2,1)S(1)} %collective-permute-done.az_low_ref, bf16[320,256]{1,0:T(8,128)(2,1)S(1)} %collective-permute-done.1.az_high_ref, ...), custom_call_target="tpu_custom_call" | custom-call | tf_op jit(solution)/shard_map/conv_block/pallas_call | solution.py:390
  (35 shorter events, 0.2 us)
Async XLA Ops:
  0.7 1.3 copy-start
  2.0 1.2 copy-start.2
  3.2 0.7 copy-start.8
  3.9 0.7 copy-start.10
  4.6 0.7 copy-start.11
  11.5 11.4 %copy-start.7 = (s32[1,1024]{1,0:T(1,128)S(1)}, s32[1,1024]{1,0:T(1,128)}, u32[]{:S(2)}) copy-start(s32[1,1024]{1,0:T(1,128)} %window_ref.1) | copy-start | bytes 12292
  11.5 33.0 %copy-start.3 = (bf16[256,1024]{1,0:T(8,128)(2,1)S(1)}, bf16[256,1024]{1,0:T(8,128)(2,1)}, u32[]{:S(2)}) copy-start(bf16[256,1024]{1,0:T(8,128)(2,1)} %mlp_in_ref.1) | copy-start | bytes 1572868
  11.5 33.0 %copy-start.4 = (bf16[1024,256]{1,0:T(8,128)(2,1)S(1)}, bf16[1024,256]{1,0:T(8,128)(2,1)}, u32[]{:S(2)}) copy-start(bf16[1024,256]{1,0:T(8,128)(2,1)} %mlp_out_ref.1) | copy-start | bytes 1572868
  11.5 33.0 %copy-start.5 = (bf16[256,768]{1,0:T(8,128)(2,1)S(1)}, bf16[256,768]{1,0:T(8,128)(2,1)}, u32[]{:S(2)}) copy-start(bf16[256,768]{1,0:T(8,128)(2,1)} %attn_in_ref.1) | copy-start | bytes 1179652
  11.6 32.9 %copy-start.6 = (bf16[256,256]{1,0:T(8,128)(2,1)S(1)}, bf16[256,256]{1,0:T(8,128)(2,1)}, u32[]{:S(2)}) copy-start(bf16[256,256]{1,0:T(8,128)(2,1)} %attn_out_ref.1) | copy-start | bytes 393220
  11.6 32.9 %copy-start.12 = (f32[256]{0:T(256)S(1)}, f32[256]{0:T(256)}, u32[]{:S(2)}) copy-start(f32[256]{0:T(256)} %param.24) | copy-start | bytes 3076
  11.6 32.9 %copy-start.13 = (f32[256]{0:T(256)S(1)}, f32[256]{0:T(256)}, u32[]{:S(2)}) copy-start(f32[256]{0:T(256)} %param.27) | copy-start | bytes 3076
  11.6 32.9 %all-to-all-start = ((bf16[128,40,128]{2,1,0:T(8,128)(2,1)}), bf16[128,40,128]{2,1,0:T(8,128)(2,1)S(1)}, u32[]{:S(2)}, u32[]{:S(2)}) async-start(bf16[128,40,128]{2,1,0:T(8,128)(2,1)} %get-tuple-element.10), calls=%async_computation | async-start | bytes 2621440 | tf_op jit(solution)/shard_map/all_to_all | solution.py:413
  75.7 28.6 %copy-start.1 = (bf16[8,8,40,256]{3,2,1,0:T(8,128)(2,1)S(1)}, bf16[8,8,40,256]{3,2,1,0:T(8,128)(2,1)}, u32[]{:S(2)}) copy-start(bf16[8,8,40,256]{3,2,1,0:T(8,128)(2,1)} %param.18) | copy-start | bytes 3932164
  75.8 28.6 %copy-start.9 = (s32[2048]{0:T(1024)S(1)}, s32[2048]{0:T(1024)}, u32[]{:S(2)}) copy-start(s32[2048]{0:T(1024)} %param.19) | copy-start | bytes 24580
  75.8 28.6 %copy-start.14 = (f32[256]{0:T(256)S(1)}, f32[256]{0:T(256)}, u32[]{:S(2)}) copy-start(f32[256]{0:T(256)} %param.30) | copy-start | bytes 3076
  75.8 28.6 %copy-start.15 = (f32[256]{0:T(256)S(1)}, f32[256]{0:T(256)}, u32[]{:S(2)}) copy-start(f32[256]{0:T(256)} %param.31) | copy-start | bytes 3076
  110.9 33.7 %copy-start.16 = (f32[256]{0:T(256)S(1)}, f32[256]{0:T(256)}, u32[]{:S(2)}) copy-start(f32[256]{0:T(256)} %param.33) | copy-start | bytes 3076
  110.9 13.7 %collective-permute-start.4 = (bf16[40,256]{1,0:T(8,128)(2,1)S(1)}, bf16[40,256]{1,0:T(8,128)(2,1)S(1)}, u32[]{:S(2)}, u32[]{:S(2)}) collective-permute-start(bf16[40,256]{1,0:T(8,128)(2,1)S(1)} %get-tuple-element.15), channel_id=1, source_target_pairs={{0,5},{1,6},{2,7},{4,9},{5,10},{6,11},{8,13},{9,14},{10,15},{12,17... | collective-permute-start | bytes 61448 | tf_op jit(solution)/shard_map/ppermute | solution.py:458
  113.3 11.8 %collective-permute-start.7 = (bf16[40,256]{1,0:T(8,128)(2,1)S(1)}, bf16[40,256]{1,0:T(8,128)(2,1)S(1)}, u32[]{:S(2)}, u32[]{:S(2)}) collective-permute-start(bf16[40,256]{1,0:T(8,128)(2,1)S(1)} %get-tuple-element.16), channel_id=1, source_target_pairs={{5,0},{6,1},{7,2},{9,4},{10,5},{11,6},{13,8},{14,9},{15,10},{17,12... | collective-permute-start | bytes 61448 | tf_op jit(solution)/shard_map/ppermute | solution.py:461
  114.6 29.9 %collective-permute-start.2 = (bf16[320,256]{1,0:T(8,128)(2,1)S(1)}, bf16[320,256]{1,0:T(8,128)(2,1)S(1)}, u32[]{:S(2)}, u32[]{:S(2)}) collective-permute-start(bf16[320,256]{1,0:T(8,128)(2,1)S(1)} %bitcast.71), channel_id=1, source_target_pairs={{0,1},{1,2},{2,3},{4,5},{5,6},{6,7},{8,9},{9,10},{10,11},{12,13},{... | collective-permute-start | bytes 491528 | tf_op jit(solution)/shard_map/ppermute | solution.py:453
  123.3 21.3 %collective-permute-start.3 = (bf16[320,256]{1,0:T(8,128)(2,1)S(1)}, bf16[320,256]{1,0:T(8,128)(2,1)S(1)}, u32[]{:S(2)}, u32[]{:S(2)}) collective-permute-start(bf16[320,256]{1,0:T(8,128)(2,1)S(1)} %bitcast.70), channel_id=1, source_target_pairs={{1,0},{2,1},{3,2},{5,4},{6,5},{7,6},{9,8},{10,9},{11,10},{13,12},{... | collective-permute-start | bytes 491528 | tf_op jit(solution)/shard_map/ppermute | solution.py:454
  124.6 20.0 %collective-permute-start.1 = (bf16[320,256]{1,0:T(8,128)(2,1)S(1)}, bf16[320,256]{1,0:T(8,128)(2,1)S(1)}, u32[]{:S(2)}, u32[]{:S(2)}) collective-permute-start(bf16[320,256]{1,0:T(8,128)(2,1)S(1)} %get-tuple-element.21), channel_id=1, source_target_pairs={{4,0},{8,4},{12,8},{16,12},{20,16},{24,20},{28,24},{32,28},{36,32}... | collective-permute-start | bytes 491528 | tf_op jit(solution)/shard_map/ppermute | solution.py:452
  124.7 19.9 %collective-permute-start = (bf16[320,256]{1,0:T(8,128)(2,1)S(1)}, bf16[320,256]{1,0:T(8,128)(2,1)S(1)}, u32[]{:S(2)}, u32[]{:S(2)}) collective-permute-start(bf16[320,256]{1,0:T(8,128)(2,1)S(1)} %get-tuple-element.22), channel_id=1, source_target_pairs={{0,4},{4,8},{8,12},{12,16},{16,20},{20,24},{24,28},{28,32},{32,36}... | collective-permute-start | bytes 491528 | tf_op jit(solution)/shard_map/ppermute | solution.py:451
  125.1 10.1 %collective-permute-start.6 = (bf16[40,256]{1,0:T(8,128)(2,1)S(1)}, bf16[40,256]{1,0:T(8,128)(2,1)S(1)}, u32[]{:S(2)}, u32[]{:S(2)}) collective-permute-start(bf16[40,256]{1,0:T(8,128)(2,1)S(1)} %get-tuple-element.17), channel_id=1, source_target_pairs={{4,1},{5,2},{6,3},{8,5},{9,6},{10,7},{12,9},{13,10},{14,11},{16,13... | collective-permute-start | bytes 61448 | tf_op jit(solution)/shard_map/ppermute | solution.py:460
  135.2 9.3 %collective-permute-start.5 = (bf16[40,256]{1,0:T(8,128)(2,1)S(1)}, bf16[40,256]{1,0:T(8,128)(2,1)S(1)}, u32[]{:S(2)}, u32[]{:S(2)}) collective-permute-start(bf16[40,256]{1,0:T(8,128)(2,1)S(1)} %get-tuple-element.18), channel_id=1, source_target_pairs={{1,4},{2,5},{3,6},{5,8},{6,9},{7,10},{9,12},{10,13},{11,14},{13,16... | collective-permute-start | bytes 61448 | tf_op jit(solution)/shard_map/ppermute | solution.py:459
where the time goes:
time: 158 us
  Pallas kernels  57 us (36%)
  starting transfers between devices  35.6 us (23%)
  waiting for transfers between devices  30.3 us (19%)
  blocking collectives  28.6 us (18%)
  local copies, waits for them, and re-layouts  4.99 us (3%)
    pallas_call x1, Pallas kernels, owner_encode(): pl.pallas_call(owner_kernel, out_shape=jax.ShapeDtypeStruct((owners, MSG,...  31.2 us
    all_to_all x1, blocking collectives, exchange(): lax.all_to_all(values, ('sector', 'blk'), split_axis=0, concat_axis=0, ti...  28.6 us
    all_to_all x1, waiting for transfers between devices, exchange(): lax.all_to_all(values, ('sector', 'blk'), split_axis=0, concat_axis=0, ti...  21 us
    pallas_call x1, Pallas kernels, conv_block(): pl.pallas_call(functools.partial(conv_kernel, dims), out_shape=jax.ShapeD...  13.1 us
    all_to_all x1, starting transfers between devices, exchange(): lax.all_to_all(values, ('sector', 'blk'), split_axis=0, concat_axis=0, ti...  11.3 us
    ppermute x1, starting transfers between devices, body(): lax.ppermute(cube[0, rad - 1], every, both(down, outward))  8.62 us
    ppermute x1, starting transfers between devices, body(): rad_low = lax.ppermute(flat(cube[:, rad - 1]), 'blk', outward)  8.62 us
    ppermute x1, waiting for transfers between devices, body(): lax.ppermute(cube[az - 1, 0], every, both(up, inward))  7.76 us
  transfers between devices with their start and end apart: 9, of which 3 were waited for; matrix products, arithmetic and copies ran while one was open for 0% of the time, Pallas kernels for 0%

commit v1 on v0

--- a/solution.py
+++ b/solution.py
@@ -1,5 +1,3 @@
-import functools
-
 import jax
 import jax.numpy as jnp
 from jax import lax
@@ -51,13 +49,30 @@
     count_ref, cells_ref, owner_ref, slot_ref, vis_ref, pos_ref,
     msg_ref, starts_ref,
     left_scr, right_scr, meta_scr, starts_smem, sem,
+    cells_in, owner_in, slot_in, vis_in, pos_in, in_sems,
 ):
     entries = cells_ref.shape[1]
     owners = msg_ref.shape[0]
     cell_total = pos_ref.shape[0]
+    loads = [
+        pltpu.make_async_copy(src, dst, in_sems.at[i])
+        for i, (src, dst) in enumerate(
+            [
+                (owner_ref, owner_in),
+                (cells_ref, cells_in),
+                (slot_ref, slot_in),
+                (pos_ref, pos_in),
+                (vis_ref, vis_in),
+            ]
+        )
+    ]
+    for load in loads:
+        load.start()
+    for load in loads[:3]:
+        load.wait()
     entry = iota((1, entries), 1)
     live = entry < count_ref[0]
-    owner = jnp.where(live, owner_ref[...], owners)
+    owner = jnp.where(live, owner_in[...], owners)
     owner_id = iota((owners, entries), 0)
     start_col = jnp.sum(jnp.where(owner < owner_id, 1.0, 0.0), axis=1, keepdims=True)
     start_row = jnp.sum(jnp.where(eye_mask(owners), start_col, 0.0), axis=0, keepdims=True)
@@ -67,8 +82,8 @@
     belongs = owner == owner_id
     first = jnp.sum(jnp.where(belongs, start_col, 0.0), axis=0, keepdims=True)
     within = jnp.where(live, entry - first.astype(I32), 64)
-    cells = cells_ref[...]
-    slots = slot_ref[...]
+    cells = cells_in[...]
+    slots = slot_in[...]
     parts = jnp.concatenate(
         [cells >> 6, cells & 63, slots >> 5, slots & 31, within, within, within, within], axis=0
     ).astype(F32).astype(BF16)
@@ -88,11 +103,13 @@
             ).astype(BF16)
         )
     meta_scr[...] = dot(one_hot(belongs), jnp.concatenate(meta_parts, axis=0))
+    for load in loads[3:]:
+        load.wait()
     step = 512
     for b in range(entries // step):
         col = jnp.concatenate(cell_cols[b * step // 128 : (b + 1) * step // 128], axis=0)
         pick = one_hot(iota((step, cell_total), 1) == col)
-        rows = vis_ref[b * step : (b + 1) * step, :].astype(F32) + dot(pick, pos_ref[...])
+        rows = vis_in[b * step : (b + 1) * step, :].astype(F32) + dot(pick, pos_in[...])
         rows = rows.astype(BF16).astype(F32)
         left_scr[b * step : (b + 1) * step, :] = rows[:, 0:128]
         right_scr[b * step : (b + 1) * step, :] = rows[:, 128:256]
@@ -124,7 +141,7 @@
             jax.ShapeDtypeStruct((owners, MSG, 128), BF16),
             jax.ShapeDtypeStruct((1, owners), I32),
         ),
-        in_specs=[smem, vmem, vmem, vmem, vmem, vmem],
+        in_specs=[smem] + [pl.BlockSpec(memory_space=pltpu.HBM)] * 5,
         out_specs=(vmem, vmem),
         scratch_shapes=[
             pltpu.VMEM((entries + 24, 128), F32),
@@ -132,6 +149,12 @@
             pltpu.VMEM((owners, 128), F32),
             pltpu.SMEM((1, owners), I32),
             pltpu.SemaphoreType.DMA,
+            pltpu.VMEM(cells.shape, I32),
+            pltpu.VMEM(cells.shape, I32),
+            pltpu.VMEM(cells.shape, I32),
+            pltpu.VMEM(vis.shape, BF16),
+            pltpu.VMEM(pos.shape, BF16),
+            pltpu.SemaphoreType.DMA((5,)),
         ],
         compiler_params=pltpu.CompilerParams(vmem_limit_bytes=VMEM_LIMIT),
         name="send_rows",
@@ -142,7 +165,7 @@
     span_ref, msg_ref, window_ref, gain1_ref, attn_in_ref, attn_out_ref, gain2_ref,
     mlp_in_ref, mlp_out_ref,
     back_ref,
-    tail_scr, q_scr, k_scr, v_scr, att_scr,
+    tail_scr, q_scr, k_scr, v_scr, win_scr, att_scr, x_scr,
 ):
     owners = msg_ref.shape[0]
     rows = window_ref.shape[1]
@@ -180,39 +203,82 @@
     ).astype(BF16)
     step = 256
     for b in range(rows // step):
+        part = slice(b * step, (b + 1) * step)
         sel = one_hot(slot_row == iota((step, slot_row.shape[1]), 0) + b * step)
         x = dot(sel[:, :full], main) + dot(sel[:, full:], rest)
-        att_scr[b * step : (b + 1) * step, :] = x
+        x_scr[part, :] = x
         normed = layer_norm(x, gain1_ref[...]).astype(BF16)
         projected = dot(normed, attn_in_ref[...]).astype(BF16)
-        q_scr[b * step : (b + 1) * step, :] = projected[:, :channels]
-        k_scr[b * step : (b + 1) * step, :] = projected[:, channels : 2 * channels]
-        v_scr[b * step : (b + 1) * step, :] = projected[:, 2 * channels :]
+        q_scr[part, :] = projected[:, :channels]
+        k_scr[part, :] = projected[:, channels : 2 * channels]
+        ones = jnp.ones((step, 128), BF16)
+        v_scr[part, 0:128] = projected[:, 2 * channels : 2 * channels + 128]
+        v_scr[part, 128:256] = ones
+        v_scr[part, 256:384] = projected[:, 2 * channels + 128 :]
+        v_scr[part, 384:512] = ones
     q_step = 128
-    win_row = window_ref[...].astype(F32)
-    head_of_lane = iota((q_step, channels), 1) // HEAD_DIM
     eye_q = eye_mask(q_step)
+    for i in range(rows // 128):
+        part = slice(i * 128, (i + 1) * 128)
+        ids = window_ref[:, part].astype(F32)
+        ids = jnp.sum(jnp.where(eye_q, ids, 0.0), axis=1, keepdims=True)
+        win_scr[part, :] = jnp.broadcast_to(ids, (128, 128)).astype(I32)
+    head_of_lane = iota((1, channels), 1) // HEAD_DIM
+    lane_head = (iota((1, channels), 1) & 127) // HEAD_DIM
+    head_mask = [one_hot(head_of_lane == h) for h in range(head_count)]
+    scale = HEAD_DIM ** (-0.5) * 1.4426950408889634
+    stack = 4
+    half_heads = head_count // 2
 
     def attend(qi, key_count, key_start):
         q_rows = pl.ds(pl.multiple_of(qi * q_step, q_step), q_step)
         k_rows = pl.ds(key_start, key_count)
         q = q_scr[q_rows, :]
         keys = k_scr[k_rows, :]
-        vals = v_scr[k_rows, :]
-        q_win = window_ref[:, q_rows].astype(F32)
-        q_win = jnp.sum(jnp.where(eye_q, q_win, 0.0), axis=1, keepdims=True)
-        k_win = window_ref[:, k_rows].astype(F32)
-        bias = jnp.where(q_win == k_win, 0.0, -jnp.inf)
-        total = jnp.zeros((q_step, channels), F32)
-        for h in range(head_count):
-            q_h = jnp.where(head_of_lane == h, q.astype(F32), 0.0).astype(BF16)
-            s = dot_nt(q_h, keys) * HEAD_DIM ** (-0.5) + bias
-            e = jnp.exp(s - jnp.max(s, axis=1, keepdims=True))
-            norm = 1.0 / jnp.sum(e, axis=1, keepdims=True)
-            o = dot(e.astype(BF16), vals) * norm
-            total = jnp.where(head_of_lane == h, o, total)
-        x = att_scr[q_rows, :] + dot(total.astype(BF16), attn_out_ref[...])
-        att_scr[q_rows, :] = x
+        q_win = win_scr[q_rows, :]
+        q_win = jnp.concatenate([q_win] * (key_count // 128), axis=1)
+        bias = jnp.where(q_win == window_ref[:, k_rows], 0.0, -jnp.inf)
+        bias = jnp.concatenate([bias] * stack, axis=0)
+        groups = []
+        for half in range(2):
+            for g in range(half_heads // 4):
+                groups.append((half, range(g * 4, (g + 1) * 4)))
+
+        def scores(half, heads):
+            queries = jnp.concatenate([q * head_mask[half * half_heads + h] for h in heads], axis=0)
+            return dot_nt(queries, keys) + bias
+
+        def weigh(s):
+            top = jnp.max(s, axis=1, keepdims=True)
+            return jnp.exp2(((s - top) * scale).astype(BF16))
+
+        totals = [None, None]
+
+        def mix(half, heads, e):
+            o = dot(e, v_scr[k_rows, 256 * half : 256 * half + 256])
+            total = totals[half]
+            for i, h in enumerate(heads):
+                block = o[i * q_step : (i + 1) * q_step]
+                total = block if total is None else jnp.where(lane_head == h, block, total)
+            totals[half] = total
+
+        ahead = scores(*groups[0])
+        held = None
+        for i in range(len(groups)):
+            s = ahead
+            if i + 1 < len(groups):
+                ahead = scores(*groups[i + 1])
+            e = weigh(s)
+            if held is not None:
+                mix(*held)
+            held = (*groups[i], e)
+        mix(*held)
+
+        for half in range(2):
+            total = totals[half]
+            att_scr[q_rows, 128 * half : 128 * half + 128] = (
+                total[:, 0:128] * (1.0 / total[:, 128:256])
+            ).astype(BF16)
 
     def q_block(qi, carry):
         low = span_ref[0, qi]
@@ -229,7 +295,7 @@
     step = 256
     for b in range(rows // step):
         part = slice(b * step, (b + 1) * step)
-        x = att_scr[part, :]
+        x = x_scr[part, :] + dot(att_scr[part, :], attn_out_ref[...])
         normed = layer_norm(x, gain2_ref[...]).astype(BF16)
         hidden = gelu(dot(normed, mlp_in_ref[...])).astype(BF16)
         q_scr[part, :] = (x + dot(hidden, mlp_out_ref[...])).astype(BF16)
@@ -277,6 +343,8 @@
             pltpu.VMEM((owners * 8, 128), F32),
             pltpu.VMEM((rows, channels), BF16),
             pltpu.VMEM((rows, channels), BF16),
+            pltpu.VMEM((rows, 2 * channels), BF16),
+            pltpu.VMEM((rows, 128), I32),
             pltpu.VMEM((rows, channels), BF16),
             pltpu.VMEM((rows, channels), F32),
         ],
@@ -285,15 +353,23 @@
     )(span, msg, window, gain1, attn_in, attn_out, gain2, mlp_in, mlp_out)
 
 
-def place_kernel(
+def fill_cells(ids, cells, rows, token, pos, gain):
+    hit = jnp.where(cells == ids, 1.0, 0.0)
+    filled = dot(hit.astype(BF16), rows)
+    seen = jnp.sum(hit, axis=1, keepdims=True)
+    filled = jnp.where(seen > 0.5, filled, token)
+    dec = (filled + pos.astype(F32)).astype(BF16)
+    return dec, layer_norm(dec.astype(F32), gain).astype(BF16)
+
+
+def edge_kernel(
     count_ref, starts_ref, back_ref, cells_ref, pos_ref, token_ref, gain_ref,
-    dec_ref, normed_ref,
+    rows_ref, dec_ref, first_ref, last_ref,
     left_scr, right_scr,
 ):
     owners = back_ref.shape[0]
     entries = cells_ref.shape[1]
-    cell_total = pos_ref.shape[0]
-    count = count_ref[0]
+    az, rad, height, channels = pos_ref.shape
     left_scr[...] = jnp.zeros(left_scr.shape, F32)
     right_scr[...] = jnp.zeros(right_scr.shape, F32)
 
@@ -306,96 +382,247 @@
         right_scr[pl.ds(start + 16, 2), :] = block[34:36]
         return carry
 
-    lax.fori_loop(0, owners, take, 0, unroll=4)
+    lax.fori_loop(0, owners, take, 0, unroll=8)
     rows = jnp.concatenate([left_scr[0:entries, :], right_scr[0:entries, :]], axis=1).astype(BF16)
-    cells = jnp.where(iota((1, entries), 1) < count, cells_ref[...], -1)
-    step = 512
-    for b in range(cell_total // step):
-        part = slice(b * step, (b + 1) * step)
-        hit = jnp.where(cells == iota((step, entries), 0) + b * step, 1.0, 0.0)
-        filled = dot(hit.astype(BF16), rows)
-        seen = jnp.sum(hit, axis=1, keepdims=True)
-        filled = jnp.where(seen > 0.5, filled, token_ref[...])
-        dec = (filled + pos_ref[part, :].astype(F32)).astype(BF16)
-        dec_ref[part, :] = dec
-        normed_ref[part, :] = layer_norm(dec.astype(F32), gain_ref[...]).astype(BF16)
-
-
-def place_rows(vis_count, starts, back, cells, pos, token, gain):
+    rows_ref[...] = rows
+    cells = jnp.where(iota((1, entries), 1) < count_ref[0], cells_ref[...], -1)
+    at = [(a, r) for r in (0, rad - 1) for a in range(az)]
+    ids = jnp.concatenate(
+        [iota((height, entries), 0) + (a * rad + r) * height for a, r in at], axis=0
+    )
+    pos = jnp.concatenate([pos_ref[a, r].astype(F32) for a, r in at], axis=0)
+    dec, normed = fill_cells(ids, cells, rows, token_ref[...], pos, gain_ref[...])
+    dec_ref[...] = dec.reshape(dec_ref.shape)
+    first_ref[...] = normed[: az * height]
+    last_ref[...] = normed[az * height :]
+
+
+def place_edges(vis_count, starts, back, cells, pos, token, gain):
+    az, rad, height, channels = pos.shape
+    entries = cells.shape[1]
     vmem = pl.BlockSpec(memory_space=pltpu.VMEM)
     smem = pl.BlockSpec(memory_space=pltpu.SMEM)
+    edges = jax.ShapeDtypeStruct((2, az * height, channels), BF16)
+    edge = jax.ShapeDtypeStruct((az * height, channels), BF16)
     return pl.pallas_call(
-        place_kernel,
-        out_shape=(
-            jax.ShapeDtypeStruct(pos.shape, BF16),
-            jax.ShapeDtypeStruct(pos.shape, BF16),
-        ),
+        edge_kernel,
+        out_shape=(jax.ShapeDtypeStruct((entries, channels), BF16), edges, edge, edge),
         in_specs=[smem, smem] + [vmem] * 5,
+        out_specs=(vmem,) * 4,
+        scratch_shapes=[pltpu.VMEM((entries + 24, 128), F32)] * 2,
+        compiler_params=pltpu.CompilerParams(vmem_limit_bytes=VMEM_LIMIT),
+        cost_estimate=pl.CostEstimate(flops=6 * 10**8, bytes_accessed=4 * 10**6, transcendentals=0),
+        name="place_edges",
+    )(vis_count, starts, back, cells, pos, token, gain)
+
+
+def mid_kernel(
+    count_ref, rows_ref, cells_ref, pos_ref, token_ref, gain_ref,
+    dec_ref, normed_ref,
+):
+    entries = cells_ref.shape[1]
+    az, rad, height, channels = pos_ref.shape
+    size = (rad - 2) * height
+    rows = rows_ref[...]
+    cells = jnp.where(iota((1, entries), 1) < count_ref[0], cells_ref[...], -1)
+    for a in range(0, az, 2):
+        ids = jnp.concatenate(
+            [iota((size, entries), 0) + (i * rad + 1) * height for i in (a, a + 1)], axis=0
+        )
+        pos = jnp.concatenate(
+            [pos_ref[i, 1 : rad - 1].reshape(size, channels) for i in (a, a + 1)], axis=0
+        )
+        dec, normed = fill_cells(ids, cells, rows, token_ref[...], pos, gain_ref[...])
+        dec_ref[a : a + 2] = dec.reshape(2, size, channels)
+        normed_ref[a : a + 2] = normed.reshape(2, size, channels)
+
+
+def place_mid(vis_count, rows, cells, pos, token, gain):
+    az, rad, height, channels = pos.shape
+    vmem = pl.BlockSpec(memory_space=pltpu.VMEM)
+    smem = pl.BlockSpec(memory_space=pltpu.SMEM)
+    mid = jax.ShapeDtypeStruct((az, (rad - 2) * height, channels), BF16)
+    return pl.pallas_call(
+        mid_kernel,
+        out_shape=(mid, mid),
+        in_specs=[smem] + [vmem] * 5,
         out_specs=(vmem, vmem),
-        scratch_shapes=[pltpu.VMEM((cells.shape[1] + 24, 128), F32)] * 2,
         compiler_params=pltpu.CompilerParams(vmem_limit_bytes=VMEM_LIMIT),
-        name="place_rows",
-    )(vis_count, starts, back, cells, pos, token, gain)
+        cost_estimate=pl.CostEstimate(flops=2 * 10**9, bytes_accessed=6 * 10**6, transcendentals=0),
+        name="place_mid",
+    )(vis_count, rows, cells, pos, token, gain)
+
+
+def rim_kernel(mid_ref, edge0_ref, edge1_ref, low_ref, high_ref, first_ref, last_ref):
+    az, size, channels = mid_ref.shape
+    height = low_ref.shape[0] // az
+    for a, ref in ((0, first_ref), (az - 1, last_ref)):
+        part = slice(a * height, (a + 1) * height)
+        ref[0:height] = low_ref[part]
+        ref[height : 2 * height] = edge0_ref[part]
+        ref[2 * height : 2 * height + size] = mid_ref[a]
+        ref[2 * height + size : 3 * height + size] = edge1_ref[part]
+        ref[3 * height + size :] = high_ref[part]
+
+
+def rim_rows(mid, edge0, edge1, low, high):
+    az, size, channels = mid.shape
+    vmem = pl.BlockSpec(memory_space=pltpu.VMEM)
+    out = jax.ShapeDtypeStruct((size + 4 * (low.shape[0] // az), channels), BF16)
+    return pl.pallas_call(
+        rim_kernel,
+        out_shape=(out, out),
+        in_specs=[vmem] * 5,
+        out_specs=(vmem, vmem),
+        compiler_params=pltpu.CompilerParams(vmem_limit_bytes=8 * 2**20),
+        name="rim_rows",
+    )(mid, edge0, edge1, low, high)
+
+
+def widen(scr, at, rows, height):
+    n, channels = rows.shape
+    h = iota((n, 1), 0) % height
+    values = rows.astype(F32)
+    scr[at : at + n, channels : 2 * channels] = rows
+    below = jnp.where(h == 0, 0.0, pltpu.roll(values, 1, 0))
+    scr[at : at + n, 0:channels] = below.astype(BF16)
+    above = jnp.where(h == height - 1, 0.0, pltpu.roll(values, n - 1, 0))
+    scr[at : at + n, 2 * channels :] = above.astype(BF16)
 
 
 def conv_kernel(
-    dims, normed_ref, dec_ref, az_low_ref, az_high_ref, rad_low_ref, rad_high_ref, corner_ref,
-    weight_ref, bias_ref,
-    out_ref,
-    wide_scr,
+    mid_ref, edge0_ref, edge1_ref, low_ref, high_ref, mid_dec_ref, edge_dec_ref, weight_ref, bias_ref,
+    out_ref, partial_ref,
+    wide_scr, weight_scr, done_scr, weight_sems, out_sems,
 ):
-    az, rad, height = dims
-    channels = bias_ref.shape[1]
-    plane = rad * height
-    pitch = (rad + 2) * height
-
-    def put(at, rows):
-        n = rows.shape[0]
-        h = iota((n, 1), 0) % height
-        values = rows.astype(F32)
-        wide_scr[at : at + n, channels : 2 * channels] = rows
-        below = jnp.where(h == 0, 0.0, pltpu.roll(values, 1, 0))
-        wide_scr[at : at + n, 0:channels] = below.astype(BF16)
-        above = jnp.where(h == height - 1, 0.0, pltpu.roll(values, n - 1, 0))
-        wide_scr[at : at + n, 2 * channels :] = above.astype(BF16)
-
-    for a in range(az + 2):
+    az, size, channels = mid_ref.shape
+    height = low_ref.shape[0] // az
+    plane = size + 2 * height
+    pitch = plane + 2 * height
+    loads = [
+        pltpu.make_async_copy(weight_ref.at[pl.ds(3 * i, 3)], weight_scr.at[pl.ds(3 * i, 3)], weight_sems.at[i])
+        for i in range(3)
+    ]
+    for load in loads:
+        load.start()
+    for a in range(az):
         base = a * pitch
-        if a == 0:
-            row, lo, hi = az_low_ref[...], corner_ref[0], corner_ref[1]
-        elif a == az + 1:
-            row, lo, hi = az_high_ref[...], corner_ref[2], corner_ref[3]
-        else:
-            i = a - 1
-            row = normed_ref[i * plane : (i + 1) * plane, :]
-            lo = rad_low_ref[i * height : (i + 1) * height, :]
-            hi = rad_high_ref[i * height : (i + 1) * height, :]
-        put(base, lo)
-        put(base + height, row)
-        put(base + height + plane, hi)
+        part = slice(a * height, (a + 1) * height)
+        widen(wide_scr, base, low_ref[part], height)
+        widen(wide_scr, base + height, edge0_ref[part], height)
+        widen(wide_scr, base + 2 * height, mid_ref[a], height)
+        widen(wide_scr, base + 2 * height + size, edge1_ref[part], height)
+        widen(wide_scr, base + 3 * height + size, high_ref[part], height)
+    for load in loads:
+        load.wait()
+    stores = []
     for a in range(az):
         total = jnp.broadcast_to(bias_ref[...], (plane, channels))
         for da in range(3):
+            if not 0 <= a + da - 1 < az:
+                continue
             for dr in range(3):
-                at = (a + da) * pitch + dr * height
-                total = total + dot(wide_scr[at : at + plane, :], weight_ref[da * 3 + dr])
-        part = slice(a * plane, (a + 1) * plane)
-        out_ref[part, :] = (dec_ref[part, :].astype(F32) + gelu(total)).astype(BF16)
-
-
-def conv_block(dims, normed, dec, az_low, az_high, rad_low, rad_high, corners, weight, bias):
-    az, rad, height = dims
-    channels = normed.shape[1]
+                at = (a + da - 1) * pitch + dr * height
+                total = total + dot(wide_scr[at : at + plane, :], weight_scr[da * 3 + dr])
+        if a in (0, az - 1):
+            partial_ref[a // (az - 1)] = total
+            continue
+        part = slice(a * height, (a + 1) * height)
+        dec = jnp.concatenate([edge_dec_ref[0, part], mid_dec_ref[a], edge_dec_ref[1, part]], axis=0)
+        done_scr[a - 1] = (dec.astype(F32) + gelu(total)).astype(BF16)
+        store = pltpu.make_async_copy(
+            done_scr.at[a - 1], out_ref.at[pl.ds(a * plane, plane)], out_sems.at[a - 1]
+        )
+        store.start()
+        stores.append(store)
+    for store in stores:
+        store.wait()
+
+
+def conv_inner(mid, edge0, edge1, low, high, mid_dec, edge_dec, weight, bias):
+    az, size, channels = mid.shape
+    height = low.shape[0] // az
+    plane = size + 2 * height
     vmem = pl.BlockSpec(memory_space=pltpu.VMEM)
+    hbm = pl.BlockSpec(memory_space=pltpu.HBM)
     return pl.pallas_call(
-        functools.partial(conv_kernel, dims),
-        out_shape=jax.ShapeDtypeStruct(normed.shape, BF16),
-        in_specs=[vmem] * 9,
-        out_specs=vmem,
-        scratch_shapes=[pltpu.VMEM(((az + 2) * (rad + 2) * height, 3 * channels), BF16)],
+        conv_kernel,
+        out_shape=(
+            jax.ShapeDtypeStruct((az * plane, channels), BF16),
+            jax.ShapeDtypeStruct((2, plane, channels), F32),
+        ),
+        in_specs=[vmem] * 7 + [hbm, vmem],
+        out_specs=(hbm, vmem),
+        scratch_shapes=[
+            pltpu.VMEM((az * (plane + 2 * height), 3 * channels), BF16),
+            pltpu.VMEM(weight.shape, BF16),
+            pltpu.VMEM((az - 2, plane, channels), BF16),
+            pltpu.SemaphoreType.DMA((3,)),
+            pltpu.SemaphoreType.DMA((az - 2,)),
+        ],
         compiler_params=pltpu.CompilerParams(vmem_limit_bytes=VMEM_LIMIT),
-        name="conv_block",
-    )(normed, dec, az_low, az_high, rad_low, rad_high, corners, weight, bias)
+        cost_estimate=pl.CostEstimate(flops=8 * 10**9, bytes_accessed=10**7, transcendentals=0),
+        name="conv_inner",
+    )(mid, edge0, edge1, low, high, mid_dec, edge_dec, weight, bias)
+
+
+def conv_edge_kernel(
+    low_ref, high_ref, partial_ref, mid_dec_ref, edge_dec_ref, weight_ref, given_ref,
+    out_ref,
+    wide_scr, weight_scr, done_scr, weight_sems, out_sems,
+):
+    az, size, channels = mid_dec_ref.shape
+    plane = partial_ref.shape[1]
+    height = (plane - size) // 2
+    pitch = plane + 2 * height
+    loads = [
+        pltpu.make_async_copy(weight_ref.at[pl.ds(6 * i, 3)], weight_scr.at[pl.ds(3 * i, 3)], weight_sems.at[i])
+        for i in range(2)
+    ]
+    for load in loads:
+        load.start()
+    widen(wide_scr, 0, low_ref[...], height)
+    widen(wide_scr, pitch, high_ref[...], height)
+    stores = []
+    for i in range(2):
+        a = i * (az - 1)
+        loads[i].wait()
+        total = partial_ref[i]
+        for dr in range(3):
+            at = i * pitch + dr * height
+            total = total + dot(wide_scr[at : at + plane, :], weight_scr[i * 3 + dr])
+        part = slice(a * height, (a + 1) * height)
+        dec = jnp.concatenate([edge_dec_ref[0, part], mid_dec_ref[a], edge_dec_ref[1, part]], axis=0)
+        done_scr[i] = (dec.astype(F32) + gelu(total)).astype(BF16)
+        store = pltpu.make_async_copy(
+            done_scr.at[i], out_ref.at[pl.ds(a * plane, plane)], out_sems.at[i]
+        )
+        store.start()
+        stores.append(store)
+    for store in stores:
+        store.wait()
+
+
+def conv_edges(low, high, partial, mid_dec, edge_dec, weight, given):
+    plane, channels = partial.shape[1:]
+    vmem = pl.BlockSpec(memory_space=pltpu.VMEM)
+    hbm = pl.BlockSpec(memory_space=pltpu.HBM)
+    return pl.pallas_call(
+        conv_edge_kernel,
+        out_shape=jax.ShapeDtypeStruct(given.shape, BF16),
+        in_specs=[vmem] * 5 + [hbm, hbm],
+        out_specs=hbm,
+        scratch_shapes=[
+            pltpu.VMEM((2 * low.shape[0], 3 * channels), BF16),
+            pltpu.VMEM((6,) + weight.shape[1:], BF16),
+            pltpu.VMEM((2, plane, channels), BF16),
+            pltpu.SemaphoreType.DMA((2,)),
+            pltpu.SemaphoreType.DMA((2,)),
+        ],
+        input_output_aliases={6: 0},
+        compiler_params=pltpu.CompilerParams(vmem_limit_bytes=24 * 2**20),
+        name="conv_edges",
+    )(low, high, partial, mid_dec, edge_dec, weight, given)
 
 
 def key_spans(window_ids, q_step):
@@ -433,38 +660,24 @@
         enc_gain2.reshape(1, -1), mlp_in, mlp_out,
     )
     back = exchange(back)
-    dec, normed = place_rows(
-        vis_count, starts, back, cells, pos, mask_token.reshape(1, -1), dec_gain.reshape(1, -1)
-    )
-    cube = normed.reshape(az, rad, height, channels)
+    token = mask_token.reshape(1, -1)
+    gain = dec_gain.reshape(1, -1)
+    rows, edge_dec, edge0, edge1 = place_edges(vis_count, starts, back, cells, grid_pos, token, gain)
+    outward = [(i, i + 1) for i in range(n_blk - 1)]
+    inward = [(t, s) for s, t in outward]
+    rad_low = lax.ppermute(edge1, "blk", outward)
+    rad_high = lax.ppermute(edge0, "blk", inward)
+    mid_dec, mid = place_mid(vis_count, rows, cells, grid_pos, token, gain)
+    first, last = rim_rows(mid, edge0, edge1, rad_low, rad_high)
     up = [(i, (i + 1) % n_sector) for i in range(n_sector)]
     down = [(t, s) for s, t in up]
-    outward = [(i, i + 1) for i in range(n_blk - 1)]
-    inward = [(t, s) for s, t in outward]
-
-    def both(first, second):
-        return [(s * n_blk + r, s2 * n_blk + r2) for s, s2 in first for r, r2 in second]
-
-    def flat(values):
-        return values.reshape(-1, channels)
-
-    az_low = lax.ppermute(flat(cube[az - 1]), "sector", up)
-    az_high = lax.ppermute(flat(cube[0]), "sector", down)
-    rad_low = lax.ppermute(flat(cube[:, rad - 1]), "blk", outward)
-    rad_high = lax.ppermute(flat(cube[:, 0]), "blk", inward)
-    every = ("sector", "blk")
-    corners = jnp.stack(
-        [
-            lax.ppermute(cube[az - 1, rad - 1], every, both(up, outward)),
-            lax.ppermute(cube[az - 1, 0], every, both(up, inward)),
-            lax.ppermute(cube[0, rad - 1], every, both(down, outward)),
-            lax.ppermute(cube[0, 0], every, both(down, inward)),
-        ]
+    az_low = lax.ppermute(last, "sector", up)
+    az_high = lax.ppermute(first, "sector", down)
+    weight = conv_weight.reshape(9, 3 * channels, channels)
+    inner, partial = conv_inner(
+        mid, edge0, edge1, rad_low, rad_high, mid_dec, edge_dec, weight, conv_bias.reshape(1, -1)
     )
-    decoded = conv_block(
-        (az, rad, height), normed, dec, az_low, az_high, rad_low, rad_high, corners,
-        conv_weight.reshape(9, 3 * channels, channels), conv_bias.reshape(1, -1),
-    )
+    decoded = conv_edges(az_low, az_high, partial, mid_dec, edge_dec, weight, inner)
     return decoded.reshape(az, rad, height, channels)
 
 

time: 158 us -> 123 us (0.78); the launches traced: 158 us -> 121 us
  starting transfers between devices: 35.6 us -> 22.3 us
  Pallas kernels: 57 us -> 43.8 us
  waiting for transfers between devices: 30.3 us -> 21 us
    pallas_call x1, Pallas kernels: 31.2 us -> 16.5 us  [owner_encode(): pl.pallas_call(owner_kernel, out_shape=jax.ShapeDtypeStruct((owners, MSG,...]
    ppermute x8 -> x4, starting transfers between devices: 24.3 us -> 11 us  [the longest x1 5.05 us: body(): az_high = lax.ppermute(first, 'sector', down)]
    ppermute x8 -> x4, waiting for transfers between devices: 9.24 us -> 0.01 us  [the longest x1 0.01 us: body(): rad_low = lax.ppermute(edge1, 'blk', outward)]
    pallas_call x2 -> x5, Pallas kernels: 19.6 us -> 20.8 us  [the longest x1 11.5 us: conv_inner(): pl.pallas_call(conv_kernel, out_shape=(jax.ShapeDtypeStruct((az * plane,...]
    unnamed x36 -> x38, local copies, waits for them, and re-layouts: 4.87 us -> 4.87 us
  transfers between devices with their start and end apart: 9 -> 5, of which waited for: 3 -> 1; matrix products, arithmetic and copies ran while one was open for 0% -> 0% of each run, Pallas kernels for 0% -> 12%
where the time goes in v1:
time: 123 us; the launch traced here: 121 us
  Pallas kernels  43.8 us (36%)
  blocking collectives  27.5 us (22%)
  starting transfers between devices  22.3 us (18%)
  waiting for transfers between devices  21 us (17%)
  local copies, waits for them, and re-layouts  4.94 us (4%)
    all_to_all x1, blocking collectives, exchange(): lax.all_to_all(values, ('sector', 'blk'), split_axis=0, concat_axis=0, ti...  27.5 us
    all_to_all x1, waiting for transfers between devices, exchange(): lax.all_to_all(values, ('sector', 'blk'), split_axis=0, concat_axis=0, ti...  21 us
    pallas_call x1, Pallas kernels, owner_encode(): pl.pallas_call(owner_kernel, out_shape=jax.ShapeDtypeStruct((owners, MSG,...  16.5 us
    pallas_call x1, Pallas kernels, conv_inner(): pl.pallas_call(conv_kernel, out_shape=(jax.ShapeDtypeStruct((az * plane,...  11.5 us
    all_to_all x1, starting transfers between devices, exchange(): lax.all_to_all(values, ('sector', 'blk'), split_axis=0, concat_axis=0, ti...  11.3 us
    pallas_call x1, Pallas kernels, send_rows(): pl.pallas_call(send_kernel, out_shape=(jax.ShapeDtypeStruct((owners, MSG,...  6.55 us
    ppermute x1, starting transfers between devices, body(): az_high = lax.ppermute(first, 'sector', down)  5.05 us
    unnamed x38, local copies, waits for them, and re-layouts  4.87 us
  transfers between devices with their start and end apart: 5, of which 1 were waited for; matrix products, arithmetic and copies ran while one was open for 0% of the time, Pallas kernels for 12%

profile of v1, /device:TPU:0, one launch (start us, length us, event | category | flops | bytes accessed | tf_op | source)
XLA Modules:
  0.0 121.0 jit_solution(354332728790702589)
XLA Ops:
  0.7 0.0 copy-start
  0.7 1.3 %copy-done = bf16[8,8,40,256]{3,2,1,0:T(8,128)(2,1)S(1)} copy-done((bf16[8,8,40,256]{3,2,1,0:T(8,128)(2,1)S(1)}, bf16[8,8,40,256]{3,2,1,0:T(8,128)(2,1)}, u32[]{:S(2)}) %copy-start) | copy-done | bytes 1310744
  2.0 1.2 %copy-done.3 = bf16[2048,256]{1,0:T(8,128)(2,1)S(1)} copy-done((bf16[2048,256]{1,0:T(8,128)(2,1)S(1)}, bf16[2048,256]{1,0:T(8,128)(2,1)}, u32[]{:S(2)}) %copy-start.3) | copy-done | bytes 1048600
  3.2 0.7 copy-done.9
  3.9 0.7 copy-done.11
  4.6 0.7 copy-done.12
  5.3 6.6 %send_rows.1 = (bf16[128,40,128]{2,1,0:T(8,128)(2,1)}, s32[1,128]{1,0:T(1,128)S(1)}) custom-call(s32[1]{0:T(128)S(6)} %copy.26.count_ref, s32[1,2048]{1,0:T(1,128)S(1)} %bitcast.44, s32[1,2048]{1,0:T(1,128)S(1)} %bitcast.47, s32[1,2048]{1,0:T(1,128)S(1)} %bitcast.48, bf16[2048,256]{1,0:T(8,128)(2,1)S(1)} %copy-done.3, bf16[2560,256]{1,0:T(8,128)(2,1)S(1)} %bitcast.39), custom_call_target="tpu_custom_call" | custom-call | tf_op jit(solution)/shard_map/send_rows/pallas_call | solution.py:138
  11.8 0.0 copy-start.8
  11.9 0.0 copy-start.4
  11.9 0.0 copy-start.5
  11.9 0.0 copy-start.6
  11.9 0.0 copy-start.13
  11.9 0.0 copy-start.14
  11.9 11.3 %all-to-all-start = ((bf16[128,40,128]{2,1,0:T(8,128)(2,1)}), bf16[128,40,128]{2,1,0:T(8,128)(2,1)S(1)}, u32[]{:S(2)}, u32[]{:S(2)}) async-start(bf16[128,40,128]{2,1,0:T(8,128)(2,1)} %get-tuple-element.18), calls=%async_computation | async-start | bytes 2621440 | tf_op jit(solution)/shard_map/all_to_all | solution.py:640
  23.3 0.1 fusion.2
  23.3 0.1 copy.24
  23.4 0.1 copy.23
  23.5 0.2 convert_reduce_fusion.1
  23.8 21.0 %all-to-all-done.msg_ref = bf16[128,40,128]{2,1,0:T(8,128)(2,1)S(1)} async-done(((bf16[128,40,128]{2,1,0:T(8,128)(2,1)}), bf16[128,40,128]{2,1,0:T(8,128)(2,1)S(1)}, u32[]{:S(2)}, u32[]{:S(2)}) %all-to-all-start) | async-done | bytes 1310752 | tf_op jit(solution)/shard_map/all_to_all | solution.py:640
  44.9 16.5 %owner_encode.1 = bf16[128,40,128]{2,1,0:T(8,128)(2,1)S(1)} custom-call(s32[2,8]{1,0:T(2,128)S(1)} %pad_add_fusion.span_ref, bf16[128,40,128]{2,1,0:T(8,128)(2,1)S(1)} %all-to-all-done.msg_ref, s32[1,1024]{1,0:T(1,128)S(1)} %copy-done.8, f32[1,256]{1,0:T(1,128)S(1)} %bitcast.49, bf16[256,768]{1,0:T(8,128)(2,1)S(1)} %copy-done.6, ...), custom_call_target="tpu_custom_call" | custom-call | tf_op jit(solution)/shard_map/owner_encode/pallas_call | solution.py:337
  61.4 0.0 copy-start.10
  61.4 0.0 copy-start.15
  61.4 27.5 %all_to_all.10.back_ref = bf16[128,40,128]{2,1,0:T(8,128)(2,1)S(1)} all-to-all(bf16[128,40,128]{2,1,0:T(8,128)(2,1)S(1)} %owner_encode.1), channel_id=1, replica_groups=mesh['sector'=32,'blk'=4] {'sector','blk'}, dimensions={0} | all-to-all | bytes 2621440 | tf_op jit(solution)/shard_map/all_to_all | solution.py:640
  89.0 2.2 %place_edges.1 = (bf16[2048,256]{1,0:T(8,128)(2,1)S(1)}, bf16[2,320,256]{2,1,0:T(8,128)(2,1)S(1)}, bf16[320,256]{1,0:T(8,128)(2,1)S(1)}, bf16[320,256]{1,0:T(8,128)(2,1)S(1)}) custom-call(s32[1]{0:T(128)S(6)} %copy.26.count_ref, s32[1,128]{1,0:T(1,128)S(1)} %get-tuple-element.17.starts_ref, bf16[128,40,128]{2,1,0:T(8,128)(2,1)S(1)} %all_to_all.10.back_ref, ...), custom_call_target="tpu_custom_call" | custom-call | flops 600000000 | bytes 4000000 | tf_op jit(solution)/shard_map/place_edges/pallas_call | solution.py:407
  91.2 1.3 %collective-permute-start.1 = (bf16[320,256]{1,0:T(8,128)(2,1)S(1)}, bf16[320,256]{1,0:T(8,128)(2,1)S(1)}, u32[]{:S(2)}, u32[]{:S(2)}) collective-permute-start(bf16[320,256]{1,0:T(8,128)(2,1)S(1)} %get-tuple-element.21.edge0_ref), channel_id=1, source_target_pairs={{1,0},{2,1},{3,2},{5,4},{6,5},{7,6},{9,8},{10,9},{11,10},{13,12},{... | collective-permute-start | bytes 491528 | tf_op jit(solution)/shard_map/ppermute | solution.py:669
  92.5 4.6 %collective-permute-start = (bf16[320,256]{1,0:T(8,128)(2,1)S(1)}, bf16[320,256]{1,0:T(8,128)(2,1)S(1)}, u32[]{:S(2)}, u32[]{:S(2)}) collective-permute-start(bf16[320,256]{1,0:T(8,128)(2,1)S(1)} %get-tuple-element.22.edge1_ref), channel_id=1, source_target_pairs={{0,1},{1,2},{2,3},{4,5},{5,6},{6,7},{8,9},{9,10},{10,11},{12,13},{... | collective-permute-start | bytes 491528 | tf_op jit(solution)/shard_map/ppermute | solution.py:668
  97.1 3.6 %place_mid.1 = (bf16[8,240,256]{2,1,0:T(8,128)(2,1)S(1)}, bf16[8,240,256]{2,1,0:T(8,128)(2,1)S(1)}) custom-call(s32[1]{0:T(128)S(6)} %copy.26.count_ref, bf16[2048,256]{1,0:T(8,128)(2,1)S(1)} %get-tuple-element.19.rows_ref, s32[1,2048]{1,0:T(1,128)S(1)} %bitcast.46, bf16[8,8,40,256]{3,2,1,0:T(8,128)(2,1)S(1)} %copy-done.1, f32[1,256]{1,0:T(1,128)S(1)} %bitcast.52, ...), custom_call_target="tpu_custom_call" | custom-call | flops 2000000000 | bytes 6000000 | tf_op jit(solution)/shard_map/place_mid/pallas_call | solution.py:445
  100.7 0.0 copy-start.17
  100.7 0.1 collective-permute-start.2
  100.8 5.1 %collective-permute-start.3 = (bf16[400,256]{1,0:T(8,128)(2,1)S(1)}, bf16[400,256]{1,0:T(8,128)(2,1)S(1)}, u32[]{:S(2)}, u32[]{:S(2)}) collective-permute-start(bf16[400,256]{1,0:T(8,128)(2,1)S(1)} %get-tuple-element.24), channel_id=1, source_target_pairs={{4,0},{8,4},{12,8},{16,12},{20,16},{24,20},{28,24},{32,28},{36,32}... | collective-permute-start | bytes 614408 | tf_op jit(solution)/shard_map/ppermute | solution.py:675
  105.9 11.5 %conv_inner.1 = (bf16[2560,256]{1,0:T(8,128)(2,1)}, f32[2,320,256]{2,1,0:T(8,128)S(1)}) custom-call(bf16[8,240,256]{2,1,0:T(8,128)(2,1)S(1)} %get-tuple-element.20.mid_ref, bf16[320,256]{1,0:T(8,128)(2,1)S(1)} %get-tuple-element.21.edge0_ref, bf16[320,256]{1,0:T(8,128)(2,1)S(1)} %get-tuple-element.22.edge1_ref, ...), custom_call_target="tpu_custom_call" | custom-call | flops 8000000000 | bytes 10000000 | tf_op jit(solution)/shard_map/conv_inner/pallas_call | solution.py:548
  117.4 3.4 %conv_edges.1 = bf16[2560,256]{1,0:T(8,128)(2,1)} custom-call(bf16[400,256]{1,0:T(8,128)(2,1)S(1)} %collective-permute-done.2.low_ref, bf16[400,256]{1,0:T(8,128)(2,1)S(1)} %collective-permute-done.3.high_ref, f32[2,320,256]{2,1,0:T(8,128)S(1)} %get-tuple-element.27.partial_ref, ...), custom_call_target="tpu_custom_call", output_to_operand_aliasing={{}: (6, {})} | custom-call | tf_op jit(solution)/shard_map/conv_edges/pallas_call | solution.py:610
  (28 shorter events, 0.1 us)
Async XLA Ops:
  0.7 1.3 %copy-start = (bf16[8,8,40,256]{3,2,1,0:T(8,128)(2,1)S(1)}, bf16[8,8,40,256]{3,2,1,0:T(8,128)(2,1)}, u32[]{:S(2)}) copy-start(bf16[8,8,40,256]{3,2,1,0:T(8,128)(2,1)} %pos_ref.3) | copy-start | bytes 3932164
  2.0 1.2 %copy-start.3 = (bf16[2048,256]{1,0:T(8,128)(2,1)S(1)}, bf16[2048,256]{1,0:T(8,128)(2,1)}, u32[]{:S(2)}) copy-start(bf16[2048,256]{1,0:T(8,128)(2,1)} %vis_ref.1) | copy-start | bytes 3145732
  3.2 0.7 copy-start.9
  3.9 0.7 copy-start.11
  4.6 0.7 copy-start.12
  11.8 11.4 %copy-start.8 = (s32[1,1024]{1,0:T(1,128)S(1)}, s32[1,1024]{1,0:T(1,128)}, u32[]{:S(2)}) copy-start(s32[1,1024]{1,0:T(1,128)} %window_ref.1) | copy-start | bytes 12292
  11.9 33.0 %copy-start.4 = (bf16[256,1024]{1,0:T(8,128)(2,1)S(1)}, bf16[256,1024]{1,0:T(8,128)(2,1)}, u32[]{:S(2)}) copy-start(bf16[256,1024]{1,0:T(8,128)(2,1)} %mlp_in_ref.1) | copy-start | bytes 1572868
  11.9 32.9 %copy-start.5 = (bf16[1024,256]{1,0:T(8,128)(2,1)S(1)}, bf16[1024,256]{1,0:T(8,128)(2,1)}, u32[]{:S(2)}) copy-start(bf16[1024,256]{1,0:T(8,128)(2,1)} %mlp_out_ref.1) | copy-start | bytes 1572868
  11.9 32.9 %copy-start.6 = (bf16[256,768]{1,0:T(8,128)(2,1)S(1)}, bf16[256,768]{1,0:T(8,128)(2,1)}, u32[]{:S(2)}) copy-start(bf16[256,768]{1,0:T(8,128)(2,1)} %attn_in_ref.1) | copy-start | bytes 1179652
  11.9 32.9 %copy-start.7 = (bf16[256,256]{1,0:T(8,128)(2,1)S(1)}, bf16[256,256]{1,0:T(8,128)(2,1)}, u32[]{:S(2)}) copy-start(bf16[256,256]{1,0:T(8,128)(2,1)} %attn_out_ref.1) | copy-start | bytes 393220
  11.9 32.9 %copy-start.13 = (f32[256]{0:T(256)S(1)}, f32[256]{0:T(256)}, u32[]{:S(2)}) copy-start(f32[256]{0:T(256)} %param.24) | copy-start | bytes 3076
  11.9 32.9 %copy-start.14 = (f32[256]{0:T(256)S(1)}, f32[256]{0:T(256)}, u32[]{:S(2)}) copy-start(f32[256]{0:T(256)} %param.27) | copy-start | bytes 3076
  11.9 32.9 %all-to-all-start = ((bf16[128,40,128]{2,1,0:T(8,128)(2,1)}), bf16[128,40,128]{2,1,0:T(8,128)(2,1)S(1)}, u32[]{:S(2)}, u32[]{:S(2)}) async-start(bf16[128,40,128]{2,1,0:T(8,128)(2,1)} %get-tuple-element.18), calls=%async_computation | async-start | bytes 2621440 | tf_op jit(solution)/shard_map/all_to_all | solution.py:640
  61.4 27.6 %copy-start.1 = (bf16[8,8,40,256]{3,2,1,0:T(8,128)(2,1)S(1)}, bf16[8,8,40,256]{3,2,1,0:T(8,128)(2,1)}, u32[]{:S(2)}) copy-start(bf16[8,8,40,256]{3,2,1,0:T(8,128)(2,1)} %pos_ref.3) | copy-start | bytes 3932164
  61.4 27.6 %copy-start.10 = (s32[2048]{0:T(1024)S(1)}, s32[2048]{0:T(1024)}, u32[]{:S(2)}) copy-start(s32[2048]{0:T(1024)} %param.19) | copy-start | bytes 24580
  61.4 27.6 %copy-start.15 = (f32[256]{0:T(256)S(1)}, f32[256]{0:T(256)}, u32[]{:S(2)}) copy-start(f32[256]{0:T(256)} %param.30) | copy-start | bytes 3076
  61.4 27.6 %copy-start.16 = (f32[256]{0:T(256)S(1)}, f32[256]{0:T(256)}, u32[]{:S(2)}) copy-start(f32[256]{0:T(256)} %param.31) | copy-start | bytes 3076
  91.2 9.5 %collective-permute-start.1 = (bf16[320,256]{1,0:T(8,128)(2,1)S(1)}, bf16[320,256]{1,0:T(8,128)(2,1)S(1)}, u32[]{:S(2)}, u32[]{:S(2)}) collective-permute-start(bf16[320,256]{1,0:T(8,128)(2,1)S(1)} %get-tuple-element.21.edge0_ref), channel_id=1, source_target_pairs={{1,0},{2,1},{3,2},{5,4},{6,5},{7,6},{9,8},{10,9},{11,10},{13,12},{... | collective-permute-start | bytes 491528 | tf_op jit(solution)/shard_map/ppermute | solution.py:669
  92.5 8.2 %collective-permute-start = (bf16[320,256]{1,0:T(8,128)(2,1)S(1)}, bf16[320,256]{1,0:T(8,128)(2,1)S(1)}, u32[]{:S(2)}, u32[]{:S(2)}) collective-permute-start(bf16[320,256]{1,0:T(8,128)(2,1)S(1)} %get-tuple-element.22.edge1_ref), channel_id=1, source_target_pairs={{0,1},{1,2},{2,3},{4,5},{5,6},{6,7},{8,9},{9,10},{10,11},{12,13},{... | collective-permute-start | bytes 491528 | tf_op jit(solution)/shard_map/ppermute | solution.py:668
  100.7 5.2 %copy-start.17 = (f32[256]{0:T(256)S(1)}, f32[256]{0:T(256)}, u32[]{:S(2)}) copy-start(f32[256]{0:T(256)} %param.33) | copy-start | bytes 3076
  100.7 16.7 %collective-permute-start.2 = (bf16[400,256]{1,0:T(8,128)(2,1)S(1)}, bf16[400,256]{1,0:T(8,128)(2,1)S(1)}, u32[]{:S(2)}, u32[]{:S(2)}) collective-permute-start(bf16[400,256]{1,0:T(8,128)(2,1)S(1)} %get-tuple-element.23), channel_id=1, source_target_pairs={{0,4},{4,8},{8,12},{12,16},{16,20},{20,24},{24,28},{28,32},{32,36}... | collective-permute-start | bytes 614408 | tf_op jit(solution)/shard_map/ppermute | solution.py:674
  100.8 16.6 %collective-permute-start.3 = (bf16[400,256]{1,0:T(8,128)(2,1)S(1)}, bf16[400,256]{1,0:T(8,128)(2,1)S(1)}, u32[]{:S(2)}, u32[]{:S(2)}) collective-permute-start(bf16[400,256]{1,0:T(8,128)(2,1)S(1)} %get-tuple-element.24), channel_id=1, source_target_pairs={{4,0},{8,4},{12,8},{16,12},{20,16},{24,20},{28,24},{32,28},{36,32}... | collective-permute-start | bytes 614408 | tf_op jit(solution)/shard_map/ppermute | solution.py:675
  105.9 11.6 %copy-start.2 = (bf16[27,256,256]{2,1,0:T(8,128)(2,1)S(1)}, bf16[27,256,256]{2,1,0:T(8,128)(2,1)}, u32[]{:S(2)}) copy-start(bf16[27,256,256]{2,1,0:T(8,128)(2,1)} %param.32) | copy-start | bytes 10616836

commit v2 on v1

--- a/solution.py
+++ b/solution.py
@@ -12,7 +12,6 @@
 I32 = jnp.int32
 CAP = 18
 MSG = 40
-VMEM_LIMIT = 48 * 2**20
 
 
 def iota(shape, dim):
@@ -156,22 +155,38 @@
             pltpu.VMEM(pos.shape, BF16),
             pltpu.SemaphoreType.DMA((5,)),
         ],
-        compiler_params=pltpu.CompilerParams(vmem_limit_bytes=VMEM_LIMIT),
+        compiler_params=pltpu.CompilerParams(vmem_limit_bytes=60 * 2**20),
         name="send_rows",
     )(vis_count, cells, owner, slot, vis, pos)
 
 
 def owner_kernel(
-    span_ref, msg_ref, window_ref, gain1_ref, attn_in_ref, attn_out_ref, gain2_ref,
+    msg_ref, window_ref, gain1_ref, attn_in_ref, attn_out_ref, gain2_ref,
     mlp_in_ref, mlp_out_ref,
     back_ref,
-    tail_scr, q_scr, k_scr, v_scr, win_scr, att_scr, x_scr,
+    order_scr, tail_scr, q_scr, k_scr, v_scr, win_scr, att_scr, x_scr,
 ):
     owners = msg_ref.shape[0]
     rows = window_ref.shape[1]
     channels = attn_out_ref.shape[0]
     head_count = channels // HEAD_DIM
     full = 16 * owners
+    ids = window_ref[...]
+    windows = range(4)
+    length = [jnp.sum(jnp.where(ids == w, 1.0, 0.0)).astype(I32) for w in windows]
+    old = [sum(length[:w], jnp.int32(0)) for w in windows]
+    new = []
+    for w in windows:
+        ahead = [
+            jnp.where(length[v] >= length[w] if v < w else length[v] > length[w], length[v], 0)
+            for v in windows
+            if v != w
+        ]
+        new.append(sum(ahead, jnp.int32(0)))
+    end = [new[w] + length[w] for w in windows]
+    place_row = iota((1, rows), 1)
+    order = sum([jnp.where(place_row >= end[w], 1, 0) for w in windows])
+    order_scr[...] = order
     tail_scr[...] = msg_ref[:, 32:40, :].astype(F32).reshape(owners * 8, 128)
 
     def tail(j):
@@ -191,6 +206,10 @@
     tail_cols = [meta32[:, j : j + 1] * 32.0 + meta32[:, j + 32 : j + 33] - 32.0 for j in (16, 17)]
     tail_slots = [jnp.sum(jnp.where(eye, c, 0.0), axis=0, keepdims=True) for c in tail_cols]
     slot_row = jnp.concatenate([slot_full] + tail_slots, axis=1).astype(I32)
+    moved = slot_row + (new[0] - old[0])
+    for w in windows[1:]:
+        moved = jnp.where(slot_row >= old[w], slot_row + (new[w] - old[w]), moved)
+    slot_row = jnp.where(slot_row >= 0, moved, -1)
     left = msg_ref[:, 0:16, :].reshape(full, 128)
     right = msg_ref[:, 16:32, :].reshape(full, 128)
     main = jnp.concatenate([left, right], axis=1)
@@ -202,6 +221,7 @@
         axis=0,
     ).astype(BF16)
     step = 256
+    step = 1024
     for b in range(rows // step):
         part = slice(b * step, (b + 1) * step)
         sel = one_hot(slot_row == iota((step, slot_row.shape[1]), 0) + b * step)
@@ -216,11 +236,11 @@
         v_scr[part, 128:256] = ones
         v_scr[part, 256:384] = projected[:, 2 * channels + 128 :]
         v_scr[part, 384:512] = ones
-    q_step = 128
-    eye_q = eye_mask(q_step)
+    q_step = 256
+    eye_q = eye_mask(128)
     for i in range(rows // 128):
         part = slice(i * 128, (i + 1) * 128)
-        ids = window_ref[:, part].astype(F32)
+        ids = order_scr[:, part].astype(F32)
         ids = jnp.sum(jnp.where(eye_q, ids, 0.0), axis=1, keepdims=True)
         win_scr[part, :] = jnp.broadcast_to(ids, (128, 128)).astype(I32)
     head_of_lane = iota((1, channels), 1) // HEAD_DIM
@@ -237,7 +257,7 @@
         keys = k_scr[k_rows, :]
         q_win = win_scr[q_rows, :]
         q_win = jnp.concatenate([q_win] * (key_count // 128), axis=1)
-        bias = jnp.where(q_win == window_ref[:, k_rows], 0.0, -jnp.inf)
+        bias = jnp.where(q_win == order_scr[:, k_rows], 0.0, -jnp.inf)
         bias = jnp.concatenate([bias] * stack, axis=0)
         groups = []
         for half in range(2):
@@ -281,8 +301,15 @@
             ).astype(BF16)
 
     def q_block(qi, carry):
-        low = span_ref[0, qi]
-        count = span_ref[1, qi]
+        first = qi * q_step
+        low = jnp.int32(0)
+        high = jnp.int32(rows)
+        for w in windows:
+            low = jnp.maximum(low, jnp.where(new[w] <= first, new[w], 0))
+            high = jnp.minimum(high, jnp.where(end[w] >= first + q_step, end[w], rows))
+        low = (low >> 7) << 7
+        count = (high - low + 255) >> 8
+        low = jnp.minimum(low, rows - 256 * count)
         for n in range(1, rows // 256 + 1):
 
             @pl.when(count == n)
@@ -328,18 +355,18 @@
             back_ref[:, 32:40, :] = tail_scr[...].astype(BF16).reshape(owners, 8, 128)
 
 
-def owner_encode(span, msg, window, gain1, attn_in, attn_out, gain2, mlp_in, mlp_out):
+def owner_encode(msg, window, gain1, attn_in, attn_out, gain2, mlp_in, mlp_out):
     owners = msg.shape[0]
     rows = window.shape[1]
     channels = attn_out.shape[0]
     vmem = pl.BlockSpec(memory_space=pltpu.VMEM)
-    smem = pl.BlockSpec(memory_space=pltpu.SMEM)
     return pl.pallas_call(
         owner_kernel,
         out_shape=jax.ShapeDtypeStruct((owners, MSG, 128), BF16),
-        in_specs=[smem] + [vmem] * 8,
+        in_specs=[vmem] * 8,
         out_specs=vmem,
         scratch_shapes=[
+            pltpu.VMEM((1, rows), I32),
             pltpu.VMEM((owners * 8, 128), F32),
             pltpu.VMEM((rows, channels), BF16),
             pltpu.VMEM((rows, channels), BF16),
@@ -348,9 +375,9 @@
             pltpu.VMEM((rows, channels), BF16),
             pltpu.VMEM((rows, channels), F32),
         ],
-        compiler_params=pltpu.CompilerParams(vmem_limit_bytes=VMEM_LIMIT),
+        compiler_params=pltpu.CompilerParams(vmem_limit_bytes=40 * 2**20),
         name="owner_encode",
-    )(span, msg, window, gain1, attn_in, attn_out, gain2, mlp_in, mlp_out)
+    )(msg, window, gain1, attn_in, attn_out, gain2, mlp_in, mlp_out)
 
 
 def fill_cells(ids, cells, rows, token, pos, gain):
@@ -410,7 +437,7 @@
         in_specs=[smem, smem] + [vmem] * 5,
         out_specs=(vmem,) * 4,
         scratch_shapes=[pltpu.VMEM((entries + 24, 128), F32)] * 2,
-        compiler_params=pltpu.CompilerParams(vmem_limit_bytes=VMEM_LIMIT),
+        compiler_params=pltpu.CompilerParams(vmem_limit_bytes=24 * 2**20),
         cost_estimate=pl.CostEstimate(flops=6 * 10**8, bytes_accessed=4 * 10**6, transcendentals=0),
         name="place_edges",
     )(vis_count, starts, back, cells, pos, token, gain)
@@ -447,7 +474,7 @@
         out_shape=(mid, mid),
         in_specs=[smem] + [vmem] * 5,
         out_specs=(vmem, vmem),
-        compiler_params=pltpu.CompilerParams(vmem_limit_bytes=VMEM_LIMIT),
+        compiler_params=pltpu.CompilerParams(vmem_limit_bytes=24 * 2**20),
         cost_estimate=pl.CostEstimate(flops=2 * 10**9, bytes_accessed=6 * 10**6, transcendentals=0),
         name="place_mid",
     )(vis_count, rows, cells, pos, token, gain)
@@ -493,19 +520,14 @@
 def conv_kernel(
     mid_ref, edge0_ref, edge1_ref, low_ref, high_ref, mid_dec_ref, edge_dec_ref, weight_ref, bias_ref,
     out_ref, partial_ref,
-    wide_scr, weight_scr, done_scr, weight_sems, out_sems,
+    wide_scr, done_scr, out_sems,
 ):
     az, size, channels = mid_ref.shape
     height = low_ref.shape[0] // az
     plane = size + 2 * height
     pitch = plane + 2 * height
-    loads = [
-        pltpu.make_async_copy(weight_ref.at[pl.ds(3 * i, 3)], weight_scr.at[pl.ds(3 * i, 3)], weight_sems.at[i])
-        for i in range(3)
-    ]
-    for load in loads:
-        load.start()
-    for a in range(az):
+
+    def spread(a):
         base = a * pitch
         part = slice(a * height, (a + 1) * height)
         widen(wide_scr, base, low_ref[part], height)
@@ -513,28 +535,43 @@
         widen(wide_scr, base + 2 * height, mid_ref[a], height)
         widen(wide_scr, base + 2 * height + size, edge1_ref[part], height)
         widen(wide_scr, base + 3 * height + size, high_ref[part], height)
-    for load in loads:
-        load.wait()
-    stores = []
-    for a in range(az):
+
+    def taps(a):
         total = jnp.broadcast_to(bias_ref[...], (plane, channels))
         for da in range(3):
             if not 0 <= a + da - 1 < az:
                 continue
             for dr in range(3):
                 at = (a + da - 1) * pitch + dr * height
-                total = total + dot(wide_scr[at : at + plane, :], weight_scr[da * 3 + dr])
+                total = total + dot(wide_scr[at : at + plane, :], weight_ref[da * 3 + dr])
+        return total
+
+    def finish(a, total):
         if a in (0, az - 1):
             partial_ref[a // (az - 1)] = total
-            continue
+            return
         part = slice(a * height, (a + 1) * height)
         dec = jnp.concatenate([edge_dec_ref[0, part], mid_dec_ref[a], edge_dec_ref[1, part]], axis=0)
         done_scr[a - 1] = (dec.astype(F32) + gelu(total)).astype(BF16)
-        store = pltpu.make_async_copy(
-            done_scr.at[a - 1], out_ref.at[pl.ds(a * plane, plane)], out_sems.at[a - 1]
-        )
-        store.start()
-        stores.append(store)
+
+    spread(0)
+    spread(1)
+    spread(2)
+    stores = []
+    held = taps(0)
+    for a in range(1, az + 1):
+        if a < az:
+            total = taps(a)
+        if a + 2 < az:
+            spread(a + 2)
+        finish(a - 1, held)
+        held = total
+        if 0 < a - 1 < az - 1:
+            store = pltpu.make_async_copy(
+                done_scr.at[a - 2], out_ref.at[pl.ds((a - 1) * plane, plane)], out_sems.at[a - 2]
+            )
+            stores.append(store)
+            store.start()
     for store in stores:
         store.wait()
 
@@ -551,16 +588,14 @@
             jax.ShapeDtypeStruct((az * plane, channels), BF16),
             jax.ShapeDtypeStruct((2, plane, channels), F32),
         ),
-        in_specs=[vmem] * 7 + [hbm, vmem],
+        in_specs=[vmem] * 9,
         out_specs=(hbm, vmem),
         scratch_shapes=[
             pltpu.VMEM((az * (plane + 2 * height), 3 * channels), BF16),
-            pltpu.VMEM(weight.shape, BF16),
             pltpu.VMEM((az - 2, plane, channels), BF16),
-            pltpu.SemaphoreType.DMA((3,)),
             pltpu.SemaphoreType.DMA((az - 2,)),
         ],
-        compiler_params=pltpu.CompilerParams(vmem_limit_bytes=VMEM_LIMIT),
+        compiler_params=pltpu.CompilerParams(vmem_limit_bytes=32 * 2**20),
         cost_estimate=pl.CostEstimate(flops=8 * 10**9, bytes_accessed=10**7, transcendentals=0),
         name="conv_inner",
     )(mid, edge0, edge1, low, high, mid_dec, edge_dec, weight, bias)
@@ -569,28 +604,21 @@
 def conv_edge_kernel(
     low_ref, high_ref, partial_ref, mid_dec_ref, edge_dec_ref, weight_ref, given_ref,
     out_ref,
-    wide_scr, weight_scr, done_scr, weight_sems, out_sems,
+    wide_scr, done_scr, out_sems,
 ):
     az, size, channels = mid_dec_ref.shape
     plane = partial_ref.shape[1]
     height = (plane - size) // 2
     pitch = plane + 2 * height
-    loads = [
-        pltpu.make_async_copy(weight_ref.at[pl.ds(6 * i, 3)], weight_scr.at[pl.ds(3 * i, 3)], weight_sems.at[i])
-        for i in range(2)
-    ]
-    for load in loads:
-        load.start()
     widen(wide_scr, 0, low_ref[...], height)
     widen(wide_scr, pitch, high_ref[...], height)
     stores = []
     for i in range(2):
         a = i * (az - 1)
-        loads[i].wait()
         total = partial_ref[i]
         for dr in range(3):
             at = i * pitch + dr * height
-            total = total + dot(wide_scr[at : at + plane, :], weight_scr[i * 3 + dr])
+            total = total + dot(wide_scr[at : at + plane, :], weight_ref[i * 6 + dr])
         part = slice(a * height, (a + 1) * height)
         dec = jnp.concatenate([edge_dec_ref[0, part], mid_dec_ref[a], edge_dec_ref[1, part]], axis=0)
         done_scr[i] = (dec.astype(F32) + gelu(total)).astype(BF16)
@@ -610,30 +638,17 @@
     return pl.pallas_call(
         conv_edge_kernel,
         out_shape=jax.ShapeDtypeStruct(given.shape, BF16),
-        in_specs=[vmem] * 5 + [hbm, hbm],
+        in_specs=[vmem] * 6 + [hbm],
         out_specs=hbm,
         scratch_shapes=[
             pltpu.VMEM((2 * low.shape[0], 3 * channels), BF16),
-            pltpu.VMEM((6,) + weight.shape[1:], BF16),
             pltpu.VMEM((2, plane, channels), BF16),
-            pltpu.SemaphoreType.DMA((2,)),
             pltpu.SemaphoreType.DMA((2,)),
         ],
         input_output_aliases={6: 0},
-        compiler_params=pltpu.CompilerParams(vmem_limit_bytes=24 * 2**20),
+        compiler_params=pltpu.CompilerParams(vmem_limit_bytes=16 * 2**20),
         name="conv_edges",
     )(low, high, partial, mid_dec, edge_dec, weight, given)
-
-
-def key_spans(window_ids, q_step):
-    rows = window_ids.shape[0]
-    blocks = window_ids.reshape(rows // q_step, q_step)
-    low = jnp.sum(window_ids[None, :] < blocks[:, 0:1], axis=1, dtype=I32)
-    high = jnp.sum(window_ids[None, :] <= blocks[:, q_step - 1 :], axis=1, dtype=I32)
-    low = low // 128 * 128
-    count = (high - low + 255) // 256
-    low = jnp.minimum(low, rows - 256 * count)
-    return jnp.stack([low, count])
 
 
 def exchange(values):
@@ -656,7 +671,7 @@
     )
     message = exchange(message)
     back = owner_encode(
-        key_spans(window[0], 128), message, window, enc_gain1.reshape(1, -1), attn_in, attn_out,
+        message, window, enc_gain1.reshape(1, -1), attn_in, attn_out,
         enc_gain2.reshape(1, -1), mlp_in, mlp_out,
     )
     back = exchange(back)

time: 123 us -> 110 us (0.89)
  blocking collectives: 27.5 us -> 58.7 us
  waiting for transfers between devices: 21 us -> 0.01 us
  starting transfers between devices: 22.3 us -> 11 us
  Pallas kernels: 43.8 us -> 38 us
  local copies, waits for them, and re-layouts: 4.94 us -> 0.09 us
    all_to_all x1 -> x2, blocking collectives: 27.5 us -> 58.7 us  [exchange(): lax.all_to_all(values, ('sector', 'blk'), split_axis=0, concat_axis=0, ti...]
    all_to_all x1 -> x0, waiting for transfers between devices: 21 us -> none  [exchange(): lax.all_to_all(values, ('sector', 'blk'), split_axis=0, concat_axis=0, ti...]
    all_to_all x1 -> x0, starting transfers between devices: 11.3 us -> none  [exchange(): lax.all_to_all(values, ('sector', 'blk'), split_axis=0, concat_axis=0, ti...]
    unnamed x38 -> x28, local copies, waits for them, and re-layouts: 4.87 us -> 0.09 us
    pallas_call x1, Pallas kernels: 16.5 us -> 13.8 us  [owner_encode(): pl.pallas_call(owner_kernel, out_shape=jax.ShapeDtypeStruct((owners, MSG,...]
    pallas_call x1, Pallas kernels: 11.5 us -> 9.43 us  [conv_inner(): pl.pallas_call(conv_kernel, out_shape=(jax.ShapeDtypeStruct((az * plane,...]
    pallas_call x1, Pallas kernels: 3.41 us -> 1.94 us  [conv_edges(): pl.pallas_call(conv_edge_kernel, out_shape=jax.ShapeDtypeStruct(given.sha...]
  transfers between devices with their start and end apart: 5 -> 4, of which waited for: 1 -> 0; matrix products, arithmetic and copies ran while one was open for 0% -> 0% of each run, Pallas kernels for 12% -> 12%
where the time goes in v2:
time: 110 us; the launch traced here: 109 us
  blocking collectives  58.7 us (53%)
  Pallas kernels  38 us (35%)
  starting transfers between devices  11 us (10%)
  between operations  1.12 us (1%)
    all_to_all x2, blocking collectives, exchange(): lax.all_to_all(values, ('sector', 'blk'), split_axis=0, concat_axis=0, ti...  58.7 us
    pallas_call x1, Pallas kernels, owner_encode(): pl.pallas_call(owner_kernel, out_shape=jax.ShapeDtypeStruct((owners, MSG,...  13.8 us
    pallas_call x1, Pallas kernels, conv_inner(): pl.pallas_call(conv_kernel, out_shape=(jax.ShapeDtypeStruct((az * plane,...  9.43 us
    pallas_call x1, Pallas kernels, send_rows(): pl.pallas_call(send_kernel, out_shape=(jax.ShapeDtypeStruct((owners, MSG,...  7.12 us
    ppermute x1, starting transfers between devices, body(): az_high = lax.ppermute(first, 'sector', down)  5.05 us
    ppermute x1, starting transfers between devices, body(): rad_low = lax.ppermute(edge1, 'blk', outward)  4.56 us
    pallas_call x1, Pallas kernels, place_mid(): pl.pallas_call(mid_kernel, out_shape=(mid, mid), in_specs=[smem] + [vmem]...  3.57 us
    pallas_call x1, Pallas kernels, place_edges(): pl.pallas_call(edge_kernel, out_shape=(jax.ShapeDtypeStruct((entries, cha...  2.2 us
  transfers between devices with their start and end apart: 4, of which 0 were waited for; matrix products, arithmetic and copies ran while one was open for 0% of the time, Pallas kernels for 12%

profile of v2, /device:TPU:0, one launch (start us, length us, event | category | flops | bytes accessed | tf_op | source)
XLA Modules:
  0.0 109.0 jit_solution(9941906858748848641)
XLA Ops:
  0.7 7.1 %send_rows.1 = (bf16[128,40,128]{2,1,0:T(8,128)(2,1)}, s32[1,128]{1,0:T(1,128)}) custom-call(s32[1]{0:T(128)S(6)} %copy.20.count_ref, s32[1,2048]{1,0:T(1,128)} %bitcast.14, s32[1,2048]{1,0:T(1,128)} %bitcast.24, s32[1,2048]{1,0:T(1,128)} %bitcast.25, bf16[2048,256]{1,0:T(8,128)(2,1)} %vis_ref.1, bf16[2560,256]{1,0:T(8,128)(2,1)} %bitcast.11), custom_call_target="tpu_custom_call" | custom-call | tf_op jit(solution)/shard_map/send_rows/pallas_call | solution.py:137
  7.8 0.0 copy-start.2
  7.8 0.0 copy-start.3
  7.8 0.0 copy-start.4
  7.8 0.0 copy-start.5
  7.8 0.0 copy-start.7
  7.8 0.0 copy-start.8
  7.8 0.0 copy-start.9
  7.9 32.9 %all_to_all.10.msg_ref = bf16[128,40,128]{2,1,0:T(8,128)(2,1)S(1)} all-to-all(bf16[128,40,128]{2,1,0:T(8,128)(2,1)} %get-tuple-element.18), channel_id=1, replica_groups=mesh['sector'=32,'blk'=4] {'sector','blk'}, dimensions={0} | all-to-all | bytes 2621440 | tf_op jit(solution)/shard_map/all_to_all | solution.py:655
  40.7 0.0 copy-done.2
  40.8 13.8 %owner_encode.1 = bf16[128,40,128]{2,1,0:T(8,128)(2,1)S(1)} custom-call(bf16[128,40,128]{2,1,0:T(8,128)(2,1)S(1)} %all_to_all.10.msg_ref, s32[1,1024]{1,0:T(1,128)S(1)} %copy-done.7, f32[1,256]{1,0:T(1,128)S(1)} %bitcast.17, bf16[256,768]{1,0:T(8,128)(2,1)S(1)} %copy-done.4, bf16[256,256]{1,0:T(8,128)(2,1)S(1)} %copy-done.5, f32[1,256]{1,0:T(1,128)S(1)} %bitcast.18, ...), custom_call_target="tpu_custom_call" | custom-call | tf_op jit(solution)/shard_map/owner_encode/pallas_call | solution.py:363
  54.6 0.0 copy-start
  54.6 0.0 copy-start.6
  54.6 0.0 copy-start.10
  54.6 0.0 copy-start.11
  54.6 0.0 copy-start.12
  54.6 25.9 %all_to_all.11.back_ref = bf16[128,40,128]{2,1,0:T(8,128)(2,1)S(1)} all-to-all(bf16[128,40,128]{2,1,0:T(8,128)(2,1)S(1)} %owner_encode.1), channel_id=1, replica_groups=mesh['sector'=32,'blk'=4] {'sector','blk'}, dimensions={0} | all-to-all | bytes 2621440 | tf_op jit(solution)/shard_map/all_to_all | solution.py:655
  80.5 0.0 copy-done
  80.5 2.2 %place_edges.1 = (bf16[2048,256]{1,0:T(8,128)(2,1)S(1)}, bf16[2,320,256]{2,1,0:T(8,128)(2,1)S(1)}, bf16[320,256]{1,0:T(8,128)(2,1)S(1)}, bf16[320,256]{1,0:T(8,128)(2,1)S(1)}) custom-call(s32[1]{0:T(128)S(6)} %copy.20.count_ref, s32[1,128]{1,0:T(1,128)S(1)} %copy-done.12, bf16[128,40,128]{2,1,0:T(8,128)(2,1)S(1)} %all_to_all.11.back_ref, ...), custom_call_target="tpu_custom_call" | custom-call | flops 600000000 | bytes 4000000 | tf_op jit(solution)/shard_map/place_edges/pallas_call | solution.py:434
  82.7 1.3 %collective-permute-start.1 = (bf16[320,256]{1,0:T(8,128)(2,1)S(1)}, bf16[320,256]{1,0:T(8,128)(2,1)S(1)}, u32[]{:S(2)}, u32[]{:S(2)}) collective-permute-start(bf16[320,256]{1,0:T(8,128)(2,1)S(1)} %get-tuple-element.21.edge0_ref), channel_id=1, source_target_pairs={{1,0},{2,1},{3,2},{5,4},{6,5},{7,6},{9,8},{10,9},{11,10},{13,12},{... | collective-permute-start | bytes 491528 | tf_op jit(solution)/shard_map/ppermute | solution.py:684
  84.0 4.6 %collective-permute-start = (bf16[320,256]{1,0:T(8,128)(2,1)S(1)}, bf16[320,256]{1,0:T(8,128)(2,1)S(1)}, u32[]{:S(2)}, u32[]{:S(2)}) collective-permute-start(bf16[320,256]{1,0:T(8,128)(2,1)S(1)} %get-tuple-element.22.edge1_ref), channel_id=1, source_target_pairs={{0,1},{1,2},{2,3},{4,5},{5,6},{6,7},{8,9},{9,10},{10,11},{12,13},{... | collective-permute-start | bytes 491528 | tf_op jit(solution)/shard_map/ppermute | solution.py:683
  88.6 0.0 copy-start.1
  88.6 3.6 %place_mid.1 = (bf16[8,240,256]{2,1,0:T(8,128)(2,1)S(1)}, bf16[8,240,256]{2,1,0:T(8,128)(2,1)S(1)}) custom-call(s32[1]{0:T(128)S(6)} %copy.20.count_ref, bf16[2048,256]{1,0:T(8,128)(2,1)S(1)} %get-tuple-element.19.rows_ref, s32[1,2048]{1,0:T(1,128)S(1)} %bitcast.16, bf16[8,8,40,256]{3,2,1,0:T(8,128)(2,1)S(1)} %copy-done, f32[1,256]{1,0:T(1,128)S(1)} %bitcast.20, ...), custom_call_target="tpu_custom_call" | custom-call | flops 2000000000 | bytes 6000000 | tf_op jit(solution)/shard_map/place_mid/pallas_call | solution.py:472
  92.2 0.0 copy-start.13
  92.2 0.0 collective-permute-done.1.high_ref
  92.2 0.0 collective-permute-done.low_ref
  92.2 0.1 collective-permute-start.2
  92.3 5.1 %collective-permute-start.3 = (bf16[400,256]{1,0:T(8,128)(2,1)S(1)}, bf16[400,256]{1,0:T(8,128)(2,1)S(1)}, u32[]{:S(2)}, u32[]{:S(2)}) collective-permute-start(bf16[400,256]{1,0:T(8,128)(2,1)S(1)} %get-tuple-element.24), channel_id=1, source_target_pairs={{4,0},{8,4},{12,8},{16,12},{20,16},{24,20},{28,24},{32,28},{36,32}... | collective-permute-start | bytes 614408 | tf_op jit(solution)/shard_map/ppermute | solution.py:690
  97.4 9.4 %conv_inner.1 = (bf16[2560,256]{1,0:T(8,128)(2,1)}, f32[2,320,256]{2,1,0:T(8,128)S(1)}) custom-call(bf16[8,240,256]{2,1,0:T(8,128)(2,1)S(1)} %get-tuple-element.20.mid_ref, bf16[320,256]{1,0:T(8,128)(2,1)S(1)} %get-tuple-element.21.edge0_ref, bf16[320,256]{1,0:T(8,128)(2,1)S(1)} %get-tuple-element.22.edge1_ref, ...), custom_call_target="tpu_custom_call" | custom-call | flops 8000000000 | bytes 10000000 | tf_op jit(solution)/shard_map/conv_inner/pallas_call | solution.py:585
  106.8 0.0 collective-permute-done.2.low_ref
  106.8 0.0 collective-permute-done.3.high_ref
  106.8 1.9 %conv_edges.1 = bf16[2560,256]{1,0:T(8,128)(2,1)} custom-call(bf16[400,256]{1,0:T(8,128)(2,1)S(1)} %collective-permute-done.2.low_ref, bf16[400,256]{1,0:T(8,128)(2,1)S(1)} %collective-permute-done.3.high_ref, f32[2,320,256]{2,1,0:T(8,128)S(1)} %get-tuple-element.27.partial_ref, ...), custom_call_target="tpu_custom_call", output_to_operand_aliasing={{}: (6, {})} | custom-call | tf_op jit(solution)/shard_map/conv_edges/pallas_call | solution.py:638
  (13 shorter events, 0.1 us)
Async XLA Ops:
  7.8 33.0 %copy-start.2 = (bf16[256,1024]{1,0:T(8,128)(2,1)S(1)}, bf16[256,1024]{1,0:T(8,128)(2,1)}, u32[]{:S(2)}) copy-start(bf16[256,1024]{1,0:T(8,128)(2,1)} %mlp_in_ref.1) | copy-start | bytes 1572868
  7.8 33.0 %copy-start.3 = (bf16[1024,256]{1,0:T(8,128)(2,1)S(1)}, bf16[1024,256]{1,0:T(8,128)(2,1)}, u32[]{:S(2)}) copy-start(bf16[1024,256]{1,0:T(8,128)(2,1)} %mlp_out_ref.1) | copy-start | bytes 1572868
  7.8 33.0 %copy-start.4 = (bf16[256,768]{1,0:T(8,128)(2,1)S(1)}, bf16[256,768]{1,0:T(8,128)(2,1)}, u32[]{:S(2)}) copy-start(bf16[256,768]{1,0:T(8,128)(2,1)} %attn_in_ref.1) | copy-start | bytes 1179652
  7.8 33.0 %copy-start.5 = (bf16[256,256]{1,0:T(8,128)(2,1)S(1)}, bf16[256,256]{1,0:T(8,128)(2,1)}, u32[]{:S(2)}) copy-start(bf16[256,256]{1,0:T(8,128)(2,1)} %attn_out_ref.1) | copy-start | bytes 393220
  7.8 32.9 %copy-start.7 = (s32[1,1024]{1,0:T(1,128)S(1)}, s32[1,1024]{1,0:T(1,128)}, u32[]{:S(2)}) copy-start(s32[1,1024]{1,0:T(1,128)} %window_ref.1) | copy-start | bytes 12292
  7.8 32.9 %copy-start.8 = (f32[256]{0:T(256)S(1)}, f32[256]{0:T(256)}, u32[]{:S(2)}) copy-start(f32[256]{0:T(256)} %param.24) | copy-start | bytes 3076
  7.8 32.9 %copy-start.9 = (f32[256]{0:T(256)S(1)}, f32[256]{0:T(256)}, u32[]{:S(2)}) copy-start(f32[256]{0:T(256)} %param.27) | copy-start | bytes 3076
  54.6 25.9 %copy-start = (bf16[8,8,40,256]{3,2,1,0:T(8,128)(2,1)S(1)}, bf16[8,8,40,256]{3,2,1,0:T(8,128)(2,1)}, u32[]{:S(2)}) copy-start(bf16[8,8,40,256]{3,2,1,0:T(8,128)(2,1)} %pos_ref.3) | copy-start | bytes 3932164
  54.6 25.9 %copy-start.6 = (s32[2048]{0:T(1024)S(1)}, s32[2048]{0:T(1024)}, u32[]{:S(2)}) copy-start(s32[2048]{0:T(1024)} %param.19) | copy-start | bytes 24580
  54.6 25.9 %copy-start.10 = (f32[256]{0:T(256)S(1)}, f32[256]{0:T(256)}, u32[]{:S(2)}) copy-start(f32[256]{0:T(256)} %param.30) | copy-start | bytes 3076
  54.6 25.9 %copy-start.11 = (f32[256]{0:T(256)S(1)}, f32[256]{0:T(256)}, u32[]{:S(2)}) copy-start(f32[256]{0:T(256)} %param.31) | copy-start | bytes 3076
  54.6 25.9 %copy-start.12 = (s32[1,128]{1,0:T(1,128)S(1)}, s32[1,128]{1,0:T(1,128)}, u32[]{:S(2)}) copy-start(s32[1,128]{1,0:T(1,128)} %get-tuple-element.17.starts_ref) | copy-start | bytes 1540
  82.7 9.5 %collective-permute-start.1 = (bf16[320,256]{1,0:T(8,128)(2,1)S(1)}, bf16[320,256]{1,0:T(8,128)(2,1)S(1)}, u32[]{:S(2)}, u32[]{:S(2)}) collective-permute-start(bf16[320,256]{1,0:T(8,128)(2,1)S(1)} %get-tuple-element.21.edge0_ref), channel_id=1, source_target_pairs={{1,0},{2,1},{3,2},{5,4},{6,5},{7,6},{9,8},{10,9},{11,10},{13,12},{... | collective-permute-start | bytes 491528 | tf_op jit(solution)/shard_map/ppermute | solution.py:684
  84.0 8.2 %collective-permute-start = (bf16[320,256]{1,0:T(8,128)(2,1)S(1)}, bf16[320,256]{1,0:T(8,128)(2,1)S(1)}, u32[]{:S(2)}, u32[]{:S(2)}) collective-permute-start(bf16[320,256]{1,0:T(8,128)(2,1)S(1)} %get-tuple-element.22.edge1_ref), channel_id=1, source_target_pairs={{0,1},{1,2},{2,3},{4,5},{5,6},{6,7},{8,9},{9,10},{10,11},{12,13},{... | collective-permute-start | bytes 491528 | tf_op jit(solution)/shard_map/ppermute | solution.py:683
  88.6 8.8 %copy-start.1 = (bf16[27,256,256]{2,1,0:T(8,128)(2,1)S(1)}, bf16[27,256,256]{2,1,0:T(8,128)(2,1)}, u32[]{:S(2)}) copy-start(bf16[27,256,256]{2,1,0:T(8,128)(2,1)} %param.32) | copy-start | bytes 10616836
  92.2 5.2 %copy-start.13 = (f32[256]{0:T(256)S(1)}, f32[256]{0:T(256)}, u32[]{:S(2)}) copy-start(f32[256]{0:T(256)} %param.33) | copy-start | bytes 3076
  92.2 14.6 %collective-permute-start.2 = (bf16[400,256]{1,0:T(8,128)(2,1)S(1)}, bf16[400,256]{1,0:T(8,128)(2,1)S(1)}, u32[]{:S(2)}, u32[]{:S(2)}) collective-permute-start(bf16[400,256]{1,0:T(8,128)(2,1)S(1)} %get-tuple-element.23), channel_id=1, source_target_pairs={{0,4},{4,8},{8,12},{12,16},{16,20},{20,24},{24,28},{28,32},{32,36}... | collective-permute-start | bytes 614408 | tf_op jit(solution)/shard_map/ppermute | solution.py:689
  92.3 14.5 %collective-permute-start.3 = (bf16[400,256]{1,0:T(8,128)(2,1)S(1)}, bf16[400,256]{1,0:T(8,128)(2,1)S(1)}, u32[]{:S(2)}, u32[]{:S(2)}) collective-permute-start(bf16[400,256]{1,0:T(8,128)(2,1)S(1)} %get-tuple-element.24), channel_id=1, source_target_pairs={{4,0},{8,4},{12,8},{16,12},{20,16},{24,20},{28,24},{32,28},{36,32}... | collective-permute-start | bytes 614408 | tf_op jit(solution)/shard_map/ppermute | solution.py:690

commit v3 on v2

--- a/solution.py
+++ b/solution.py
@@ -380,23 +380,65 @@
     )(msg, window, gain1, attn_in, attn_out, gain2, mlp_in, mlp_out)
 
 
-def fill_cells(ids, cells, rows, token, pos, gain):
-    hit = jnp.where(cells == ids, 1.0, 0.0)
-    filled = dot(hit.astype(BF16), rows)
-    seen = jnp.sum(hit, axis=1, keepdims=True)
-    filled = jnp.where(seen > 0.5, filled, token)
-    dec = (filled + pos.astype(F32)).astype(BF16)
-    return dec, layer_norm(dec.astype(F32), gain).astype(BF16)
+def hit_kernel(
+    count_ref, cells_ref, pos_ref, token_ref,
+    edge_hit_ref, edge_base_ref, mid_hit_ref, mid_base_ref,
+):
+    entries = cells_ref.shape[1]
+    az, rad, height, channels = pos_ref.shape
+    cells = jnp.where(iota((1, entries), 1) < count_ref[0], cells_ref[...], -1)
+
+    def prepare(first, rows, pos):
+        hit = jnp.where(cells == iota((rows, entries), 0) + first, 1.0, 0.0)
+        seen = jnp.sum(hit, axis=1, keepdims=True)
+        pos = pos.astype(F32)
+        return hit.astype(BF16), jnp.where(seen > 0.5, pos, token_ref[...] + pos)
+
+    for a in range(az):
+        for side, r in ((0, 0), (1, rad - 1)):
+            at = (side * az + a) * height
+            hit, base = prepare((a * rad + r) * height, height, pos_ref[a, r])
+            edge_hit_ref[at : at + height, :] = hit
+            edge_base_ref[at : at + height, :] = base
+        size = (rad - 2) * height
+        hit, base = prepare(
+            (a * rad + 1) * height, size, pos_ref[a, 1 : rad - 1].reshape(size, channels)
+        )
+        mid_hit_ref[a * size : (a + 1) * size, :] = hit
+        mid_base_ref[a * size : (a + 1) * size, :] = base
+
+
+def cell_hits(vis_count, cells, pos, token):
+    az, rad, height, channels = pos.shape
+    entries = cells.shape[1]
+    vmem = pl.BlockSpec(memory_space=pltpu.VMEM)
+    smem = pl.BlockSpec(memory_space=pltpu.SMEM)
+    edge = 2 * az * height
+    mid = az * (rad - 2) * height
+    return pl.pallas_call(
+        hit_kernel,
+        out_shape=(
+            jax.ShapeDtypeStruct((edge, entries), BF16),
+            jax.ShapeDtypeStruct((edge, channels), F32),
+            jax.ShapeDtypeStruct((mid, entries), BF16),
+            jax.ShapeDtypeStruct((mid, channels), F32),
+        ),
+        in_specs=[smem] + [vmem] * 3,
+        out_specs=(vmem,) * 4,
+        compiler_params=pltpu.CompilerParams(vmem_limit_bytes=24 * 2**20),
+        cost_estimate=pl.CostEstimate(flops=3 * 10**9, bytes_accessed=15 * 10**6, transcendentals=0),
+        name="cell_hits",
+    )(vis_count, cells, pos, token)
 
 
 def edge_kernel(
-    count_ref, starts_ref, back_ref, cells_ref, pos_ref, token_ref, gain_ref,
+    starts_ref, back_ref, hit_ref, base_ref, gain_ref,
     rows_ref, dec_ref, first_ref, last_ref,
     left_scr, right_scr,
 ):
     owners = back_ref.shape[0]
-    entries = cells_ref.shape[1]
-    az, rad, height, channels = pos_ref.shape
+    entries = hit_ref.shape[1]
+    half = first_ref.shape[0]
     left_scr[...] = jnp.zeros(left_scr.shape, F32)
     right_scr[...] = jnp.zeros(right_scr.shape, F32)
 
@@ -412,84 +454,73 @@
     lax.fori_loop(0, owners, take, 0, unroll=8)
     rows = jnp.concatenate([left_scr[0:entries, :], right_scr[0:entries, :]], axis=1).astype(BF16)
     rows_ref[...] = rows
-    cells = jnp.where(iota((1, entries), 1) < count_ref[0], cells_ref[...], -1)
-    at = [(a, r) for r in (0, rad - 1) for a in range(az)]
-    ids = jnp.concatenate(
-        [iota((height, entries), 0) + (a * rad + r) * height for a, r in at], axis=0
-    )
-    pos = jnp.concatenate([pos_ref[a, r].astype(F32) for a, r in at], axis=0)
-    dec, normed = fill_cells(ids, cells, rows, token_ref[...], pos, gain_ref[...])
+    dec = (dot(hit_ref[...], rows) + base_ref[...]).astype(BF16)
+    normed = layer_norm(dec.astype(F32), gain_ref[...]).astype(BF16)
     dec_ref[...] = dec.reshape(dec_ref.shape)
-    first_ref[...] = normed[: az * height]
-    last_ref[...] = normed[az * height :]
-
-
-def place_edges(vis_count, starts, back, cells, pos, token, gain):
-    az, rad, height, channels = pos.shape
-    entries = cells.shape[1]
+    first_ref[...] = normed[:half]
+    last_ref[...] = normed[half:]
+
+
+def place_edges(starts, back, hit, base, gain):
+    entries = hit.shape[1]
+    cells, channels = base.shape
     vmem = pl.BlockSpec(memory_space=pltpu.VMEM)
     smem = pl.BlockSpec(memory_space=pltpu.SMEM)
-    edges = jax.ShapeDtypeStruct((2, az * height, channels), BF16)
-    edge = jax.ShapeDtypeStruct((az * height, channels), BF16)
+    edges = jax.ShapeDtypeStruct((2, cells // 2, channels), BF16)
+    edge = jax.ShapeDtypeStruct((cells // 2, channels), BF16)
     return pl.pallas_call(
         edge_kernel,
         out_shape=(jax.ShapeDtypeStruct((entries, channels), BF16), edges, edge, edge),
-        in_specs=[smem, smem] + [vmem] * 5,
+        in_specs=[smem] + [vmem] * 4,
         out_specs=(vmem,) * 4,
         scratch_shapes=[pltpu.VMEM((entries + 24, 128), F32)] * 2,
-        compiler_params=pltpu.CompilerParams(vmem_limit_bytes=24 * 2**20),
+        compiler_params=pltpu.CompilerParams(vmem_limit_bytes=16 * 2**20),
         cost_estimate=pl.CostEstimate(flops=6 * 10**8, bytes_accessed=4 * 10**6, transcendentals=0),
         name="place_edges",
-    )(vis_count, starts, back, cells, pos, token, gain)
-
-
-def mid_kernel(
-    count_ref, rows_ref, cells_ref, pos_ref, token_ref, gain_ref,
-    dec_ref, normed_ref,
-):
-    entries = cells_ref.shape[1]
-    az, rad, height, channels = pos_ref.shape
-    size = (rad - 2) * height
-    rows = rows_ref[...]
-    cells = jnp.where(iota((1, entries), 1) < count_ref[0], cells_ref[...], -1)
+    )(starts, back, hit, base, gain)
+
+
+def mid_kernel(rows_ref, hit_ref, base_ref, gain_ref, dec_ref, normed_ref):
+    az, size, channels = dec_ref.shape
     for a in range(0, az, 2):
-        ids = jnp.concatenate(
-            [iota((size, entries), 0) + (i * rad + 1) * height for i in (a, a + 1)], axis=0
-        )
-        pos = jnp.concatenate(
-            [pos_ref[i, 1 : rad - 1].reshape(size, channels) for i in (a, a + 1)], axis=0
-        )
-        dec, normed = fill_cells(ids, cells, rows, token_ref[...], pos, gain_ref[...])
+        part = slice(a * size, (a + 2) * size)
+        dec = (dot(hit_ref[part, :], rows_ref[...]) + base_ref[part, :]).astype(BF16)
+        normed = layer_norm(dec.astype(F32), gain_ref[...]).astype(BF16)
         dec_ref[a : a + 2] = dec.reshape(2, size, channels)
         normed_ref[a : a + 2] = normed.reshape(2, size, channels)
 
 
-def place_mid(vis_count, rows, cells, pos, token, gain):
-    az, rad, height, channels = pos.shape
+def place_mid(az, rows, hit, base, gain):
+    cells, channels = base.shape
     vmem = pl.BlockSpec(memory_space=pltpu.VMEM)
-    smem = pl.BlockSpec(memory_space=pltpu.SMEM)
-    mid = jax.ShapeDtypeStruct((az, (rad - 2) * height, channels), BF16)
+    mid = jax.ShapeDtypeStruct((az, cells // az, channels), BF16)
     return pl.pallas_call(
         mid_kernel,
         out_shape=(mid, mid),
-        in_specs=[smem] + [vmem] * 5,
+        in_specs=[vmem] * 4,
         out_specs=(vmem, vmem),
-        compiler_params=pltpu.CompilerParams(vmem_limit_bytes=24 * 2**20),
+        compiler_params=pltpu.CompilerParams(vmem_limit_bytes=16 * 2**20),
         cost_estimate=pl.CostEstimate(flops=2 * 10**9, bytes_accessed=6 * 10**6, transcendentals=0),
         name="place_mid",
-    )(vis_count, rows, cells, pos, token, gain)
+    )(rows, hit, base, gain)
+
+
+def ring_ends():
+    place = lax.axis_index("blk")
+    return place == 0, place == lax.axis_size("blk") - 1
 
 
 def rim_kernel(mid_ref, edge0_ref, edge1_ref, low_ref, high_ref, first_ref, last_ref):
     az, size, channels = mid_ref.shape
     height = low_ref.shape[0] // az
+    inside, outside = ring_ends()
     for a, ref in ((0, first_ref), (az - 1, last_ref)):
         part = slice(a * height, (a + 1) * height)
-        ref[0:height] = low_ref[part]
+        ref[0:height] = jnp.where(inside, 0.0, low_ref[part].astype(F32)).astype(BF16)
         ref[height : 2 * height] = edge0_ref[part]
         ref[2 * height : 2 * height + size] = mid_ref[a]
         ref[2 * height + size : 3 * height + size] = edge1_ref[part]
-        ref[3 * height + size :] = high_ref[part]
+        ref[3 * height + size :] = jnp.where(outside, 0.0, high_ref[part].astype(F32)).astype(BF16)
 
 
 def rim_rows(mid, edge0, edge1, low, high):
@@ -506,10 +537,13 @@
     )(mid, edge0, edge1, low, high)
 
 
-def widen(scr, at, rows, height):
+def widen(scr, at, rows, height, drop=None):
     n, channels = rows.shape
     h = iota((n, 1), 0) % height
     values = rows.astype(F32)
+    if drop is not None:
+        values = jnp.where(drop, 0.0, values)
+        rows = values.astype(BF16)
     scr[at : at + n, channels : 2 * channels] = rows
     below = jnp.where(h == 0, 0.0, pltpu.roll(values, 1, 0))
     scr[at : at + n, 0:channels] = below.astype(BF16)
@@ -526,15 +560,16 @@
     height = low_ref.shape[0] // az
     plane = size + 2 * height
     pitch = plane + 2 * height
+    inside, outside = ring_ends()
 
     def spread(a):
         base = a * pitch
         part = slice(a * height, (a + 1) * height)
-        widen(wide_scr, base, low_ref[part], height)
+        widen(wide_scr, base, low_ref[part], height, inside)
         widen(wide_scr, base + height, edge0_ref[part], height)
         widen(wide_scr, base + 2 * height, mid_ref[a], height)
         widen(wide_scr, base + 2 * height + size, edge1_ref[part], height)
-        widen(wide_scr, base + 3 * height + size, high_ref[part], height)
+        widen(wide_scr, base + 3 * height + size, high_ref[part], height, outside)
 
     def taps(a):
         total = jnp.broadcast_to(bias_ref[...], (plane, channels))
@@ -674,15 +709,18 @@
         message, window, enc_gain1.reshape(1, -1), attn_in, attn_out,
         enc_gain2.reshape(1, -1), mlp_in, mlp_out,
     )
+    back, count_later, cells_later = lax.optimization_barrier((back, vis_count, cells))
+    edge_hit, edge_base, mid_hit, mid_base = cell_hits(
+        count_later, cells_later, grid_pos, mask_token.reshape(1, -1)
+    )
     back = exchange(back)
-    token = mask_token.reshape(1, -1)
     gain = dec_gain.reshape(1, -1)
-    rows, edge_dec, edge0, edge1 = place_edges(vis_count, starts, back, cells, grid_pos, token, gain)
-    outward = [(i, i + 1) for i in range(n_blk - 1)]
+    rows, edge_dec, edge0, edge1 = place_edges(starts, back, edge_hit, edge_base, gain)
+    outward = [(i, (i + 1) % n_blk) for i in range(n_blk)]
     inward = [(t, s) for s, t in outward]
     rad_low = lax.ppermute(edge1, "blk", outward)
     rad_high = lax.ppermute(edge0, "blk", inward)
-    mid_dec, mid = place_mid(vis_count, rows, cells, grid_pos, token, gain)
+    mid_dec, mid = place_mid(az, rows, mid_hit, mid_base, gain)
     first, last = rim_rows(mid, edge0, edge1, rad_low, rad_high)
     up = [(i, (i + 1) % n_sector) for i in range(n_sector)]
     down = [(t, s) for s, t in up]

time: 110 us -> 112 us (1.018)
  blocking collectives: 58.7 us -> 32.9 us
  local copies, waits for them, and re-layouts: 0.09 us -> 12.9 us
  waiting for transfers between devices: 0.01 us -> 12.3 us
  Pallas kernels: 38 us -> 40.7 us
    all_to_all x2 -> x1, blocking collectives: 58.7 us -> 32.9 us  [exchange(): lax.all_to_all(values, ('sector', 'blk'), split_axis=0, concat_axis=0, ti...]
    unnamed x28 -> x40, local copies, waits for them, and re-layouts: 0.09 us -> 12.9 us
    all_to_all x0 -> x1, waiting for transfers between devices: none -> 12.1 us  [exchange(): lax.all_to_all(values, ('sector', 'blk'), split_axis=0, concat_axis=0, ti...]
    all_to_all x0 -> x1, starting transfers between devices: none -> 4.77 us  [exchange(): lax.all_to_all(values, ('sector', 'blk'), split_axis=0, concat_axis=0, ti...]
    ppermute x1, starting transfers between devices: 4.56 us -> 0.42 us  [body(): rad_low = lax.ppermute(edge1, 'blk', outward)]
    pallas_call x1 -> x2, Pallas kernels: 3.57 us -> 5.41 us  [the longest x1 2.78 us: cell_hits(): pl.pallas_call(hit_kernel, out_shape=(jax.ShapeDtypeStruct((edge, entries...]
  transfers between devices with their start and end apart: 4 -> 5, of which waited for: 0 -> 2; matrix products, arithmetic and copies ran while one was open for 0% -> 0% of each run, Pallas kernels for 12% -> 13%
where the time goes in v3:
time: 112 us
  Pallas kernels  40.7 us (36%)
  blocking collectives  32.9 us (29%)
  local copies, waits for them, and re-layouts  12.9 us (12%)
  waiting for transfers between devices  12.3 us (11%)
  starting transfers between devices  12 us (11%)
    all_to_all x1, blocking collectives, exchange(): lax.all_to_all(values, ('sector', 'blk'), split_axis=0, concat_axis=0, ti...  32.9 us
    pallas_call x1, Pallas kernels, owner_encode(): pl.pallas_call(owner_kernel, out_shape=jax.ShapeDtypeStruct((owners, MSG,...  14.8 us
    unnamed x40, local copies, waits for them, and re-layouts  12.9 us
    all_to_all x1, waiting for transfers between devices, exchange(): lax.all_to_all(values, ('sector', 'blk'), split_axis=0, concat_axis=0, ti...  12.1 us
    pallas_call x1, Pallas kernels, conv_inner(): pl.pallas_call(conv_kernel, out_shape=(jax.ShapeDtypeStruct((az * plane,...  9.42 us
    pallas_call x1, Pallas kernels, send_rows(): pl.pallas_call(send_kernel, out_shape=(jax.ShapeDtypeStruct((owners, MSG,...  7.12 us
    ppermute x1, starting transfers between devices, body(): az_high = lax.ppermute(first, 'sector', down)  5.05 us
    all_to_all x1, starting transfers between devices, exchange(): lax.all_to_all(values, ('sector', 'blk'), split_axis=0, concat_axis=0, ti...  4.77 us
  transfers between devices with their start and end apart: 5, of which 2 were waited for; matrix products, arithmetic and copies ran while one was open for 0% of the time, Pallas kernels for 13%

profile of v3, /device:TPU:0, one launch (start us, length us, event | category | flops | bytes accessed | tf_op | source)
XLA Modules:
  0.0 111.9 jit_solution(5744155836968960555)
XLA Ops:
  0.7 7.1 %send_rows.1 = (bf16[128,40,128]{2,1,0:T(8,128)(2,1)}, s32[1,128]{1,0:T(1,128)}) custom-call(s32[1]{0:T(128)S(6)} %copy.20.count_ref, s32[1,2048]{1,0:T(1,128)} %bitcast.14, s32[1,2048]{1,0:T(1,128)} %bitcast.22, s32[1,2048]{1,0:T(1,128)} %bitcast.23, bf16[2048,256]{1,0:T(8,128)(2,1)} %vis_ref.1, bf16[2560,256]{1,0:T(8,128)(2,1)} %bitcast.13), custom_call_target="tpu_custom_call" | custom-call | tf_op jit(solution)/shard_map/send_rows/pallas_call | solution.py:137
  7.8 0.0 copy-start.8
  7.8 0.0 copy-start.9
  7.8 0.0 copy-start.10
  7.8 0.0 copy-start.11
  7.8 0.0 copy-start.13
  7.8 0.0 copy-start.15
  7.8 0.0 copy-start.16
  7.9 32.9 %all_to_all.10.msg_ref = bf16[128,40,128]{2,1,0:T(8,128)(2,1)S(1)} all-to-all(bf16[128,40,128]{2,1,0:T(8,128)(2,1)} %get-tuple-element.25), channel_id=1, replica_groups=mesh['sector'=32,'blk'=4] {'sector','blk'}, dimensions={0} | all-to-all | bytes 2621440 | tf_op jit(solution)/shard_map/all_to_all | solution.py:690
  40.8 14.8 %owner_encode.1 = bf16[128,40,128]{2,1,0:T(8,128)(2,1)} custom-call(bf16[128,40,128]{2,1,0:T(8,128)(2,1)S(1)} %all_to_all.10.msg_ref, s32[1,1024]{1,0:T(1,128)S(1)} %copy-done.13, f32[1,256]{1,0:T(1,128)S(1)} %bitcast.18, bf16[256,768]{1,0:T(8,128)(2,1)S(1)} %copy-done.10, bf16[256,256]{1,0:T(8,128)(2,1)S(1)} %copy-done.11, f32[1,256]{1,0:T(1,128)S(1)} %bitcast.19, ...), custom_call_target="tpu_custom_call" | custom-call | tf_op jit(solution)/shard_map/owner_encode/pallas_call | solution.py:363
  55.6 4.8 %all-to-all-start.1 = ((bf16[128,40,128]{2,1,0:T(8,128)(2,1)}), bf16[128,40,128]{2,1,0:T(8,128)(2,1)S(1)}, u32[]{:S(2)}, u32[]{:S(2)}) async-start(bf16[128,40,128]{2,1,0:T(8,128)(2,1)} %owner_encode.1), calls=%async_computation.1 | async-start | bytes 2621440 | tf_op jit(solution)/shard_map/all_to_all | solution.py:690
  60.4 0.0 copy-start.5
  60.4 1.3 %copy-done.5 = bf16[8,8,40,256]{3,2,1,0:T(8,128)(2,1)S(1)} copy-done((bf16[8,8,40,256]{3,2,1,0:T(8,128)(2,1)S(1)}, bf16[8,8,40,256]{3,2,1,0:T(8,128)(2,1)}, u32[]{:S(2)}) %copy-start.5) | copy-done | bytes 1310744
  61.7 2.8 %cell_hits.1 = (bf16[640,2048]{1,0:T(8,128)(2,1)S(1)}, f32[640,256]{1,0:T(8,128)S(1)}, bf16[1920,2048]{1,0:T(8,128)(2,1)S(1)}, f32[1920,256]{1,0:T(8,128)S(1)}) custom-call(s32[1]{0:T(128)S(6)} %copy.20.count_ref, s32[1,2048]{1,0:T(1,128)S(1)} %bitcast.15, bf16[8,8,40,256]{3,2,1,0:T(8,128)(2,1)S(1)} %copy-done.5, f32[1,256]{1,0:T(1,128)S(1)} %bitcast.20), custom_call_target="tpu_custom_call" | custom-call | flops 3000000000 | bytes 15000000 | tf_op jit(solution)/shard_map/cell_hits/pallas_call | solution.py:418
  64.5 3.1 %copy-done = bf16[1920,2048]{1,0:T(8,128)(2,1)} copy-done((bf16[1920,2048]{1,0:T(8,128)(2,1)}, bf16[1920,2048]{1,0:T(8,128)(2,1)S(1)}, u32[]{:S(2)}) %copy-start) | copy-done | bytes 7864344
  67.6 1.6 %copy-done.3 = bf16[640,2048]{1,0:T(8,128)(2,1)} copy-done((bf16[640,2048]{1,0:T(8,128)(2,1)}, bf16[640,2048]{1,0:T(8,128)(2,1)S(1)}, u32[]{:S(2)}) %copy-start.3) | copy-done | bytes 2621464
  69.1 0.9 copy-done.6
  70.0 12.1 %all-to-all-done.1.back_ref = bf16[128,40,128]{2,1,0:T(8,128)(2,1)S(1)} async-done(((bf16[128,40,128]{2,1,0:T(8,128)(2,1)}), bf16[128,40,128]{2,1,0:T(8,128)(2,1)S(1)}, u32[]{:S(2)}, u32[]{:S(2)}) %all-to-all-start.1) | async-done | bytes 1310752 | tf_op jit(solution)/shard_map/all_to_all | solution.py:690
  82.1 1.7 %copy-done.4 = bf16[640,2048]{1,0:T(8,128)(2,1)S(1)} copy-done((bf16[640,2048]{1,0:T(8,128)(2,1)S(1)}, bf16[640,2048]{1,0:T(8,128)(2,1)}, u32[]{:S(2)}) %copy-start.4) | copy-done | bytes 2621464
  83.9 1.1 copy-done.7
  85.0 2.0 %place_edges.1 = (bf16[2048,256]{1,0:T(8,128)(2,1)S(1)}, bf16[2,320,256]{2,1,0:T(8,128)(2,1)S(1)}, bf16[320,256]{1,0:T(8,128)(2,1)S(1)}, bf16[320,256]{1,0:T(8,128)(2,1)S(1)}) custom-call(s32[1,128]{1,0:T(1,128)S(1)} %copy-done.17, bf16[128,40,128]{2,1,0:T(8,128)(2,1)S(1)} %all-to-all-done.1.back_ref, bf16[640,2048]{1,0:T(8,128)(2,1)S(1)} %copy-done.4, ...), custom_call_target="tpu_custom_call" | custom-call | flops 600000000 | bytes 4000000 | tf_op jit(solution)/shard_map/place_edges/pallas_call | solution.py:471
  87.0 1.7 %collective-permute-start.1 = (bf16[320,256]{1,0:T(8,128)(2,1)S(1)}, bf16[320,256]{1,0:T(8,128)(2,1)S(1)}, u32[]{:S(2)}, u32[]{:S(2)}) collective-permute-start(bf16[320,256]{1,0:T(8,128)(2,1)S(1)} %get-tuple-element.35.edge0_ref), channel_id=1, source_target_pairs={{1,0},{2,1},{3,2},{0,3},{5,4},{6,5},{7,6},{4,7},{9,8},{10,9},{11,1... | collective-permute-start | bytes 491528 | tf_op jit(solution)/shard_map/ppermute | solution.py:722
  88.6 0.4 collective-permute-start
  89.1 3.2 %copy-done.1 = bf16[1920,2048]{1,0:T(8,128)(2,1)S(1)} copy-done((bf16[1920,2048]{1,0:T(8,128)(2,1)S(1)}, bf16[1920,2048]{1,0:T(8,128)(2,1)}, u32[]{:S(2)}) %copy-start.1) | copy-done | bytes 7864344
  92.3 2.6 %place_mid.1 = (bf16[8,240,256]{2,1,0:T(8,128)(2,1)S(1)}, bf16[8,240,256]{2,1,0:T(8,128)(2,1)S(1)}) custom-call(bf16[2048,256]{1,0:T(8,128)(2,1)S(1)} %get-tuple-element.31.rows_ref, bf16[1920,2048]{1,0:T(8,128)(2,1)S(1)} %copy-done.1, f32[1920,256]{1,0:T(8,128)S(1)} %get-tuple-element.33.base_ref, f32[1,256]{1,0:T(1,128)S(1)} %bitcast.17), custom_call_target="tpu_custom_call" | custom-call | flops 2000000000 | bytes 6000000 | tf_op jit(solution)/shard_map/place_mid/pallas_call | solution.py:497
  94.9 0.0 copy-start.19
  94.9 0.2 collective-permute-done.low_ref
  95.2 0.1 collective-permute-start.2
  95.3 5.1 %collective-permute-start.3 = (bf16[400,256]{1,0:T(8,128)(2,1)S(1)}, bf16[400,256]{1,0:T(8,128)(2,1)S(1)}, u32[]{:S(2)}, u32[]{:S(2)}) collective-permute-start(bf16[400,256]{1,0:T(8,128)(2,1)S(1)} %get-tuple-element.38), channel_id=1, source_target_pairs={{4,0},{8,4},{12,8},{16,12},{20,16},{24,20},{28,24},{32,28},{36,32}... | collective-permute-start | bytes 614408 | tf_op jit(solution)/shard_map/ppermute | solution.py:728
  100.4 9.4 %conv_inner.1 = (bf16[2560,256]{1,0:T(8,128)(2,1)}, f32[2,320,256]{2,1,0:T(8,128)S(1)}) custom-call(bf16[8,240,256]{2,1,0:T(8,128)(2,1)S(1)} %get-tuple-element.34.mid_ref, bf16[320,256]{1,0:T(8,128)(2,1)S(1)} %get-tuple-element.35.edge0_ref, bf16[320,256]{1,0:T(8,128)(2,1)S(1)} %get-tuple-element.36.edge1_ref, ...), custom_call_target="tpu_custom_call" | custom-call | flops 8000000000 | bytes 10000000 | tf_op jit(solution)/shard_map/conv_inner/pallas_call | solution.py:620
  109.8 0.0 collective-permute-done.2.low_ref
  109.8 1.9 %conv_edges.1 = bf16[2560,256]{1,0:T(8,128)(2,1)} custom-call(bf16[400,256]{1,0:T(8,128)(2,1)S(1)} %collective-permute-done.2.low_ref, bf16[400,256]{1,0:T(8,128)(2,1)S(1)} %collective-permute-done.3.high_ref, f32[2,320,256]{2,1,0:T(8,128)S(1)} %get-tuple-element.41.partial_ref, ...), custom_call_target="tpu_custom_call", output_to_operand_aliasing={{}: (6, {})} | custom-call | tf_op jit(solution)/shard_map/conv_edges/pallas_call | solution.py:673
  (27 shorter events, 0.1 us)
Async XLA Ops:
  7.8 33.0 %copy-start.8 = (bf16[256,1024]{1,0:T(8,128)(2,1)S(1)}, bf16[256,1024]{1,0:T(8,128)(2,1)}, u32[]{:S(2)}) copy-start(bf16[256,1024]{1,0:T(8,128)(2,1)} %mlp_in_ref.1) | copy-start | bytes 1572868
  7.8 33.0 %copy-start.9 = (bf16[1024,256]{1,0:T(8,128)(2,1)S(1)}, bf16[1024,256]{1,0:T(8,128)(2,1)}, u32[]{:S(2)}) copy-start(bf16[1024,256]{1,0:T(8,128)(2,1)} %mlp_out_ref.1) | copy-start | bytes 1572868
  7.8 33.0 %copy-start.10 = (bf16[256,768]{1,0:T(8,128)(2,1)S(1)}, bf16[256,768]{1,0:T(8,128)(2,1)}, u32[]{:S(2)}) copy-start(bf16[256,768]{1,0:T(8,128)(2,1)} %attn_in_ref.1) | copy-start | bytes 1179652
  7.8 33.0 %copy-start.11 = (bf16[256,256]{1,0:T(8,128)(2,1)S(1)}, bf16[256,256]{1,0:T(8,128)(2,1)}, u32[]{:S(2)}) copy-start(bf16[256,256]{1,0:T(8,128)(2,1)} %attn_out_ref.1) | copy-start | bytes 393220
  7.8 32.9 %copy-start.13 = (s32[1,1024]{1,0:T(1,128)S(1)}, s32[1,1024]{1,0:T(1,128)}, u32[]{:S(2)}) copy-start(s32[1,1024]{1,0:T(1,128)} %window_ref.1) | copy-start | bytes 12292
  7.8 32.9 %copy-start.15 = (f32[256]{0:T(256)S(1)}, f32[256]{0:T(256)}, u32[]{:S(2)}) copy-start(f32[256]{0:T(256)} %param.24) | copy-start | bytes 3076
  7.8 32.9 %copy-start.16 = (f32[256]{0:T(256)S(1)}, f32[256]{0:T(256)}, u32[]{:S(2)}) copy-start(f32[256]{0:T(256)} %param.27) | copy-start | bytes 3076
  55.6 4.8 %copy-start.12 = (s32[2048]{0:T(1024)S(1)}, s32[2048]{0:T(1024)}, u32[]{:S(2)}) copy-start(s32[2048]{0:T(1024)} %param.19) | copy-start | bytes 24580
  55.6 4.8 %copy-start.18 = (f32[256]{0:T(256)S(1)}, f32[256]{0:T(256)}, u32[]{:S(2)}) copy-start(f32[256]{0:T(256)} %param.30) | copy-start | bytes 3076
  55.6 26.5 %all-to-all-start.1 = ((bf16[128,40,128]{2,1,0:T(8,128)(2,1)}), bf16[128,40,128]{2,1,0:T(8,128)(2,1)S(1)}, u32[]{:S(2)}, u32[]{:S(2)}) async-start(bf16[128,40,128]{2,1,0:T(8,128)(2,1)} %owner_encode.1), calls=%async_computation.1 | async-start | bytes 2621440 | tf_op jit(solution)/shard_map/all_to_all | solution.py:690
  60.4 1.3 %copy-start.5 = (bf16[8,8,40,256]{3,2,1,0:T(8,128)(2,1)S(1)}, bf16[8,8,40,256]{3,2,1,0:T(8,128)(2,1)}, u32[]{:S(2)}) copy-start(bf16[8,8,40,256]{3,2,1,0:T(8,128)(2,1)} %pos_ref.1) | copy-start | bytes 3932164
  61.7 20.4 %copy-start.14 = (f32[256]{0:T(256)S(1)}, f32[256]{0:T(256)}, u32[]{:S(2)}) copy-start(f32[256]{0:T(256)} %param.31) | copy-start | bytes 3076
  61.7 20.4 %copy-start.17 = (s32[1,128]{1,0:T(1,128)S(1)}, s32[1,128]{1,0:T(1,128)}, u32[]{:S(2)}) copy-start(s32[1,128]{1,0:T(1,128)} %get-tuple-element.24.starts_ref) | copy-start | bytes 1540
  64.5 3.1 %copy-start = (bf16[1920,2048]{1,0:T(8,128)(2,1)}, bf16[1920,2048]{1,0:T(8,128)(2,1)S(1)}, u32[]{:S(2)}) copy-start(bf16[1920,2048]{1,0:T(8,128)(2,1)S(1)} %get-tuple-element.32.hit_ref) | copy-start | bytes 23592964
  67.6 1.6 %copy-start.3 = (bf16[640,2048]{1,0:T(8,128)(2,1)}, bf16[640,2048]{1,0:T(8,128)(2,1)S(1)}, u32[]{:S(2)}) copy-start(bf16[640,2048]{1,0:T(8,128)(2,1)S(1)} %get-tuple-element.29.hit_ref) | copy-start | bytes 7864324
  69.1 0.9 copy-start.6
  82.1 1.7 %copy-start.4 = (bf16[640,2048]{1,0:T(8,128)(2,1)S(1)}, bf16[640,2048]{1,0:T(8,128)(2,1)}, u32[]{:S(2)}) copy-start(bf16[640,2048]{1,0:T(8,128)(2,1)} %copy-done.3) | copy-start | bytes 7864324
  83.9 1.1 copy-start.7
  87.0 8.0 %collective-permute-start.1 = (bf16[320,256]{1,0:T(8,128)(2,1)S(1)}, bf16[320,256]{1,0:T(8,128)(2,1)S(1)}, u32[]{:S(2)}, u32[]{:S(2)}) collective-permute-start(bf16[320,256]{1,0:T(8,128)(2,1)S(1)} %get-tuple-element.35.edge0_ref), channel_id=1, source_target_pairs={{1,0},{2,1},{3,2},{0,3},{5,4},{6,5},{7,6},{4,7},{9,8},{10,9},{11,1... | collective-permute-start | bytes 491528 | tf_op jit(solution)/shard_map/ppermute | solution.py:722
  88.6 6.6 %collective-permute-start = (bf16[320,256]{1,0:T(8,128)(2,1)S(1)}, bf16[320,256]{1,0:T(8,128)(2,1)S(1)}, u32[]{:S(2)}, u32[]{:S(2)}) collective-permute-start(bf16[320,256]{1,0:T(8,128)(2,1)S(1)} %get-tuple-element.36.edge1_ref), channel_id=1, source_target_pairs={{0,1},{1,2},{2,3},{3,0},{4,5},{5,6},{6,7},{7,4},{8,9},{9,10},{10,1... | collective-permute-start | bytes 491528 | tf_op jit(solution)/shard_map/ppermute | solution.py:721
  89.0 3.2 %copy-start.1 = (bf16[1920,2048]{1,0:T(8,128)(2,1)S(1)}, bf16[1920,2048]{1,0:T(8,128)(2,1)}, u32[]{:S(2)}) copy-start(bf16[1920,2048]{1,0:T(8,128)(2,1)} %copy-done) | copy-start | bytes 23592964
  92.3 8.1 %copy-start.2 = (bf16[27,256,256]{2,1,0:T(8,128)(2,1)S(1)}, bf16[27,256,256]{2,1,0:T(8,128)(2,1)}, u32[]{:S(2)}) copy-start(bf16[27,256,256]{2,1,0:T(8,128)(2,1)} %param.32) | copy-start | bytes 10616836
  94.9 5.4 %copy-start.19 = (f32[256]{0:T(256)S(1)}, f32[256]{0:T(256)}, u32[]{:S(2)}) copy-start(f32[256]{0:T(256)} %param.33) | copy-start | bytes 3076
  95.2 14.6 %collective-permute-start.2 = (bf16[400,256]{1,0:T(8,128)(2,1)S(1)}, bf16[400,256]{1,0:T(8,128)(2,1)S(1)}, u32[]{:S(2)}, u32[]{:S(2)}) collective-permute-start(bf16[400,256]{1,0:T(8,128)(2,1)S(1)} %get-tuple-element.37), channel_id=1, source_target_pairs={{0,4},{4,8},{8,12},{12,16},{16,20},{20,24},{24,28},{28,32},{32,36}... | collective-permute-start | bytes 614408 | tf_op jit(solution)/shard_map/ppermute | solution.py:727
  95.3 14.5 %collective-permute-start.3 = (bf16[400,256]{1,0:T(8,128)(2,1)S(1)}, bf16[400,256]{1,0:T(8,128)(2,1)S(1)}, u32[]{:S(2)}, u32[]{:S(2)}) collective-permute-start(bf16[400,256]{1,0:T(8,128)(2,1)S(1)} %get-tuple-element.38), channel_id=1, source_target_pairs={{4,0},{8,4},{12,8},{16,12},{20,16},{24,20},{28,24},{32,28},{36,32}... | collective-permute-start | bytes 614408 | tf_op jit(solution)/shard_map/ppermute | solution.py:728

commit v4 on v2

--- a/solution.py
+++ b/solution.py
@@ -9,6 +9,7 @@
 EPSILON = 1e-05
 F32 = jnp.float32
 BF16 = jnp.bfloat16
+I16 = jnp.int16
 I32 = jnp.int32
 CAP = 18
 MSG = 40
@@ -20,6 +21,15 @@
 
 def one_hot(mask):
     return jnp.where(mask, 1.0, 0.0).astype(BF16)
+
+
+def match(col, row):
+    n, k = col.shape[0], row.shape[1]
+    col = jnp.broadcast_to(col, (n, 128)).astype(I16)
+    row = jnp.broadcast_to(row, (16, k)).astype(I16)
+    col = jnp.concatenate([col] * (k // 128), axis=1)
+    row = jnp.concatenate([row] * (n // 16), axis=0)
+    return jnp.where(col == row, jnp.ones((), BF16), jnp.zeros((), BF16))
 
 
 def dot(a, b):
@@ -107,7 +117,7 @@
     step = 512
     for b in range(entries // step):
         col = jnp.concatenate(cell_cols[b * step // 128 : (b + 1) * step // 128], axis=0)
-        pick = one_hot(iota((step, cell_total), 1) == col)
+        pick = match(col, iota((1, cell_total), 1))
         rows = vis_in[b * step : (b + 1) * step, :].astype(F32) + dot(pick, pos_in[...])
         rows = rows.astype(BF16).astype(F32)
         left_scr[b * step : (b + 1) * step, :] = rows[:, 0:128]
@@ -224,7 +234,7 @@
     step = 1024
     for b in range(rows // step):
         part = slice(b * step, (b + 1) * step)
-        sel = one_hot(slot_row == iota((step, slot_row.shape[1]), 0) + b * step)
+        sel = match(iota((step, 1), 0) + b * step, slot_row)
         x = dot(sel[:, :full], main) + dot(sel[:, full:], rest)
         x_scr[part, :] = x
         normed = layer_norm(x, gain1_ref[...]).astype(BF16)
@@ -338,7 +348,7 @@
                 jnp.sum(jnp.where(eye128, slot_f[:, at : at + 128], 0.0), axis=1, keepdims=True)
             )
         col = jnp.concatenate(cols, axis=0).astype(I32)
-        pick = one_hot(iota((size, rows), 1) == col)
+        pick = match(col, iota((1, rows), 1))
         out = dot(pick, q_scr[...])
         if b < full // step:
             o = b * step // 16
@@ -381,9 +391,10 @@
 
 
 def fill_cells(ids, cells, rows, token, pos, gain):
-    hit = jnp.where(cells == ids, 1.0, 0.0)
-    filled = dot(hit.astype(BF16), rows)
-    seen = jnp.sum(hit, axis=1, keepdims=True)
+    hit = match(ids, cells)
+    filled = dot(hit, rows)
+    seen = sum([hit[:, i : i + 128] for i in range(0, hit.shape[1], 128)])
+    seen = jnp.sum(seen.astype(F32), axis=1, keepdims=True)
     filled = jnp.where(seen > 0.5, filled, token)
     dec = (filled + pos.astype(F32)).astype(BF16)
     return dec, layer_norm(dec.astype(F32), gain).astype(BF16)
@@ -415,7 +426,7 @@
     cells = jnp.where(iota((1, entries), 1) < count_ref[0], cells_ref[...], -1)
     at = [(a, r) for r in (0, rad - 1) for a in range(az)]
     ids = jnp.concatenate(
-        [iota((height, entries), 0) + (a * rad + r) * height for a, r in at], axis=0
+        [iota((height, 1), 0) + (a * rad + r) * height for a, r in at], axis=0
     )
     pos = jnp.concatenate([pos_ref[a, r].astype(F32) for a, r in at], axis=0)
     dec, normed = fill_cells(ids, cells, rows, token_ref[...], pos, gain_ref[...])
@@ -454,7 +465,7 @@
     cells = jnp.where(iota((1, entries), 1) < count_ref[0], cells_ref[...], -1)
     for a in range(0, az, 2):
         ids = jnp.concatenate(
-            [iota((size, entries), 0) + (i * rad + 1) * height for i in (a, a + 1)], axis=0
+            [iota((size, 1), 0) + (i * rad + 1) * height for i in (a, a + 1)], axis=0
         )
         pos = jnp.concatenate(
             [pos_ref[i, 1 : rad - 1].reshape(size, channels) for i in (a, a + 1)], axis=0
@@ -480,16 +491,22 @@
     )(vis_count, rows, cells, pos, token, gain)
 
 
+def ring_ends():
+    place = lax.axis_index("blk")
+    return place == 0, place == lax.axis_size("blk") - 1
+
+
 def rim_kernel(mid_ref, edge0_ref, edge1_ref, low_ref, high_ref, first_ref, last_ref):
     az, size, channels = mid_ref.shape
     height = low_ref.shape[0] // az
+    inside, outside = ring_ends()
     for a, ref in ((0, first_ref), (az - 1, last_ref)):
         part = slice(a * height, (a + 1) * height)
-        ref[0:height] = low_ref[part]
+        ref[0:height] = jnp.where(inside, 0.0, low_ref[part].astype(F32)).astype(BF16)
         ref[height : 2 * height] = edge0_ref[part]
         ref[2 * height : 2 * height + size] = mid_ref[a]
         ref[2 * height + size : 3 * height + size] = edge1_ref[part]
-        ref[3 * height + size :] = high_ref[part]
+        ref[3 * height + size :] = jnp.where(outside, 0.0, high_ref[part].astype(F32)).astype(BF16)
 
 
 def rim_rows(mid, edge0, edge1, low, high):
@@ -506,10 +523,13 @@
     )(mid, edge0, edge1, low, high)
 
 
-def widen(scr, at, rows, height):
+def widen(scr, at, rows, height, drop=None):
     n, channels = rows.shape
     h = iota((n, 1), 0) % height
     values = rows.astype(F32)
+    if drop is not None:
+        values = jnp.where(drop, 0.0, values)
+        rows = values.astype(BF16)
     scr[at : at + n, channels : 2 * channels] = rows
     below = jnp.where(h == 0, 0.0, pltpu.roll(values, 1, 0))
     scr[at : at + n, 0:channels] = below.astype(BF16)
@@ -526,15 +546,16 @@
     height = low_ref.shape[0] // az
     plane = size + 2 * height
     pitch = plane + 2 * height
+    inside, outside = ring_ends()
 
     def spread(a):
         base = a * pitch
         part = slice(a * height, (a + 1) * height)
-        widen(wide_scr, base, low_ref[part], height)
+        widen(wide_scr, base, low_ref[part], height, inside)
         widen(wide_scr, base + height, edge0_ref[part], height)
         widen(wide_scr, base + 2 * height, mid_ref[a], height)
         widen(wide_scr, base + 2 * height + size, edge1_ref[part], height)
-        widen(wide_scr, base + 3 * height + size, high_ref[part], height)
+        widen(wide_scr, base + 3 * height + size, high_ref[part], height, outside)
 
     def taps(a):
         total = jnp.broadcast_to(bias_ref[...], (plane, channels))
@@ -678,7 +699,7 @@
     token = mask_token.reshape(1, -1)
     gain = dec_gain.reshape(1, -1)
     rows, edge_dec, edge0, edge1 = place_edges(vis_count, starts, back, cells, grid_pos, token, gain)
-    outward = [(i, i + 1) for i in range(n_blk - 1)]
+    outward = [(i, (i + 1) % n_blk) for i in range(n_blk)]
     inward = [(t, s) for s, t in outward]
     rad_low = lax.ppermute(edge1, "blk", outward)
     rad_high = lax.ppermute(edge0, "blk", inward)

time: 110 us -> 108 us (0.982)
  starting transfers between devices: 11 us -> 7.22 us
  waiting for transfers between devices: 0.01 us -> 3.04 us
    ppermute x1, starting transfers between devices: 4.56 us -> 0.42 us  [body(): rad_low = lax.ppermute(edge1, 'blk', outward)]
    ppermute x1, waiting for transfers between devices: 0.01 us -> 1.79 us  [body(): rad_low = lax.ppermute(edge1, 'blk', outward)]
    ppermute x1, waiting for transfers between devices: 0.01 us -> 1.25 us  [body(): rad_high = lax.ppermute(edge0, 'blk', inward)]
  transfers between devices with their start and end apart: 4 -> 4, of which waited for: 0 -> 2; matrix products, arithmetic and copies ran while one was open for 0% -> 0% of each run, Pallas kernels for 12% -> 12%
where the time goes in v4:
time: 108 us
  blocking collectives  58.7 us (54%)
  Pallas kernels  37.5 us (35%)
  starting transfers between devices  7.22 us (7%)
  waiting for transfers between devices  3.04 us (3%)
  between operations  1.08 us (1%)
    all_to_all x2, blocking collectives, exchange(): lax.all_to_all(values, ('sector', 'blk'), split_axis=0, concat_axis=0, ti...  58.7 us
    pallas_call x1, Pallas kernels, owner_encode(): pl.pallas_call(owner_kernel, out_shape=jax.ShapeDtypeStruct((owners, MSG,...  13.8 us
    pallas_call x1, Pallas kernels, conv_inner(): pl.pallas_call(conv_kernel, out_shape=(jax.ShapeDtypeStruct((az * plane,...  9.42 us
    pallas_call x1, Pallas kernels, send_rows(): pl.pallas_call(send_kernel, out_shape=(jax.ShapeDtypeStruct((owners, MSG,...  7.09 us
    ppermute x1, starting transfers between devices, body(): az_high = lax.ppermute(first, 'sector', down)  5.05 us
    pallas_call x1, Pallas kernels, place_mid(): pl.pallas_call(mid_kernel, out_shape=(mid, mid), in_specs=[smem] + [vmem]...  3.08 us
    pallas_call x1, Pallas kernels, place_edges(): pl.pallas_call(edge_kernel, out_shape=(jax.ShapeDtypeStruct((entries, cha...  2.19 us
  transfers between devices with their start and end apart: 4, of which 2 were waited for; matrix products, arithmetic and copies ran while one was open for 0% of the time, Pallas kernels for 12%

profile of v4, /device:TPU:0, one launch (start us, length us, event | category | flops | bytes accessed | tf_op | source)
XLA Modules:
  0.0 107.7 jit_solution(293223517839108134)
XLA Ops:
  0.7 7.1 %send_rows.1 = (bf16[128,40,128]{2,1,0:T(8,128)(2,1)}, s32[1,128]{1,0:T(1,128)}) custom-call(s32[1]{0:T(128)S(6)} %copy.20.count_ref, s32[1,2048]{1,0:T(1,128)} %bitcast.14, s32[1,2048]{1,0:T(1,128)} %bitcast.24, s32[1,2048]{1,0:T(1,128)} %bitcast.25, bf16[2048,256]{1,0:T(8,128)(2,1)} %vis_ref.1, bf16[2560,256]{1,0:T(8,128)(2,1)} %bitcast.11), custom_call_target="tpu_custom_call" | custom-call | tf_op jit(solution)/shard_map/send_rows/pallas_call | solution.py:147
  7.8 0.0 copy-start.2
  7.8 0.0 copy-start.3
  7.8 0.0 copy-start.4
  7.8 0.0 copy-start.5
  7.8 0.0 copy-start.7
  7.8 0.0 copy-start.8
  7.8 0.0 copy-start.9
  7.8 32.9 %all_to_all.10.msg_ref = bf16[128,40,128]{2,1,0:T(8,128)(2,1)S(1)} all-to-all(bf16[128,40,128]{2,1,0:T(8,128)(2,1)} %get-tuple-element.18), channel_id=1, replica_groups=mesh['sector'=32,'blk'=4] {'sector','blk'}, dimensions={0} | all-to-all | bytes 2621440 | tf_op jit(solution)/shard_map/all_to_all | solution.py:676
  40.7 0.0 copy-done.2
  40.8 13.8 %owner_encode.1 = bf16[128,40,128]{2,1,0:T(8,128)(2,1)S(1)} custom-call(bf16[128,40,128]{2,1,0:T(8,128)(2,1)S(1)} %all_to_all.10.msg_ref, s32[1,1024]{1,0:T(1,128)S(1)} %copy-done.7, f32[1,256]{1,0:T(1,128)S(1)} %bitcast.17, bf16[256,768]{1,0:T(8,128)(2,1)S(1)} %copy-done.4, bf16[256,256]{1,0:T(8,128)(2,1)S(1)} %copy-done.5, f32[1,256]{1,0:T(1,128)S(1)} %bitcast.18, ...), custom_call_target="tpu_custom_call" | custom-call | tf_op jit(solution)/shard_map/owner_encode/pallas_call | solution.py:373
  54.6 0.0 copy-start
  54.6 0.0 copy-start.6
  54.6 0.0 copy-start.10
  54.6 0.0 copy-start.11
  54.6 0.0 copy-start.12
  54.6 25.9 %all_to_all.11.back_ref = bf16[128,40,128]{2,1,0:T(8,128)(2,1)S(1)} all-to-all(bf16[128,40,128]{2,1,0:T(8,128)(2,1)S(1)} %owner_encode.1), channel_id=1, replica_groups=mesh['sector'=32,'blk'=4] {'sector','blk'}, dimensions={0} | all-to-all | bytes 2621440 | tf_op jit(solution)/shard_map/all_to_all | solution.py:676
  80.5 0.0 copy-done
  80.5 2.2 %place_edges.1 = (bf16[2048,256]{1,0:T(8,128)(2,1)S(1)}, bf16[2,320,256]{2,1,0:T(8,128)(2,1)S(1)}, bf16[320,256]{1,0:T(8,128)(2,1)S(1)}, bf16[320,256]{1,0:T(8,128)(2,1)S(1)}) custom-call(s32[1]{0:T(128)S(6)} %copy.20.count_ref, s32[1,128]{1,0:T(1,128)S(1)} %copy-done.12, bf16[128,40,128]{2,1,0:T(8,128)(2,1)S(1)} %all_to_all.11.back_ref, ...), custom_call_target="tpu_custom_call" | custom-call | flops 600000000 | bytes 4000000 | tf_op jit(solution)/shard_map/place_edges/pallas_call | solution.py:445
  82.7 1.7 %collective-permute-start.1 = (bf16[320,256]{1,0:T(8,128)(2,1)S(1)}, bf16[320,256]{1,0:T(8,128)(2,1)S(1)}, u32[]{:S(2)}, u32[]{:S(2)}) collective-permute-start(bf16[320,256]{1,0:T(8,128)(2,1)S(1)} %get-tuple-element.21.edge0_ref), channel_id=1, source_target_pairs={{1,0},{2,1},{3,2},{0,3},{5,4},{6,5},{7,6},{4,7},{9,8},{10,9},{11,1... | collective-permute-start | bytes 491528 | tf_op jit(solution)/shard_map/ppermute | solution.py:705
  84.4 0.4 collective-permute-start
  84.8 3.1 %place_mid.1 = (bf16[8,240,256]{2,1,0:T(8,128)(2,1)S(1)}, bf16[8,240,256]{2,1,0:T(8,128)(2,1)S(1)}) custom-call(s32[1]{0:T(128)S(6)} %copy.20.count_ref, bf16[2048,256]{1,0:T(8,128)(2,1)S(1)} %get-tuple-element.19.rows_ref, s32[1,2048]{1,0:T(1,128)S(1)} %bitcast.16, bf16[8,8,40,256]{3,2,1,0:T(8,128)(2,1)S(1)} %copy-done, f32[1,256]{1,0:T(1,128)S(1)} %bitcast.20, ...), custom_call_target="tpu_custom_call" | custom-call | flops 2000000000 | bytes 6000000 | tf_op jit(solution)/shard_map/place_mid/pallas_call | solution.py:483
  87.9 0.0 copy-start.13
  87.9 1.2 %collective-permute-done.1.high_ref = bf16[320,256]{1,0:T(8,128)(2,1)S(1)} collective-permute-done((bf16[320,256]{1,0:T(8,128)(2,1)S(1)}, bf16[320,256]{1,0:T(8,128)(2,1)S(1)}, u32[]{:S(2)}, u32[]{:S(2)}) %collective-permute-start.1) | collective-permute-done | bytes 163872 | tf_op jit(solution)/shard_map/ppermute | solution.py:705
  89.2 1.8 %collective-permute-done.low_ref = bf16[320,256]{1,0:T(8,128)(2,1)S(1)} collective-permute-done((bf16[320,256]{1,0:T(8,128)(2,1)S(1)}, bf16[320,256]{1,0:T(8,128)(2,1)S(1)}, u32[]{:S(2)}, u32[]{:S(2)}) %collective-permute-start) | collective-permute-done | bytes 163872 | tf_op jit(solution)/shard_map/ppermute | solution.py:704
  91.0 0.1 collective-permute-start.2
  91.1 5.1 %collective-permute-start.3 = (bf16[400,256]{1,0:T(8,128)(2,1)S(1)}, bf16[400,256]{1,0:T(8,128)(2,1)S(1)}, u32[]{:S(2)}, u32[]{:S(2)}) collective-permute-start(bf16[400,256]{1,0:T(8,128)(2,1)S(1)} %get-tuple-element.24), channel_id=1, source_target_pairs={{4,0},{8,4},{12,8},{16,12},{20,16},{24,20},{28,24},{32,28},{36,32}... | collective-permute-start | bytes 614408 | tf_op jit(solution)/shard_map/ppermute | solution.py:711
  96.1 0.0 copy-done.13
  96.1 9.4 %conv_inner.1 = (bf16[2560,256]{1,0:T(8,128)(2,1)}, f32[2,320,256]{2,1,0:T(8,128)S(1)}) custom-call(bf16[8,240,256]{2,1,0:T(8,128)(2,1)S(1)} %get-tuple-element.20.mid_ref, bf16[320,256]{1,0:T(8,128)(2,1)S(1)} %get-tuple-element.21.edge0_ref, bf16[320,256]{1,0:T(8,128)(2,1)S(1)} %get-tuple-element.22.edge1_ref, ...), custom_call_target="tpu_custom_call" | custom-call | flops 8000000000 | bytes 10000000 | tf_op jit(solution)/shard_map/conv_inner/pallas_call | solution.py:606
  105.6 0.0 collective-permute-done.2.low_ref
  105.6 0.0 collective-permute-done.3.high_ref
  105.6 1.9 %conv_edges.1 = bf16[2560,256]{1,0:T(8,128)(2,1)} custom-call(bf16[400,256]{1,0:T(8,128)(2,1)S(1)} %collective-permute-done.2.low_ref, bf16[400,256]{1,0:T(8,128)(2,1)S(1)} %collective-permute-done.3.high_ref, f32[2,320,256]{2,1,0:T(8,128)S(1)} %get-tuple-element.27.partial_ref, ...), custom_call_target="tpu_custom_call", output_to_operand_aliasing={{}: (6, {})} | custom-call | tf_op jit(solution)/shard_map/conv_edges/pallas_call | solution.py:659
  (13 shorter events, 0.1 us)
Async XLA Ops:
  7.8 33.0 %copy-start.2 = (bf16[256,1024]{1,0:T(8,128)(2,1)S(1)}, bf16[256,1024]{1,0:T(8,128)(2,1)}, u32[]{:S(2)}) copy-start(bf16[256,1024]{1,0:T(8,128)(2,1)} %mlp_in_ref.1) | copy-start | bytes 1572868
  7.8 33.0 %copy-start.3 = (bf16[1024,256]{1,0:T(8,128)(2,1)S(1)}, bf16[1024,256]{1,0:T(8,128)(2,1)}, u32[]{:S(2)}) copy-start(bf16[1024,256]{1,0:T(8,128)(2,1)} %mlp_out_ref.1) | copy-start | bytes 1572868
  7.8 33.0 %copy-start.4 = (bf16[256,768]{1,0:T(8,128)(2,1)S(1)}, bf16[256,768]{1,0:T(8,128)(2,1)}, u32[]{:S(2)}) copy-start(bf16[256,768]{1,0:T(8,128)(2,1)} %attn_in_ref.1) | copy-start | bytes 1179652
  7.8 33.0 %copy-start.5 = (bf16[256,256]{1,0:T(8,128)(2,1)S(1)}, bf16[256,256]{1,0:T(8,128)(2,1)}, u32[]{:S(2)}) copy-start(bf16[256,256]{1,0:T(8,128)(2,1)} %attn_out_ref.1) | copy-start | bytes 393220
  7.8 32.9 %copy-start.7 = (s32[1,1024]{1,0:T(1,128)S(1)}, s32[1,1024]{1,0:T(1,128)}, u32[]{:S(2)}) copy-start(s32[1,1024]{1,0:T(1,128)} %window_ref.1) | copy-start | bytes 12292
  7.8 32.9 %copy-start.8 = (f32[256]{0:T(256)S(1)}, f32[256]{0:T(256)}, u32[]{:S(2)}) copy-start(f32[256]{0:T(256)} %param.24) | copy-start | bytes 3076
  7.8 32.9 %copy-start.9 = (f32[256]{0:T(256)S(1)}, f32[256]{0:T(256)}, u32[]{:S(2)}) copy-start(f32[256]{0:T(256)} %param.27) | copy-start | bytes 3076
  54.6 25.9 %copy-start = (bf16[8,8,40,256]{3,2,1,0:T(8,128)(2,1)S(1)}, bf16[8,8,40,256]{3,2,1,0:T(8,128)(2,1)}, u32[]{:S(2)}) copy-start(bf16[8,8,40,256]{3,2,1,0:T(8,128)(2,1)} %pos_ref.3) | copy-start | bytes 3932164
  54.6 25.9 %copy-start.6 = (s32[2048]{0:T(1024)S(1)}, s32[2048]{0:T(1024)}, u32[]{:S(2)}) copy-start(s32[2048]{0:T(1024)} %param.19) | copy-start | bytes 24580
  54.6 25.9 %copy-start.10 = (f32[256]{0:T(256)S(1)}, f32[256]{0:T(256)}, u32[]{:S(2)}) copy-start(f32[256]{0:T(256)} %param.30) | copy-start | bytes 3076
  54.6 25.9 %copy-start.11 = (f32[256]{0:T(256)S(1)}, f32[256]{0:T(256)}, u32[]{:S(2)}) copy-start(f32[256]{0:T(256)} %param.31) | copy-start | bytes 3076
  54.6 25.9 %copy-start.12 = (s32[1,128]{1,0:T(1,128)S(1)}, s32[1,128]{1,0:T(1,128)}, u32[]{:S(2)}) copy-start(s32[1,128]{1,0:T(1,128)} %get-tuple-element.17.starts_ref) | copy-start | bytes 1540
  82.7 6.4 %collective-permute-start.1 = (bf16[320,256]{1,0:T(8,128)(2,1)S(1)}, bf16[320,256]{1,0:T(8,128)(2,1)S(1)}, u32[]{:S(2)}, u32[]{:S(2)}) collective-permute-start(bf16[320,256]{1,0:T(8,128)(2,1)S(1)} %get-tuple-element.21.edge0_ref), channel_id=1, source_target_pairs={{1,0},{2,1},{3,2},{0,3},{5,4},{6,5},{7,6},{4,7},{9,8},{10,9},{11,1... | collective-permute-start | bytes 491528 | tf_op jit(solution)/shard_map/ppermute | solution.py:705
  84.4 6.6 %collective-permute-start = (bf16[320,256]{1,0:T(8,128)(2,1)S(1)}, bf16[320,256]{1,0:T(8,128)(2,1)S(1)}, u32[]{:S(2)}, u32[]{:S(2)}) collective-permute-start(bf16[320,256]{1,0:T(8,128)(2,1)S(1)} %get-tuple-element.22.edge1_ref), channel_id=1, source_target_pairs={{0,1},{1,2},{2,3},{3,0},{4,5},{5,6},{6,7},{7,4},{8,9},{9,10},{10,1... | collective-permute-start | bytes 491528 | tf_op jit(solution)/shard_map/ppermute | solution.py:704
  84.8 11.3 %copy-start.1 = (bf16[27,256,256]{2,1,0:T(8,128)(2,1)S(1)}, bf16[27,256,256]{2,1,0:T(8,128)(2,1)}, u32[]{:S(2)}) copy-start(bf16[27,256,256]{2,1,0:T(8,128)(2,1)} %param.32) | copy-start | bytes 10616836
  87.9 8.2 %copy-start.13 = (f32[256]{0:T(256)S(1)}, f32[256]{0:T(256)}, u32[]{:S(2)}) copy-start(f32[256]{0:T(256)} %param.33) | copy-start | bytes 3076
  91.0 14.6 %collective-permute-start.2 = (bf16[400,256]{1,0:T(8,128)(2,1)S(1)}, bf16[400,256]{1,0:T(8,128)(2,1)S(1)}, u32[]{:S(2)}, u32[]{:S(2)}) collective-permute-start(bf16[400,256]{1,0:T(8,128)(2,1)S(1)} %get-tuple-element.23), channel_id=1, source_target_pairs={{0,4},{4,8},{8,12},{12,16},{16,20},{20,24},{24,28},{28,32},{32,36}... | collective-permute-start | bytes 614408 | tf_op jit(solution)/shard_map/ppermute | solution.py:710
  91.1 14.5 %collective-permute-start.3 = (bf16[400,256]{1,0:T(8,128)(2,1)S(1)}, bf16[400,256]{1,0:T(8,128)(2,1)S(1)}, u32[]{:S(2)}, u32[]{:S(2)}) collective-permute-start(bf16[400,256]{1,0:T(8,128)(2,1)S(1)} %get-tuple-element.24), channel_id=1, source_target_pairs={{4,0},{8,4},{12,8},{16,12},{20,16},{24,20},{28,24},{32,28},{36,32}... | collective-permute-start | bytes 614408 | tf_op jit(solution)/shard_map/ppermute | solution.py:711

commit v5 on v4

--- a/solution.py
+++ b/solution.py
@@ -496,17 +496,34 @@
     return place == 0, place == lax.axis_size("blk") - 1
 
 
-def rim_kernel(mid_ref, edge0_ref, edge1_ref, low_ref, high_ref, first_ref, last_ref):
+def even_sector():
+    return lax.bitwise_and(lax.axis_index("sector"), 1) == 0
+
+
+def rim_kernel(mid_ref, edge0_ref, edge1_ref, low_ref, high_ref, near_ref, far_ref):
     az, size, channels = mid_ref.shape
     height = low_ref.shape[0] // az
     inside, outside = ring_ends()
-    for a, ref in ((0, first_ref), (az - 1, last_ref)):
+
+    def fill(ref, a):
         part = slice(a * height, (a + 1) * height)
         ref[0:height] = jnp.where(inside, 0.0, low_ref[part].astype(F32)).astype(BF16)
         ref[height : 2 * height] = edge0_ref[part]
         ref[2 * height : 2 * height + size] = mid_ref[a]
         ref[2 * height + size : 3 * height + size] = edge1_ref[part]
         ref[3 * height + size :] = jnp.where(outside, 0.0, high_ref[part].astype(F32)).astype(BF16)
+
+    even = even_sector()
+
+    @pl.when(even)
+    def _():
+        fill(near_ref, az - 1)
+        fill(far_ref, 0)
+
+    @pl.when(jnp.logical_not(even))
+    def _():
+        fill(near_ref, 0)
+        fill(far_ref, az - 1)
 
 
 def rim_rows(mid, edge0, edge1, low, high):
@@ -623,7 +640,7 @@
 
 
 def conv_edge_kernel(
-    low_ref, high_ref, partial_ref, mid_dec_ref, edge_dec_ref, weight_ref, given_ref,
+    near_ref, far_ref, partial_ref, mid_dec_ref, edge_dec_ref, weight_ref, given_ref,
     out_ref,
     wide_scr, done_scr, out_sems,
 ):
@@ -631,8 +648,18 @@
     plane = partial_ref.shape[1]
     height = (plane - size) // 2
     pitch = plane + 2 * height
-    widen(wide_scr, 0, low_ref[...], height)
-    widen(wide_scr, pitch, high_ref[...], height)
+    even = even_sector()
+
+    @pl.when(even)
+    def _():
+        widen(wide_scr, 0, far_ref[...], height)
+        widen(wide_scr, pitch, near_ref[...], height)
+
+    @pl.when(jnp.logical_not(even))
+    def _():
+        widen(wide_scr, 0, near_ref[...], height)
+        widen(wide_scr, pitch, far_ref[...], height)
+
     stores = []
     for i in range(2):
         a = i * (az - 1)
@@ -652,7 +679,7 @@
         store.wait()
 
 
-def conv_edges(low, high, partial, mid_dec, edge_dec, weight, given):
+def conv_edges(near, far, partial, mid_dec, edge_dec, weight, given):
     plane, channels = partial.shape[1:]
     vmem = pl.BlockSpec(memory_space=pltpu.VMEM)
     hbm = pl.BlockSpec(memory_space=pltpu.HBM)
@@ -662,14 +689,14 @@
         in_specs=[vmem] * 6 + [hbm],
         out_specs=hbm,
         scratch_shapes=[
-            pltpu.VMEM((2 * low.shape[0], 3 * channels), BF16),
+            pltpu.VMEM((2 * near.shape[0], 3 * channels), BF16),
             pltpu.VMEM((2, plane, channels), BF16),
             pltpu.SemaphoreType.DMA((2,)),
         ],
         input_output_aliases={6: 0},
         compiler_params=pltpu.CompilerParams(vmem_limit_bytes=16 * 2**20),
         name="conv_edges",
-    )(low, high, partial, mid_dec, edge_dec, weight, given)
+    )(near, far, partial, mid_dec, edge_dec, weight, given)
 
 
 def exchange(values):
@@ -704,16 +731,16 @@
     rad_low = lax.ppermute(edge1, "blk", outward)
     rad_high = lax.ppermute(edge0, "blk", inward)
     mid_dec, mid = place_mid(vis_count, rows, cells, grid_pos, token, gain)
-    first, last = rim_rows(mid, edge0, edge1, rad_low, rad_high)
-    up = [(i, (i + 1) % n_sector) for i in range(n_sector)]
-    down = [(t, s) for s, t in up]
-    az_low = lax.ppermute(last, "sector", up)
-    az_high = lax.ppermute(first, "sector", down)
+    near, far = rim_rows(mid, edge0, edge1, rad_low, rad_high)
+    pairs = [(i, i + 1) for i in range(0, n_sector, 2)]
+    across = [(i, (i + 1) % n_sector) for i in range(1, n_sector, 2)]
+    near = lax.ppermute(near, "sector", pairs + [(t, s) for s, t in pairs])
+    far = lax.ppermute(far, "sector", across + [(t, s) for s, t in across])
     weight = conv_weight.reshape(9, 3 * channels, channels)
     inner, partial = conv_inner(
         mid, edge0, edge1, rad_low, rad_high, mid_dec, edge_dec, weight, conv_bias.reshape(1, -1)
     )
-    decoded = conv_edges(az_low, az_high, partial, mid_dec, edge_dec, weight, inner)
+    decoded = conv_edges(near, far, partial, mid_dec, edge_dec, weight, inner)
     return decoded.reshape(az, rad, height, channels)
 
 

time: 108 us -> 105 us (0.972)
  starting transfers between devices: 7.22 us -> 3.17 us
    ppermute x2, starting transfers between devices: 5.13 us -> 1.08 us  [the longest x1 0.99 us: body(): far = lax.ppermute(far, 'sector', across + [(t, s) for s, t in across])]
where the time goes in v5:
time: 105 us; the launch traced here: 104 us
  blocking collectives  58.7 us (56%)
  Pallas kernels  37.8 us (36%)
  starting transfers between devices  3.17 us (3%)
  waiting for transfers between devices  3.04 us (3%)
  between operations  1.09 us (1%)
    all_to_all x2, blocking collectives, exchange(): lax.all_to_all(values, ('sector', 'blk'), split_axis=0, concat_axis=0, ti...  58.7 us
    pallas_call x1, Pallas kernels, owner_encode(): pl.pallas_call(owner_kernel, out_shape=jax.ShapeDtypeStruct((owners, MSG,...  13.8 us
    pallas_call x1, Pallas kernels, conv_inner(): pl.pallas_call(conv_kernel, out_shape=(jax.ShapeDtypeStruct((az * plane,...  9.41 us
    pallas_call x1, Pallas kernels, send_rows(): pl.pallas_call(send_kernel, out_shape=(jax.ShapeDtypeStruct((owners, MSG,...  7.09 us
    pallas_call x1, Pallas kernels, place_mid(): pl.pallas_call(mid_kernel, out_shape=(mid, mid), in_specs=[smem] + [vmem]...  3.08 us
    pallas_call x1, Pallas kernels, conv_edges(): pl.pallas_call(conv_edge_kernel, out_shape=jax.ShapeDtypeStruct(given.sha...  2.23 us
    pallas_call x1, Pallas kernels, place_edges(): pl.pallas_call(edge_kernel, out_shape=(jax.ShapeDtypeStruct((entries, cha...  2.19 us
  transfers between devices with their start and end apart: 4, of which 2 were waited for; matrix products, arithmetic and copies ran while one was open for 0% of the time, Pallas kernels for 12%

profile of v5, /device:TPU:0, one launch (start us, length us, event | category | flops | bytes accessed | tf_op | source)
XLA Modules:
  0.0 104.0 jit_solution(12080141177749288506)
XLA Ops:
  0.7 7.1 %send_rows.1 = (bf16[128,40,128]{2,1,0:T(8,128)(2,1)}, s32[1,128]{1,0:T(1,128)}) custom-call(s32[1]{0:T(128)S(6)} %copy.20.count_ref, s32[1,2048]{1,0:T(1,128)} %bitcast.14, s32[1,2048]{1,0:T(1,128)} %bitcast.24, s32[1,2048]{1,0:T(1,128)} %bitcast.25, bf16[2048,256]{1,0:T(8,128)(2,1)} %vis_ref.1, bf16[2560,256]{1,0:T(8,128)(2,1)} %bitcast.11), custom_call_target="tpu_custom_call" | custom-call | tf_op jit(solution)/shard_map/send_rows/pallas_call | solution.py:147
  7.8 0.0 copy-start.2
  7.8 0.0 copy-start.3
  7.8 0.0 copy-start.4
  7.8 0.0 copy-start.5
  7.8 0.0 copy-start.7
  7.8 0.0 copy-start.8
  7.8 0.0 copy-start.9
  7.8 32.9 %all_to_all.10.msg_ref = bf16[128,40,128]{2,1,0:T(8,128)(2,1)S(1)} all-to-all(bf16[128,40,128]{2,1,0:T(8,128)(2,1)} %get-tuple-element.18), channel_id=1, replica_groups=mesh['sector'=32,'blk'=4] {'sector','blk'}, dimensions={0} | all-to-all | bytes 2621440 | tf_op jit(solution)/shard_map/all_to_all | solution.py:703
  40.7 0.0 copy-done.2
  40.7 0.0 copy-done.3
  40.7 0.0 copy-done.4
  40.8 13.8 %owner_encode.1 = bf16[128,40,128]{2,1,0:T(8,128)(2,1)S(1)} custom-call(bf16[128,40,128]{2,1,0:T(8,128)(2,1)S(1)} %all_to_all.10.msg_ref, s32[1,1024]{1,0:T(1,128)S(1)} %copy-done.7, f32[1,256]{1,0:T(1,128)S(1)} %bitcast.17, bf16[256,768]{1,0:T(8,128)(2,1)S(1)} %copy-done.4, bf16[256,256]{1,0:T(8,128)(2,1)S(1)} %copy-done.5, f32[1,256]{1,0:T(1,128)S(1)} %bitcast.18, ...), custom_call_target="tpu_custom_call" | custom-call | tf_op jit(solution)/shard_map/owner_encode/pallas_call | solution.py:373
  54.6 0.0 copy-start
  54.6 0.0 copy-start.6
  54.6 0.0 copy-start.10
  54.6 0.0 copy-start.11
  54.6 25.9 %all_to_all.11.back_ref = bf16[128,40,128]{2,1,0:T(8,128)(2,1)S(1)} all-to-all(bf16[128,40,128]{2,1,0:T(8,128)(2,1)S(1)} %owner_encode.1), channel_id=1, replica_groups=mesh['sector'=32,'blk'=4] {'sector','blk'}, dimensions={0} | all-to-all | bytes 2621440 | tf_op jit(solution)/shard_map/all_to_all | solution.py:703
  80.5 2.2 %place_edges.1 = (bf16[2048,256]{1,0:T(8,128)(2,1)S(1)}, bf16[2,320,256]{2,1,0:T(8,128)(2,1)S(1)}, bf16[320,256]{1,0:T(8,128)(2,1)S(1)}, bf16[320,256]{1,0:T(8,128)(2,1)S(1)}) custom-call(s32[1]{0:T(128)S(6)} %copy.20.count_ref, s32[1,128]{1,0:T(1,128)S(1)} %copy-done.12, bf16[128,40,128]{2,1,0:T(8,128)(2,1)S(1)} %all_to_all.11.back_ref, ...), custom_call_target="tpu_custom_call" | custom-call | flops 600000000 | bytes 4000000 | tf_op jit(solution)/shard_map/place_edges/pallas_call | solution.py:445
  82.7 1.7 %collective-permute-start.1 = (bf16[320,256]{1,0:T(8,128)(2,1)S(1)}, bf16[320,256]{1,0:T(8,128)(2,1)S(1)}, u32[]{:S(2)}, u32[]{:S(2)}) collective-permute-start(bf16[320,256]{1,0:T(8,128)(2,1)S(1)} %get-tuple-element.21.edge0_ref), channel_id=1, source_target_pairs={{1,0},{2,1},{3,2},{0,3},{5,4},{6,5},{7,6},{4,7},{9,8},{10,9},{11,1... | collective-permute-start | bytes 491528 | tf_op jit(solution)/shard_map/ppermute | solution.py:732
  84.4 0.4 collective-permute-start
  84.8 3.1 %place_mid.1 = (bf16[8,240,256]{2,1,0:T(8,128)(2,1)S(1)}, bf16[8,240,256]{2,1,0:T(8,128)(2,1)S(1)}) custom-call(s32[1]{0:T(128)S(6)} %copy.20.count_ref, bf16[2048,256]{1,0:T(8,128)(2,1)S(1)} %get-tuple-element.19.rows_ref, s32[1,2048]{1,0:T(1,128)S(1)} %bitcast.16, bf16[8,8,40,256]{3,2,1,0:T(8,128)(2,1)S(1)} %copy-done, f32[1,256]{1,0:T(1,128)S(1)} %bitcast.20, ...), custom_call_target="tpu_custom_call" | custom-call | flops 2000000000 | bytes 6000000 | tf_op jit(solution)/shard_map/place_mid/pallas_call | solution.py:483
  87.9 0.0 copy-start.13
  87.9 1.2 %collective-permute-done.1.high_ref = bf16[320,256]{1,0:T(8,128)(2,1)S(1)} collective-permute-done((bf16[320,256]{1,0:T(8,128)(2,1)S(1)}, bf16[320,256]{1,0:T(8,128)(2,1)S(1)}, u32[]{:S(2)}, u32[]{:S(2)}) %collective-permute-start.1) | collective-permute-done | bytes 163872 | tf_op jit(solution)/shard_map/ppermute | solution.py:732
  89.2 1.8 %collective-permute-done.low_ref = bf16[320,256]{1,0:T(8,128)(2,1)S(1)} collective-permute-done((bf16[320,256]{1,0:T(8,128)(2,1)S(1)}, bf16[320,256]{1,0:T(8,128)(2,1)S(1)}, u32[]{:S(2)}, u32[]{:S(2)}) %collective-permute-start) | collective-permute-done | bytes 163872 | tf_op jit(solution)/shard_map/ppermute | solution.py:731
  91.0 0.1 collective-permute-start.2
  91.1 1.0 collective-permute-start.3
  92.1 0.0 copy-done.13
  92.1 9.4 %conv_inner.1 = (bf16[2560,256]{1,0:T(8,128)(2,1)}, f32[2,320,256]{2,1,0:T(8,128)S(1)}) custom-call(bf16[8,240,256]{2,1,0:T(8,128)(2,1)S(1)} %get-tuple-element.20.mid_ref, bf16[320,256]{1,0:T(8,128)(2,1)S(1)} %get-tuple-element.21.edge0_ref, bf16[320,256]{1,0:T(8,128)(2,1)S(1)} %get-tuple-element.22.edge1_ref, ...), custom_call_target="tpu_custom_call" | custom-call | flops 8000000000 | bytes 10000000 | tf_op jit(solution)/shard_map/conv_inner/pallas_call | solution.py:623
  101.5 0.0 collective-permute-done.2.near_ref
  101.5 0.0 collective-permute-done.3.far_ref
  101.5 2.2 %conv_edges.1 = bf16[2560,256]{1,0:T(8,128)(2,1)} custom-call(bf16[400,256]{1,0:T(8,128)(2,1)S(1)} %collective-permute-done.2.near_ref, bf16[400,256]{1,0:T(8,128)(2,1)S(1)} %collective-permute-done.3.far_ref, f32[2,320,256]{2,1,0:T(8,128)S(1)} %get-tuple-element.27.partial_ref, ...), custom_call_target="tpu_custom_call", output_to_operand_aliasing={{}: (6, {})} | custom-call | tf_op jit(solution)/shard_map/conv_edges/pallas_call | solution.py:686
  (13 shorter events, 0.1 us)
Async XLA Ops:
  7.8 33.0 %copy-start.2 = (bf16[256,1024]{1,0:T(8,128)(2,1)S(1)}, bf16[256,1024]{1,0:T(8,128)(2,1)}, u32[]{:S(2)}) copy-start(bf16[256,1024]{1,0:T(8,128)(2,1)} %mlp_in_ref.1) | copy-start | bytes 1572868
  7.8 33.0 %copy-start.3 = (bf16[1024,256]{1,0:T(8,128)(2,1)S(1)}, bf16[1024,256]{1,0:T(8,128)(2,1)}, u32[]{:S(2)}) copy-start(bf16[1024,256]{1,0:T(8,128)(2,1)} %mlp_out_ref.1) | copy-start | bytes 1572868
  7.8 33.0 %copy-start.4 = (bf16[256,768]{1,0:T(8,128)(2,1)S(1)}, bf16[256,768]{1,0:T(8,128)(2,1)}, u32[]{:S(2)}) copy-start(bf16[256,768]{1,0:T(8,128)(2,1)} %attn_in_ref.1) | copy-start | bytes 1179652
  7.8 33.0 %copy-start.5 = (bf16[256,256]{1,0:T(8,128)(2,1)S(1)}, bf16[256,256]{1,0:T(8,128)(2,1)}, u32[]{:S(2)}) copy-start(bf16[256,256]{1,0:T(8,128)(2,1)} %attn_out_ref.1) | copy-start | bytes 393220
  7.8 32.9 %copy-start.7 = (s32[1,1024]{1,0:T(1,128)S(1)}, s32[1,1024]{1,0:T(1,128)}, u32[]{:S(2)}) copy-start(s32[1,1024]{1,0:T(1,128)} %window_ref.1) | copy-start | bytes 12292
  7.8 32.9 %copy-start.8 = (f32[256]{0:T(256)S(1)}, f32[256]{0:T(256)}, u32[]{:S(2)}) copy-start(f32[256]{0:T(256)} %param.24) | copy-start | bytes 3076
  7.8 32.9 %copy-start.9 = (f32[256]{0:T(256)S(1)}, f32[256]{0:T(256)}, u32[]{:S(2)}) copy-start(f32[256]{0:T(256)} %param.27) | copy-start | bytes 3076
  54.6 25.9 %copy-start = (bf16[8,8,40,256]{3,2,1,0:T(8,128)(2,1)S(1)}, bf16[8,8,40,256]{3,2,1,0:T(8,128)(2,1)}, u32[]{:S(2)}) copy-start(bf16[8,8,40,256]{3,2,1,0:T(8,128)(2,1)} %pos_ref.3) | copy-start | bytes 3932164
  54.6 25.9 %copy-start.6 = (s32[2048]{0:T(1024)S(1)}, s32[2048]{0:T(1024)}, u32[]{:S(2)}) copy-start(s32[2048]{0:T(1024)} %param.19) | copy-start | bytes 24580
  54.6 25.9 %copy-start.10 = (f32[256]{0:T(256)S(1)}, f32[256]{0:T(256)}, u32[]{:S(2)}) copy-start(f32[256]{0:T(256)} %param.30) | copy-start | bytes 3076
  54.6 25.9 %copy-start.11 = (f32[256]{0:T(256)S(1)}, f32[256]{0:T(256)}, u32[]{:S(2)}) copy-start(f32[256]{0:T(256)} %param.31) | copy-start | bytes 3076
  54.6 25.9 %copy-start.12 = (s32[1,128]{1,0:T(1,128)S(1)}, s32[1,128]{1,0:T(1,128)}, u32[]{:S(2)}) copy-start(s32[1,128]{1,0:T(1,128)} %get-tuple-element.17.starts_ref) | copy-start | bytes 1540
  82.7 6.4 %collective-permute-start.1 = (bf16[320,256]{1,0:T(8,128)(2,1)S(1)}, bf16[320,256]{1,0:T(8,128)(2,1)S(1)}, u32[]{:S(2)}, u32[]{:S(2)}) collective-permute-start(bf16[320,256]{1,0:T(8,128)(2,1)S(1)} %get-tuple-element.21.edge0_ref), channel_id=1, source_target_pairs={{1,0},{2,1},{3,2},{0,3},{5,4},{6,5},{7,6},{4,7},{9,8},{10,9},{11,1... | collective-permute-start | bytes 491528 | tf_op jit(solution)/shard_map/ppermute | solution.py:732
  84.4 6.6 %collective-permute-start = (bf16[320,256]{1,0:T(8,128)(2,1)S(1)}, bf16[320,256]{1,0:T(8,128)(2,1)S(1)}, u32[]{:S(2)}, u32[]{:S(2)}) collective-permute-start(bf16[320,256]{1,0:T(8,128)(2,1)S(1)} %get-tuple-element.22.edge1_ref), channel_id=1, source_target_pairs={{0,1},{1,2},{2,3},{3,0},{4,5},{5,6},{6,7},{7,4},{8,9},{9,10},{10,1... | collective-permute-start | bytes 491528 | tf_op jit(solution)/shard_map/ppermute | solution.py:731
  84.8 7.3 %copy-start.1 = (bf16[27,256,256]{2,1,0:T(8,128)(2,1)S(1)}, bf16[27,256,256]{2,1,0:T(8,128)(2,1)}, u32[]{:S(2)}) copy-start(bf16[27,256,256]{2,1,0:T(8,128)(2,1)} %param.32) | copy-start | bytes 10616836
  87.9 4.2 %copy-start.13 = (f32[256]{0:T(256)S(1)}, f32[256]{0:T(256)}, u32[]{:S(2)}) copy-start(f32[256]{0:T(256)} %param.33) | copy-start | bytes 3076
  91.0 10.5 %collective-permute-start.2 = (bf16[400,256]{1,0:T(8,128)(2,1)S(1)}, bf16[400,256]{1,0:T(8,128)(2,1)S(1)}, u32[]{:S(2)}, u32[]{:S(2)}) collective-permute-start(bf16[400,256]{1,0:T(8,128)(2,1)S(1)} %get-tuple-element.23), channel_id=1, source_target_pairs={{0,4},{8,12},{16,20},{24,28},{32,36},{40,44},{48,52},{56,60},{64,6... | collective-permute-start | bytes 614408 | tf_op jit(solution)/shard_map/ppermute | solution.py:737
  91.1 10.4 %collective-permute-start.3 = (bf16[400,256]{1,0:T(8,128)(2,1)S(1)}, bf16[400,256]{1,0:T(8,128)(2,1)S(1)}, u32[]{:S(2)}, u32[]{:S(2)}) collective-permute-start(bf16[400,256]{1,0:T(8,128)(2,1)S(1)} %get-tuple-element.24), channel_id=1, source_target_pairs={{4,8},{12,16},{20,24},{28,32},{36,40},{44,48},{52,56},{60,64},{68,... | collective-permute-start | bytes 614408 | tf_op jit(solution)/shard_map/ppermute | solution.py:738

commit v6 on v5

--- a/solution.py
+++ b/solution.py
@@ -12,6 +12,7 @@
 I16 = jnp.int16
 I32 = jnp.int32
 CAP = 18
+PLANES_FIRST = 2
 MSG = 40
 
 
@@ -500,7 +501,7 @@
     return lax.bitwise_and(lax.axis_index("sector"), 1) == 0
 
 
-def rim_kernel(mid_ref, edge0_ref, edge1_ref, low_ref, high_ref, near_ref, far_ref):
+def rim_kernel(mid_ref, edge0_ref, edge1_ref, low_ref, high_ref, after_ref, near_ref, far_ref):
     az, size, channels = mid_ref.shape
     height = low_ref.shape[0] // az
     inside, outside = ring_ends()
@@ -526,18 +527,18 @@
         fill(far_ref, az - 1)
 
 
-def rim_rows(mid, edge0, edge1, low, high):
+def rim_rows(mid, edge0, edge1, low, high, after):
     az, size, channels = mid.shape
     vmem = pl.BlockSpec(memory_space=pltpu.VMEM)
     out = jax.ShapeDtypeStruct((size + 4 * (low.shape[0] // az), channels), BF16)
     return pl.pallas_call(
         rim_kernel,
         out_shape=(out, out),
-        in_specs=[vmem] * 5,
+        in_specs=[vmem] * 5 + [pl.BlockSpec(memory_space=pl.ANY)],
         out_specs=(vmem, vmem),
         compiler_params=pltpu.CompilerParams(vmem_limit_bytes=8 * 2**20),
         name="rim_rows",
-    )(mid, edge0, edge1, low, high)
+    )(mid, edge0, edge1, low, high, after)
 
 
 def widen(scr, at, rows, height, drop=None):
@@ -554,8 +555,58 @@
     scr[at : at + n, 2 * channels :] = above.astype(BF16)
 
 
+def first_kernel(
+    mid_ref, edge0_ref, edge1_ref, mid_dec_ref, weight_ref, bias_ref,
+    out_ref,
+    wide_scr,
+):
+    planes, size, channels = out_ref.shape
+    height = edge0_ref.shape[0] // mid_ref.shape[0]
+    pitch = size + 2 * height
+
+    def spread(a):
+        base = a * pitch
+        part = slice(a * height, (a + 1) * height)
+        widen(wide_scr, base, edge0_ref[part], height)
+        widen(wide_scr, base + height, mid_ref[a], height)
+        widen(wide_scr, base + height + size, edge1_ref[part], height)
+
+    def taps(a):
+        total = jnp.broadcast_to(bias_ref[...], (size, channels))
+        for da in range(3):
+            for dr in range(3):
+                at = (a + da - 1) * pitch + dr * height
+                total = total + dot(wide_scr[at : at + size, :], weight_ref[da * 3 + dr])
+        return total
+
+    for a in range(3):
+        spread(a)
+    for a in range(1, planes + 1):
+        total = taps(a)
+        if a < planes:
+            spread(a + 2)
+        out_ref[a - 1] = (mid_dec_ref[a].astype(F32) + gelu(total)).astype(BF16)
+
+
+def conv_first(planes, mid, edge0, edge1, mid_dec, weight, bias):
+    az, size, channels = mid.shape
+    pitch = size + 2 * (edge0.shape[0] // az)
+    vmem = pl.BlockSpec(memory_space=pltpu.VMEM)
+    return pl.pallas_call(
+        first_kernel,
+        out_shape=jax.ShapeDtypeStruct((planes, size, channels), BF16),
+        in_specs=[vmem] * 6,
+        out_specs=vmem,
+        scratch_shapes=[pltpu.VMEM(((planes + 2) * pitch, 3 * channels), BF16)],
+        compiler_params=pltpu.CompilerParams(vmem_limit_bytes=24 * 2**20),
+        cost_estimate=pl.CostEstimate(flops=25 * 10**8, bytes_accessed=10**7, transcendentals=0),
+        name="conv_first",
+    )(mid, edge0, edge1, mid_dec, weight, bias)
+
+
 def conv_kernel(
     mid_ref, edge0_ref, edge1_ref, low_ref, high_ref, mid_dec_ref, edge_dec_ref, weight_ref, bias_ref,
+    first_ref,
     out_ref, partial_ref,
     wide_scr, done_scr, out_sems,
 ):
@@ -584,37 +635,70 @@
                 total = total + dot(wide_scr[at : at + plane, :], weight_ref[da * 3 + dr])
         return total
 
-    def finish(a, total):
-        if a in (0, az - 1):
-            partial_ref[a // (az - 1)] = total
-            return
-        part = slice(a * height, (a + 1) * height)
-        dec = jnp.concatenate([edge_dec_ref[0, part], mid_dec_ref[a], edge_dec_ref[1, part]], axis=0)
-        done_scr[a - 1] = (dec.astype(F32) + gelu(total)).astype(BF16)
-
-    spread(0)
-    spread(1)
-    spread(2)
+    def side_taps():
+        total = jnp.broadcast_to(bias_ref[...], (2 * planes * height, channels))
+        for da in range(3):
+            for dr in range(3):
+                at = [
+                    (a + da - 1) * pitch + (r + dr) * height
+                    for a in range(1, planes + 1)
+                    for r in (0, size // height + 1)
+                ]
+                rows = jnp.concatenate([wide_scr[i : i + height, :] for i in at], axis=0)
+                total = total + dot(rows, weight_ref[da * 3 + dr])
+        return total
+
+    def finish(unit, total):
+        if unit == "sides":
+            done = []
+            for a in range(1, planes + 1):
+                part = slice(a * height, (a + 1) * height)
+                for side, to in ((0, 0), (1, height + size)):
+                    at = (2 * (a - 1) + side) * height
+                    value = edge_dec_ref[side, part].astype(F32) + gelu(total[at : at + height])
+                    done_scr[a - 1, to : to + height] = value.astype(BF16)
+                done_scr[a - 1, height : height + size] = first_ref[a - 1]
+                done.append(a)
+            return done
+        if unit in (0, az - 1):
+            partial_ref[unit // (az - 1)] = total
+            return []
+        part = slice(unit * height, (unit + 1) * height)
+        dec = jnp.concatenate(
+            [edge_dec_ref[0, part], mid_dec_ref[unit], edge_dec_ref[1, part]], axis=0
+        )
+        done_scr[unit - 1] = (dec.astype(F32) + gelu(total)).astype(BF16)
+        return [unit]
+
+    planes = first_ref.shape[0]
+    units = [(0, 1), ("sides", planes + 1)] + [(a, a + 1) for a in range(planes + 1, az)]
+    ready = 0
     stores = []
-    held = taps(0)
-    for a in range(1, az + 1):
-        if a < az:
-            total = taps(a)
-        if a + 2 < az:
-            spread(a + 2)
-        finish(a - 1, held)
-        held = total
-        if 0 < a - 1 < az - 1:
-            store = pltpu.make_async_copy(
-                done_scr.at[a - 2], out_ref.at[pl.ds((a - 1) * plane, plane)], out_sems.at[a - 2]
-            )
-            stores.append(store)
-            store.start()
+    held = None
+    for i, (unit, need) in enumerate(units):
+        ahead = units[i + 1][1] if i + 1 < len(units) else az
+        if held is None:
+            while ready < need + 1:
+                spread(ready)
+                ready += 1
+        total = side_taps() if unit == "sides" else taps(unit)
+        while ready < min(ahead + 1, az):
+            spread(ready)
+            ready += 1
+        if held is not None:
+            for a in finish(*held):
+                store = pltpu.make_async_copy(
+                    done_scr.at[a - 1], out_ref.at[pl.ds(a * plane, plane)], out_sems.at[a - 1]
+                )
+                store.start()
+                stores.append(store)
+        held = (unit, total)
+    finish(*held)
     for store in stores:
         store.wait()
 
 
-def conv_inner(mid, edge0, edge1, low, high, mid_dec, edge_dec, weight, bias):
+def conv_inner(mid, edge0, edge1, low, high, mid_dec, edge_dec, weight, bias, first):
     az, size, channels = mid.shape
     height = low.shape[0] // az
     plane = size + 2 * height
@@ -626,7 +710,7 @@
             jax.ShapeDtypeStruct((az * plane, channels), BF16),
             jax.ShapeDtypeStruct((2, plane, channels), F32),
         ),
-        in_specs=[vmem] * 9,
+        in_specs=[vmem] * 10,
         out_specs=(hbm, vmem),
         scratch_shapes=[
             pltpu.VMEM((az * (plane + 2 * height), 3 * channels), BF16),
@@ -634,9 +718,9 @@
             pltpu.SemaphoreType.DMA((az - 2,)),
         ],
         compiler_params=pltpu.CompilerParams(vmem_limit_bytes=32 * 2**20),
-        cost_estimate=pl.CostEstimate(flops=8 * 10**9, bytes_accessed=10**7, transcendentals=0),
+        cost_estimate=pl.CostEstimate(flops=6 * 10**9, bytes_accessed=10**7, transcendentals=0),
         name="conv_inner",
-    )(mid, edge0, edge1, low, high, mid_dec, edge_dec, weight, bias)
+    )(mid, edge0, edge1, low, high, mid_dec, edge_dec, weight, bias, first)
 
 
 def conv_edge_kernel(
@@ -731,14 +815,16 @@
     rad_low = lax.ppermute(edge1, "blk", outward)
     rad_high = lax.ppermute(edge0, "blk", inward)
     mid_dec, mid = place_mid(vis_count, rows, cells, grid_pos, token, gain)
-    near, far = rim_rows(mid, edge0, edge1, rad_low, rad_high)
+    weight = conv_weight.reshape(9, 3 * channels, channels)
+    bias = conv_bias.reshape(1, -1)
+    first = conv_first(PLANES_FIRST, mid, edge0, edge1, mid_dec, weight, bias)
+    near, far = rim_rows(mid, edge0, edge1, rad_low, rad_high, first)
     pairs = [(i, i + 1) for i in range(0, n_sector, 2)]
     across = [(i, (i + 1) % n_sector) for i in range(1, n_sector, 2)]
     near = lax.ppermute(near, "sector", pairs + [(t, s) for s, t in pairs])
     far = lax.ppermute(far, "sector", across + [(t, s) for s, t in across])
-    weight = conv_weight.reshape(9, 3 * channels, channels)
     inner, partial = conv_inner(
-        mid, edge0, edge1, rad_low, rad_high, mid_dec, edge_dec, weight, conv_bias.reshape(1, -1)
+        mid, edge0, edge1, rad_low, rad_high, mid_dec, edge_dec, weight, bias, first
     )
     decoded = conv_edges(near, far, partial, mid_dec, edge_dec, weight, inner)
     return decoded.reshape(az, rad, height, channels)

time: 105 us -> 104 us (level)
  waiting for transfers between devices: 3.04 us -> 0.93 us
    pallas_call x1 -> x2, Pallas kernels: 0.03 us -> 2.12 us  [the longest x1 2.09 us: conv_first(): pl.pallas_call(first_kernel, out_shape=jax.ShapeDtypeStruct((planes, size...]
    pallas_call x1, Pallas kernels: 9.41 us -> 7.92 us  [conv_inner(): pl.pallas_call(conv_kernel, out_shape=(jax.ShapeDtypeStruct((az * plane,...]
    ppermute x1, waiting for transfers between devices: 1.25 us -> 0.01 us  [body(): rad_high = lax.ppermute(edge0, 'blk', inward)]
  transfers between devices with their start and end apart: 4 -> 4, of which waited for: 2 -> 1; matrix products, arithmetic and copies ran while one was open for 0% -> 0% of each run, Pallas kernels for 12% -> 13%
where the time goes in v6:
time: 104 us; the launch traced here: 102 us
  blocking collectives  58.7 us (56%)
  Pallas kernels  38.4 us (37%)
  starting transfers between devices  3.17 us (3%)
  between operations  1.11 us (1%)
    all_to_all x2, blocking collectives, exchange(): lax.all_to_all(values, ('sector', 'blk'), split_axis=0, concat_axis=0, ti...  58.7 us
    pallas_call x1, Pallas kernels, owner_encode(): pl.pallas_call(owner_kernel, out_shape=jax.ShapeDtypeStruct((owners, MSG,...  13.8 us
    pallas_call x1, Pallas kernels, conv_inner(): pl.pallas_call(conv_kernel, out_shape=(jax.ShapeDtypeStruct((az * plane,...  7.92 us
    pallas_call x1, Pallas kernels, send_rows(): pl.pallas_call(send_kernel, out_shape=(jax.ShapeDtypeStruct((owners, MSG,...  7.09 us
    pallas_call x1, Pallas kernels, place_mid(): pl.pallas_call(mid_kernel, out_shape=(mid, mid), in_specs=[smem] + [vmem]...  3.09 us
    pallas_call x1, Pallas kernels, conv_edges(): pl.pallas_call(conv_edge_kernel, out_shape=jax.ShapeDtypeStruct(given.sha...  2.24 us
    pallas_call x1, Pallas kernels, place_edges(): pl.pallas_call(edge_kernel, out_shape=(jax.ShapeDtypeStruct((entries, cha...  2.19 us
    pallas_call x1, Pallas kernels, conv_first(): pl.pallas_call(first_kernel, out_shape=jax.ShapeDtypeStruct((planes, size...  2.09 us
  transfers between devices with their start and end apart: 4, of which 1 were waited for; matrix products, arithmetic and copies ran while one was open for 0% of the time, Pallas kernels for 13%

profile of v6, /device:TPU:0, one launch (start us, length us, event | category | flops | bytes accessed | tf_op | source)
XLA Modules:
  0.0 102.5 jit_solution(17752055926250885654)
XLA Ops:
  0.7 7.1 %send_rows.1 = (bf16[128,40,128]{2,1,0:T(8,128)(2,1)}, s32[1,128]{1,0:T(1,128)}) custom-call(s32[1]{0:T(128)S(6)} %copy.20.count_ref, s32[1,2048]{1,0:T(1,128)} %bitcast.15, s32[1,2048]{1,0:T(1,128)} %bitcast.26, s32[1,2048]{1,0:T(1,128)} %bitcast.27, bf16[2048,256]{1,0:T(8,128)(2,1)} %vis_ref.1, bf16[2560,256]{1,0:T(8,128)(2,1)} %bitcast.11), custom_call_target="tpu_custom_call" | custom-call | tf_op jit(solution)/shard_map/send_rows/pallas_call | solution.py:148
  7.8 0.0 copy-start.2
  7.8 0.0 copy-start.3
  7.8 0.0 copy-start.4
  7.8 0.0 copy-start.5
  7.8 0.0 copy-start.7
  7.8 0.0 copy-start.8
  7.8 0.0 copy-start.9
  7.8 32.9 %all_to_all.10.msg_ref = bf16[128,40,128]{2,1,0:T(8,128)(2,1)S(1)} all-to-all(bf16[128,40,128]{2,1,0:T(8,128)(2,1)} %get-tuple-element.18), channel_id=1, replica_groups=mesh['sector'=32,'blk'=4] {'sector','blk'}, dimensions={0} | all-to-all | bytes 2621440 | tf_op jit(solution)/shard_map/all_to_all | solution.py:787
  40.7 0.0 copy-done.5
  40.7 0.0 copy-done.7
  40.8 0.0 copy-done.8
  40.8 0.0 copy-done.9
  40.8 13.8 %owner_encode.1 = bf16[128,40,128]{2,1,0:T(8,128)(2,1)S(1)} custom-call(bf16[128,40,128]{2,1,0:T(8,128)(2,1)S(1)} %all_to_all.10.msg_ref, s32[1,1024]{1,0:T(1,128)S(1)} %copy-done.7, f32[1,256]{1,0:T(1,128)S(1)} %bitcast.18, bf16[256,768]{1,0:T(8,128)(2,1)S(1)} %copy-done.4, bf16[256,256]{1,0:T(8,128)(2,1)S(1)} %copy-done.5, f32[1,256]{1,0:T(1,128)S(1)} %bitcast.19, ...), custom_call_target="tpu_custom_call" | custom-call | tf_op jit(solution)/shard_map/owner_encode/pallas_call | solution.py:374
  54.6 0.0 copy-start
  54.6 0.0 copy-start.6
  54.6 0.0 copy-start.10
  54.6 0.0 copy-start.11
  54.6 25.9 %all_to_all.11.back_ref = bf16[128,40,128]{2,1,0:T(8,128)(2,1)S(1)} all-to-all(bf16[128,40,128]{2,1,0:T(8,128)(2,1)S(1)} %owner_encode.1), channel_id=1, replica_groups=mesh['sector'=32,'blk'=4] {'sector','blk'}, dimensions={0} | all-to-all | bytes 2621440 | tf_op jit(solution)/shard_map/all_to_all | solution.py:787
  80.5 2.2 %place_edges.1 = (bf16[2048,256]{1,0:T(8,128)(2,1)S(1)}, bf16[2,320,256]{2,1,0:T(8,128)(2,1)S(1)}, bf16[320,256]{1,0:T(8,128)(2,1)S(1)}, bf16[320,256]{1,0:T(8,128)(2,1)S(1)}) custom-call(s32[1]{0:T(128)S(6)} %copy.20.count_ref, s32[1,128]{1,0:T(1,128)S(1)} %copy-done.12, bf16[128,40,128]{2,1,0:T(8,128)(2,1)S(1)} %all_to_all.11.back_ref, ...), custom_call_target="tpu_custom_call" | custom-call | flops 600000000 | bytes 4000000 | tf_op jit(solution)/shard_map/place_edges/pallas_call | solution.py:446
  82.7 1.7 %collective-permute-start.1 = (bf16[320,256]{1,0:T(8,128)(2,1)S(1)}, bf16[320,256]{1,0:T(8,128)(2,1)S(1)}, u32[]{:S(2)}, u32[]{:S(2)}) collective-permute-start(bf16[320,256]{1,0:T(8,128)(2,1)S(1)} %get-tuple-element.21.edge0_ref), channel_id=1, source_target_pairs={{1,0},{2,1},{3,2},{0,3},{5,4},{6,5},{7,6},{4,7},{9,8},{10,9},{11,1... | collective-permute-start | bytes 491528 | tf_op jit(solution)/shard_map/ppermute | solution.py:816
  84.4 0.4 collective-permute-start
  84.8 3.1 %place_mid.1 = (bf16[8,240,256]{2,1,0:T(8,128)(2,1)S(1)}, bf16[8,240,256]{2,1,0:T(8,128)(2,1)S(1)}) custom-call(s32[1]{0:T(128)S(6)} %copy.20.count_ref, bf16[2048,256]{1,0:T(8,128)(2,1)S(1)} %get-tuple-element.19.rows_ref, s32[1,2048]{1,0:T(1,128)S(1)} %bitcast.17, bf16[8,8,40,256]{3,2,1,0:T(8,128)(2,1)S(1)} %copy-done, f32[1,256]{1,0:T(1,128)S(1)} %bitcast.21, ...), custom_call_target="tpu_custom_call" | custom-call | flops 2000000000 | bytes 6000000 | tf_op jit(solution)/shard_map/place_mid/pallas_call | solution.py:484
  87.9 2.1 %conv_first.1.after_ref.first_ref = bf16[2,240,256]{2,1,0:T(8,128)(2,1)S(1)} custom-call(bf16[8,240,256]{2,1,0:T(8,128)(2,1)S(1)} %get-tuple-element.20.mid_ref, bf16[320,256]{1,0:T(8,128)(2,1)S(1)} %get-tuple-element.21.edge0_ref, bf16[320,256]{1,0:T(8,128)(2,1)S(1)} %get-tuple-element.22.edge1_ref, bf16[8,240,256]{2,1,0:T(8,128)(2,1)S(1)} %get-tuple-element.23.mid_dec_ref, ...), custom_call_target="tpu_custom_call" | custom-call | flops 2500000000 | bytes 10000000 | tf_op jit(solution)/shard_map/conv_first/pallas_call | solution.py:595
  90.0 0.0 collective-permute-done.1.high_ref
  90.0 0.9 collective-permute-done.low_ref
  91.0 0.1 collective-permute-start.2
  91.1 1.0 collective-permute-start.3
  92.1 7.9 %conv_inner.1 = (bf16[2560,256]{1,0:T(8,128)(2,1)}, f32[2,320,256]{2,1,0:T(8,128)S(1)}) custom-call(bf16[8,240,256]{2,1,0:T(8,128)(2,1)S(1)} %get-tuple-element.20.mid_ref, bf16[320,256]{1,0:T(8,128)(2,1)S(1)} %get-tuple-element.21.edge0_ref, bf16[320,256]{1,0:T(8,128)(2,1)S(1)} %get-tuple-element.22.edge1_ref, ...), custom_call_target="tpu_custom_call" | custom-call | flops 6000000000 | bytes 10000000 | tf_op jit(solution)/shard_map/conv_inner/pallas_call | solution.py:707
  100.0 0.0 collective-permute-done.2.near_ref
  100.0 0.0 collective-permute-done.3.far_ref
  100.0 2.2 %conv_edges.1 = bf16[2560,256]{1,0:T(8,128)(2,1)} custom-call(bf16[400,256]{1,0:T(8,128)(2,1)S(1)} %collective-permute-done.2.near_ref, bf16[400,256]{1,0:T(8,128)(2,1)S(1)} %collective-permute-done.3.far_ref, f32[2,320,256]{2,1,0:T(8,128)S(1)} %get-tuple-element.27.partial_ref, ...), custom_call_target="tpu_custom_call", output_to_operand_aliasing={{}: (6, {})} | custom-call | tf_op jit(solution)/shard_map/conv_edges/pallas_call | solution.py:770
  (14 shorter events, 0.1 us)
Async XLA Ops:
  7.8 33.0 %copy-start.2 = (bf16[256,1024]{1,0:T(8,128)(2,1)S(1)}, bf16[256,1024]{1,0:T(8,128)(2,1)}, u32[]{:S(2)}) copy-start(bf16[256,1024]{1,0:T(8,128)(2,1)} %mlp_in_ref.1) | copy-start | bytes 1572868
  7.8 33.0 %copy-start.3 = (bf16[1024,256]{1,0:T(8,128)(2,1)S(1)}, bf16[1024,256]{1,0:T(8,128)(2,1)}, u32[]{:S(2)}) copy-start(bf16[1024,256]{1,0:T(8,128)(2,1)} %mlp_out_ref.1) | copy-start | bytes 1572868
  7.8 33.0 %copy-start.4 = (bf16[256,768]{1,0:T(8,128)(2,1)S(1)}, bf16[256,768]{1,0:T(8,128)(2,1)}, u32[]{:S(2)}) copy-start(bf16[256,768]{1,0:T(8,128)(2,1)} %attn_in_ref.1) | copy-start | bytes 1179652
  7.8 33.0 %copy-start.5 = (bf16[256,256]{1,0:T(8,128)(2,1)S(1)}, bf16[256,256]{1,0:T(8,128)(2,1)}, u32[]{:S(2)}) copy-start(bf16[256,256]{1,0:T(8,128)(2,1)} %attn_out_ref.1) | copy-start | bytes 393220
  7.8 32.9 %copy-start.7 = (s32[1,1024]{1,0:T(1,128)S(1)}, s32[1,1024]{1,0:T(1,128)}, u32[]{:S(2)}) copy-start(s32[1,1024]{1,0:T(1,128)} %window_ref.1) | copy-start | bytes 12292
  7.8 32.9 %copy-start.8 = (f32[256]{0:T(256)S(1)}, f32[256]{0:T(256)}, u32[]{:S(2)}) copy-start(f32[256]{0:T(256)} %param.24) | copy-start | bytes 3076
  7.8 32.9 %copy-start.9 = (f32[256]{0:T(256)S(1)}, f32[256]{0:T(256)}, u32[]{:S(2)}) copy-start(f32[256]{0:T(256)} %param.27) | copy-start | bytes 3076
  54.6 25.9 %copy-start = (bf16[8,8,40,256]{3,2,1,0:T(8,128)(2,1)S(1)}, bf16[8,8,40,256]{3,2,1,0:T(8,128)(2,1)}, u32[]{:S(2)}) copy-start(bf16[8,8,40,256]{3,2,1,0:T(8,128)(2,1)} %pos_ref.3) | copy-start | bytes 3932164
  54.6 25.9 %copy-start.6 = (s32[2048]{0:T(1024)S(1)}, s32[2048]{0:T(1024)}, u32[]{:S(2)}) copy-start(s32[2048]{0:T(1024)} %param.19) | copy-start | bytes 24580
  54.6 25.9 %copy-start.10 = (f32[256]{0:T(256)S(1)}, f32[256]{0:T(256)}, u32[]{:S(2)}) copy-start(f32[256]{0:T(256)} %param.30) | copy-start | bytes 3076
  54.6 25.9 %copy-start.11 = (f32[256]{0:T(256)S(1)}, f32[256]{0:T(256)}, u32[]{:S(2)}) copy-start(f32[256]{0:T(256)} %param.31) | copy-start | bytes 3076
  54.6 25.9 %copy-start.12 = (s32[1,128]{1,0:T(1,128)S(1)}, s32[1,128]{1,0:T(1,128)}, u32[]{:S(2)}) copy-start(s32[1,128]{1,0:T(1,128)} %get-tuple-element.17.starts_ref) | copy-start | bytes 1540
  82.7 7.3 %collective-permute-start.1 = (bf16[320,256]{1,0:T(8,128)(2,1)S(1)}, bf16[320,256]{1,0:T(8,128)(2,1)S(1)}, u32[]{:S(2)}, u32[]{:S(2)}) collective-permute-start(bf16[320,256]{1,0:T(8,128)(2,1)S(1)} %get-tuple-element.21.edge0_ref), channel_id=1, source_target_pairs={{1,0},{2,1},{3,2},{0,3},{5,4},{6,5},{7,6},{4,7},{9,8},{10,9},{11,1... | collective-permute-start | bytes 491528 | tf_op jit(solution)/shard_map/ppermute | solution.py:816
  84.4 6.6 %collective-permute-start = (bf16[320,256]{1,0:T(8,128)(2,1)S(1)}, bf16[320,256]{1,0:T(8,128)(2,1)S(1)}, u32[]{:S(2)}, u32[]{:S(2)}) collective-permute-start(bf16[320,256]{1,0:T(8,128)(2,1)S(1)} %get-tuple-element.22.edge1_ref), channel_id=1, source_target_pairs={{0,1},{1,2},{2,3},{3,0},{4,5},{5,6},{6,7},{7,4},{8,9},{9,10},{10,1... | collective-permute-start | bytes 491528 | tf_op jit(solution)/shard_map/ppermute | solution.py:815
  84.8 3.1 %copy-start.1 = (bf16[27,256,256]{2,1,0:T(8,128)(2,1)S(1)}, bf16[27,256,256]{2,1,0:T(8,128)(2,1)}, u32[]{:S(2)}) copy-start(bf16[27,256,256]{2,1,0:T(8,128)(2,1)} %param.32) | copy-start | bytes 10616836
  84.8 3.1 %copy-start.13 = (f32[256]{0:T(256)S(1)}, f32[256]{0:T(256)}, u32[]{:S(2)}) copy-start(f32[256]{0:T(256)} %param.33) | copy-start | bytes 3076
  91.0 9.0 %collective-permute-start.2 = (bf16[400,256]{1,0:T(8,128)(2,1)S(1)}, bf16[400,256]{1,0:T(8,128)(2,1)S(1)}, u32[]{:S(2)}, u32[]{:S(2)}) collective-permute-start(bf16[400,256]{1,0:T(8,128)(2,1)S(1)} %get-tuple-element.24), channel_id=1, source_target_pairs={{0,4},{8,12},{16,20},{24,28},{32,36},{40,44},{48,52},{56,60},{64,6... | collective-permute-start | bytes 614408 | tf_op jit(solution)/shard_map/ppermute | solution.py:824
  91.1 8.9 %collective-permute-start.3 = (bf16[400,256]{1,0:T(8,128)(2,1)S(1)}, bf16[400,256]{1,0:T(8,128)(2,1)S(1)}, u32[]{:S(2)}, u32[]{:S(2)}) collective-permute-start(bf16[400,256]{1,0:T(8,128)(2,1)S(1)} %get-tuple-element.25), channel_id=1, source_target_pairs={{4,8},{12,16},{20,24},{28,32},{36,40},{44,48},{52,56},{60,64},{68,... | collective-permute-start | bytes 614408 | tf_op jit(solution)/shard_map/ppermute | solution.py:825

commit v7 on v6

--- a/solution.py
+++ b/solution.py
@@ -12,7 +12,7 @@
 I16 = jnp.int16
 I32 = jnp.int32
 CAP = 18
-PLANES_FIRST = 2
+PLANES_FIRST = 3
 MSG = 40
 
 
@@ -391,13 +391,14 @@
     )(msg, window, gain1, attn_in, attn_out, gain2, mlp_in, mlp_out)
 
 
-def fill_cells(ids, cells, rows, token, pos, gain):
+def cell_hits(ids, cells):
     hit = match(ids, cells)
-    filled = dot(hit, rows)
     seen = sum([hit[:, i : i + 128] for i in range(0, hit.shape[1], 128)])
-    seen = jnp.sum(seen.astype(F32), axis=1, keepdims=True)
-    filled = jnp.where(seen > 0.5, filled, token)
-    dec = (filled + pos.astype(F32)).astype(BF16)
+    return hit, jnp.sum(seen.astype(F32), axis=1, keepdims=True) > 0.5
+
+
+def norm_cells(filled, seen, token, pos, gain):
+    dec = (jnp.where(seen, filled, token) + pos.astype(F32)).astype(BF16)
     return dec, layer_norm(dec.astype(F32), gain).astype(BF16)
 
 
@@ -430,7 +431,8 @@
         [iota((height, 1), 0) + (a * rad + r) * height for a, r in at], axis=0
     )
     pos = jnp.concatenate([pos_ref[a, r].astype(F32) for a, r in at], axis=0)
-    dec, normed = fill_cells(ids, cells, rows, token_ref[...], pos, gain_ref[...])
+    hit, seen = cell_hits(ids, cells)
+    dec, normed = norm_cells(dot(hit, rows), seen, token_ref[...], pos, gain_ref[...])
     dec_ref[...] = dec.reshape(dec_ref.shape)
     first_ref[...] = normed[: az * height]
     last_ref[...] = normed[az * height :]
@@ -464,16 +466,27 @@
     size = (rad - 2) * height
     rows = rows_ref[...]
     cells = jnp.where(iota((1, entries), 1) < count_ref[0], cells_ref[...], -1)
-    for a in range(0, az, 2):
-        ids = jnp.concatenate(
-            [iota((size, 1), 0) + (i * rad + 1) * height for i in (a, a + 1)], axis=0
-        )
-        pos = jnp.concatenate(
-            [pos_ref[i, 1 : rad - 1].reshape(size, channels) for i in (a, a + 1)], axis=0
-        )
-        dec, normed = fill_cells(ids, cells, rows, token_ref[...], pos, gain_ref[...])
-        dec_ref[a : a + 2] = dec.reshape(2, size, channels)
-        normed_ref[a : a + 2] = normed.reshape(2, size, channels)
+
+    def pick(a):
+        return cell_hits(iota((size, 1), 0) + (a * rad + 1) * height, cells)
+
+    def finish(a, filled, seen):
+        pos = pos_ref[a, 1 : rad - 1].reshape(size, channels)
+        dec, normed = norm_cells(filled, seen, token_ref[...], pos, gain_ref[...])
+        dec_ref[a] = dec
+        normed_ref[a] = normed
+
+    ahead = pick(0)
+    held = None
+    for a in range(az):
+        hit, seen = ahead
+        if a + 1 < az:
+            ahead = pick(a + 1)
+        filled = dot(hit, rows)
+        if held is not None:
+            finish(*held)
+        held = (a, filled, seen)
+    finish(*held)
 
 
 def place_mid(vis_count, rows, cells, pos, token, gain):

time: 104 us -> 105 us (level); the launches traced: 102 us -> 105 us
  waiting for transfers between devices: 0.93 us -> 2.28 us
  starting transfers between devices: 3.17 us -> 4.24 us
  transfers between devices with their start and end apart: 4 -> 4, of which waited for: 1 -> 2; matrix products, arithmetic and copies ran while one was open for 0% -> 0% of each run, Pallas kernels for 13% -> 10%
where the time goes in v7:
time: 105 us
  blocking collectives  58.7 us (56%)
  Pallas kernels  38.1 us (36%)
  starting transfers between devices  4.24 us (4%)
  waiting for transfers between devices  2.28 us (2%)
  between operations  1.09 us (1%)
    all_to_all x2, blocking collectives, exchange(): lax.all_to_all(values, ('sector', 'blk'), split_axis=0, concat_axis=0, ti...  58.7 us
    pallas_call x1, Pallas kernels, owner_encode(): pl.pallas_call(owner_kernel, out_shape=jax.ShapeDtypeStruct((owners, MSG,...  13.8 us
    pallas_call x1, Pallas kernels, send_rows(): pl.pallas_call(send_kernel, out_shape=(jax.ShapeDtypeStruct((owners, MSG,...  7.09 us
    pallas_call x1, Pallas kernels, conv_inner(): pl.pallas_call(conv_kernel, out_shape=(jax.ShapeDtypeStruct((az * plane,...  7.03 us
    pallas_call x1, Pallas kernels, conv_first(): pl.pallas_call(first_kernel, out_shape=jax.ShapeDtypeStruct((planes, size...  3.02 us
    pallas_call x1, Pallas kernels, place_mid(): pl.pallas_call(mid_kernel, out_shape=(mid, mid), in_specs=[smem] + [vmem]...  2.71 us
    ppermute x1, starting transfers between devices, body(): rad_high = lax.ppermute(edge0, 'blk', inward)  2.66 us
    pallas_call x1, Pallas kernels, conv_edges(): pl.pallas_call(conv_edge_kernel, out_shape=jax.ShapeDtypeStruct(given.sha...  2.22 us
  transfers between devices with their start and end apart: 4, of which 2 were waited for; matrix products, arithmetic and copies ran while one was open for 0% of the time, Pallas kernels for 10%

profile of v7, /device:TPU:0, one launch (start us, length us, event | category | flops | bytes accessed | tf_op | source)
XLA Modules:
  0.0 104.5 jit_solution(7645414222882486759)
XLA Ops:
  0.7 7.1 %send_rows.1 = (bf16[128,40,128]{2,1,0:T(8,128)(2,1)}, s32[1,128]{1,0:T(1,128)}) custom-call(s32[1]{0:T(128)S(6)} %copy.20.count_ref, s32[1,2048]{1,0:T(1,128)} %bitcast.15, s32[1,2048]{1,0:T(1,128)} %bitcast.26, s32[1,2048]{1,0:T(1,128)} %bitcast.27, bf16[2048,256]{1,0:T(8,128)(2,1)} %vis_ref.1, bf16[2560,256]{1,0:T(8,128)(2,1)} %bitcast.11), custom_call_target="tpu_custom_call" | custom-call | tf_op jit(solution)/shard_map/send_rows/pallas_call | solution.py:148
  7.8 0.0 copy-start.2
  7.8 0.0 copy-start.3
  7.8 0.0 copy-start.4
  7.8 0.0 copy-start.5
  7.8 0.0 copy-start.7
  7.8 0.0 copy-start.8
  7.8 0.0 copy-start.9
  7.8 32.9 %all_to_all.10.msg_ref = bf16[128,40,128]{2,1,0:T(8,128)(2,1)S(1)} all-to-all(bf16[128,40,128]{2,1,0:T(8,128)(2,1)} %get-tuple-element.18), channel_id=1, replica_groups=mesh['sector'=32,'blk'=4] {'sector','blk'}, dimensions={0} | all-to-all | bytes 2621440 | tf_op jit(solution)/shard_map/all_to_all | solution.py:800
  40.7 0.0 copy-done.4
  40.7 0.0 copy-done.5
  40.8 13.8 %owner_encode.1 = bf16[128,40,128]{2,1,0:T(8,128)(2,1)S(1)} custom-call(bf16[128,40,128]{2,1,0:T(8,128)(2,1)S(1)} %all_to_all.10.msg_ref, s32[1,1024]{1,0:T(1,128)S(1)} %copy-done.7, f32[1,256]{1,0:T(1,128)S(1)} %bitcast.18, bf16[256,768]{1,0:T(8,128)(2,1)S(1)} %copy-done.4, bf16[256,256]{1,0:T(8,128)(2,1)S(1)} %copy-done.5, f32[1,256]{1,0:T(1,128)S(1)} %bitcast.19, ...), custom_call_target="tpu_custom_call" | custom-call | tf_op jit(solution)/shard_map/owner_encode/pallas_call | solution.py:374
  54.6 0.0 copy-start
  54.6 0.0 copy-start.6
  54.6 0.0 copy-start.10
  54.6 0.0 copy-start.11
  54.6 25.9 %all_to_all.11.back_ref = bf16[128,40,128]{2,1,0:T(8,128)(2,1)S(1)} all-to-all(bf16[128,40,128]{2,1,0:T(8,128)(2,1)S(1)} %owner_encode.1), channel_id=1, replica_groups=mesh['sector'=32,'blk'=4] {'sector','blk'}, dimensions={0} | all-to-all | bytes 2621440 | tf_op jit(solution)/shard_map/all_to_all | solution.py:800
  80.5 2.2 %place_edges.1 = (bf16[2048,256]{1,0:T(8,128)(2,1)S(1)}, bf16[2,320,256]{2,1,0:T(8,128)(2,1)S(1)}, bf16[320,256]{1,0:T(8,128)(2,1)S(1)}, bf16[320,256]{1,0:T(8,128)(2,1)S(1)}) custom-call(s32[1]{0:T(128)S(6)} %copy.20.count_ref, s32[1,128]{1,0:T(1,128)S(1)} %copy-done.12, bf16[128,40,128]{2,1,0:T(8,128)(2,1)S(1)} %all_to_all.11.back_ref, ...), custom_call_target="tpu_custom_call" | custom-call | flops 600000000 | bytes 4000000 | tf_op jit(solution)/shard_map/place_edges/pallas_call | solution.py:448
  82.7 0.0 copy-start.1
  82.7 0.0 copy-start.13
  82.7 2.7 %place_mid.1 = (bf16[8,240,256]{2,1,0:T(8,128)(2,1)S(1)}, bf16[8,240,256]{2,1,0:T(8,128)(2,1)S(1)}) custom-call(s32[1]{0:T(128)S(6)} %copy.20.count_ref, bf16[2048,256]{1,0:T(8,128)(2,1)S(1)} %get-tuple-element.19.rows_ref, s32[1,2048]{1,0:T(1,128)S(1)} %bitcast.17, bf16[8,8,40,256]{3,2,1,0:T(8,128)(2,1)S(1)} %copy-done, f32[1,256]{1,0:T(1,128)S(1)} %bitcast.21, ...), custom_call_target="tpu_custom_call" | custom-call | flops 2000000000 | bytes 6000000 | tf_op jit(solution)/shard_map/place_mid/pallas_call | solution.py:497
  85.5 0.7 collective-permute-start
  86.1 2.7 %collective-permute-start.1 = (bf16[320,256]{1,0:T(8,128)(2,1)S(1)}, bf16[320,256]{1,0:T(8,128)(2,1)S(1)}, u32[]{:S(2)}, u32[]{:S(2)}) collective-permute-start(bf16[320,256]{1,0:T(8,128)(2,1)S(1)} %get-tuple-element.21.edge0_ref), channel_id=1, source_target_pairs={{1,0},{2,1},{3,2},{0,3},{5,4},{6,5},{7,6},{4,7},{9,8},{10,9},{11,1... | collective-permute-start | bytes 491528 | tf_op jit(solution)/shard_map/ppermute | solution.py:829
  88.8 3.0 %conv_first.1.after_ref.first_ref = bf16[3,240,256]{2,1,0:T(8,128)(2,1)S(1)} custom-call(bf16[8,240,256]{2,1,0:T(8,128)(2,1)S(1)} %get-tuple-element.20.mid_ref, bf16[320,256]{1,0:T(8,128)(2,1)S(1)} %get-tuple-element.21.edge0_ref, bf16[320,256]{1,0:T(8,128)(2,1)S(1)} %get-tuple-element.22.edge1_ref, bf16[8,240,256]{2,1,0:T(8,128)(2,1)S(1)} %get-tuple-element.23.mid_dec_ref, ...), custom_call_target="tpu_custom_call" | custom-call | flops 2500000000 | bytes 10000000 | tf_op jit(solution)/shard_map/conv_first/pallas_call | solution.py:608
  91.8 1.3 %collective-permute-done.low_ref = bf16[320,256]{1,0:T(8,128)(2,1)S(1)} collective-permute-done((bf16[320,256]{1,0:T(8,128)(2,1)S(1)}, bf16[320,256]{1,0:T(8,128)(2,1)S(1)}, u32[]{:S(2)}, u32[]{:S(2)}) %collective-permute-start) | collective-permute-done | bytes 163872 | tf_op jit(solution)/shard_map/ppermute | solution.py:828
  93.1 0.0 collective-permute-done.1.high_ref
  93.2 0.1 collective-permute-start.2
  93.3 0.8 collective-permute-start.3
  94.1 7.0 %conv_inner.1 = (bf16[2560,256]{1,0:T(8,128)(2,1)}, f32[2,320,256]{2,1,0:T(8,128)S(1)}) custom-call(bf16[8,240,256]{2,1,0:T(8,128)(2,1)S(1)} %get-tuple-element.20.mid_ref, bf16[320,256]{1,0:T(8,128)(2,1)S(1)} %get-tuple-element.21.edge0_ref, bf16[320,256]{1,0:T(8,128)(2,1)S(1)} %get-tuple-element.22.edge1_ref, ...), custom_call_target="tpu_custom_call" | custom-call | flops 6000000000 | bytes 10000000 | tf_op jit(solution)/shard_map/conv_inner/pallas_call | solution.py:720
  101.1 0.0 collective-permute-done.2.near_ref
  101.1 1.0 collective-permute-done.3.far_ref
  102.1 2.2 %conv_edges.1 = bf16[2560,256]{1,0:T(8,128)(2,1)} custom-call(bf16[400,256]{1,0:T(8,128)(2,1)S(1)} %collective-permute-done.2.near_ref, bf16[400,256]{1,0:T(8,128)(2,1)S(1)} %collective-permute-done.3.far_ref, f32[2,320,256]{2,1,0:T(8,128)S(1)} %get-tuple-element.27.partial_ref, ...), custom_call_target="tpu_custom_call", output_to_operand_aliasing={{}: (6, {})} | custom-call | tf_op jit(solution)/shard_map/conv_edges/pallas_call | solution.py:783
  (14 shorter events, 0.1 us)
Async XLA Ops:
  7.8 33.0 %copy-start.2 = (bf16[256,1024]{1,0:T(8,128)(2,1)S(1)}, bf16[256,1024]{1,0:T(8,128)(2,1)}, u32[]{:S(2)}) copy-start(bf16[256,1024]{1,0:T(8,128)(2,1)} %mlp_in_ref.1) | copy-start | bytes 1572868
  7.8 33.0 %copy-start.3 = (bf16[1024,256]{1,0:T(8,128)(2,1)S(1)}, bf16[1024,256]{1,0:T(8,128)(2,1)}, u32[]{:S(2)}) copy-start(bf16[1024,256]{1,0:T(8,128)(2,1)} %mlp_out_ref.1) | copy-start | bytes 1572868
  7.8 33.0 %copy-start.4 = (bf16[256,768]{1,0:T(8,128)(2,1)S(1)}, bf16[256,768]{1,0:T(8,128)(2,1)}, u32[]{:S(2)}) copy-start(bf16[256,768]{1,0:T(8,128)(2,1)} %attn_in_ref.1) | copy-start | bytes 1179652
  7.8 33.0 %copy-start.5 = (bf16[256,256]{1,0:T(8,128)(2,1)S(1)}, bf16[256,256]{1,0:T(8,128)(2,1)}, u32[]{:S(2)}) copy-start(bf16[256,256]{1,0:T(8,128)(2,1)} %attn_out_ref.1) | copy-start | bytes 393220
  7.8 32.9 %copy-start.7 = (s32[1,1024]{1,0:T(1,128)S(1)}, s32[1,1024]{1,0:T(1,128)}, u32[]{:S(2)}) copy-start(s32[1,1024]{1,0:T(1,128)} %window_ref.1) | copy-start | bytes 12292
  7.8 32.9 %copy-start.8 = (f32[256]{0:T(256)S(1)}, f32[256]{0:T(256)}, u32[]{:S(2)}) copy-start(f32[256]{0:T(256)} %param.24) | copy-start | bytes 3076
  7.8 32.9 %copy-start.9 = (f32[256]{0:T(256)S(1)}, f32[256]{0:T(256)}, u32[]{:S(2)}) copy-start(f32[256]{0:T(256)} %param.27) | copy-start | bytes 3076
  54.6 25.9 %copy-start = (bf16[8,8,40,256]{3,2,1,0:T(8,128)(2,1)S(1)}, bf16[8,8,40,256]{3,2,1,0:T(8,128)(2,1)}, u32[]{:S(2)}) copy-start(bf16[8,8,40,256]{3,2,1,0:T(8,128)(2,1)} %pos_ref.3) | copy-start | bytes 3932164
  54.6 25.9 %copy-start.6 = (s32[2048]{0:T(1024)S(1)}, s32[2048]{0:T(1024)}, u32[]{:S(2)}) copy-start(s32[2048]{0:T(1024)} %param.19) | copy-start | bytes 24580
  54.6 25.9 %copy-start.10 = (f32[256]{0:T(256)S(1)}, f32[256]{0:T(256)}, u32[]{:S(2)}) copy-start(f32[256]{0:T(256)} %param.30) | copy-start | bytes 3076
  54.6 25.9 %copy-start.11 = (f32[256]{0:T(256)S(1)}, f32[256]{0:T(256)}, u32[]{:S(2)}) copy-start(f32[256]{0:T(256)} %param.31) | copy-start | bytes 3076
  54.6 25.9 %copy-start.12 = (s32[1,128]{1,0:T(1,128)S(1)}, s32[1,128]{1,0:T(1,128)}, u32[]{:S(2)}) copy-start(s32[1,128]{1,0:T(1,128)} %get-tuple-element.17.starts_ref) | copy-start | bytes 1540
  82.7 6.0 %copy-start.1 = (bf16[27,256,256]{2,1,0:T(8,128)(2,1)S(1)}, bf16[27,256,256]{2,1,0:T(8,128)(2,1)}, u32[]{:S(2)}) copy-start(bf16[27,256,256]{2,1,0:T(8,128)(2,1)} %param.32) | copy-start | bytes 10616836
  82.7 6.0 %copy-start.13 = (f32[256]{0:T(256)S(1)}, f32[256]{0:T(256)}, u32[]{:S(2)}) copy-start(f32[256]{0:T(256)} %param.33) | copy-start | bytes 3076
  85.5 7.7 %collective-permute-start = (bf16[320,256]{1,0:T(8,128)(2,1)S(1)}, bf16[320,256]{1,0:T(8,128)(2,1)S(1)}, u32[]{:S(2)}, u32[]{:S(2)}) collective-permute-start(bf16[320,256]{1,0:T(8,128)(2,1)S(1)} %get-tuple-element.22.edge1_ref), channel_id=1, source_target_pairs={{0,1},{1,2},{2,3},{3,0},{4,5},{5,6},{6,7},{7,4},{8,9},{9,10},{10,1... | collective-permute-start | bytes 491528 | tf_op jit(solution)/shard_map/ppermute | solution.py:828
  86.1 7.0 %collective-permute-start.1 = (bf16[320,256]{1,0:T(8,128)(2,1)S(1)}, bf16[320,256]{1,0:T(8,128)(2,1)S(1)}, u32[]{:S(2)}, u32[]{:S(2)}) collective-permute-start(bf16[320,256]{1,0:T(8,128)(2,1)S(1)} %get-tuple-element.21.edge0_ref), channel_id=1, source_target_pairs={{1,0},{2,1},{3,2},{0,3},{5,4},{6,5},{7,6},{4,7},{9,8},{10,9},{11,1... | collective-permute-start | bytes 491528 | tf_op jit(solution)/shard_map/ppermute | solution.py:829
  93.2 8.0 %collective-permute-start.2 = (bf16[400,256]{1,0:T(8,128)(2,1)S(1)}, bf16[400,256]{1,0:T(8,128)(2,1)S(1)}, u32[]{:S(2)}, u32[]{:S(2)}) collective-permute-start(bf16[400,256]{1,0:T(8,128)(2,1)S(1)} %get-tuple-element.24), channel_id=1, source_target_pairs={{0,4},{8,12},{16,20},{24,28},{32,36},{40,44},{48,52},{56,60},{64,6... | collective-permute-start | bytes 614408 | tf_op jit(solution)/shard_map/ppermute | solution.py:837
  93.3 8.8 %collective-permute-start.3 = (bf16[400,256]{1,0:T(8,128)(2,1)S(1)}, bf16[400,256]{1,0:T(8,128)(2,1)S(1)}, u32[]{:S(2)}, u32[]{:S(2)}) collective-permute-start(bf16[400,256]{1,0:T(8,128)(2,1)S(1)} %get-tuple-element.25), channel_id=1, source_target_pairs={{4,8},{12,16},{20,24},{28,32},{36,40},{44,48},{52,56},{60,64},{68,... | collective-permute-start | bytes 614408 | tf_op jit(solution)/shard_map/ppermute | solution.py:838

commit v8 on v7

--- a/solution.py
+++ b/solution.py
@@ -500,7 +500,7 @@
         in_specs=[smem] + [vmem] * 5,
         out_specs=(vmem, vmem),
         compiler_params=pltpu.CompilerParams(vmem_limit_bytes=24 * 2**20),
-        cost_estimate=pl.CostEstimate(flops=2 * 10**9, bytes_accessed=6 * 10**6, transcendentals=0),
+        cost_estimate=pl.CostEstimate(flops=3 * 10**8, bytes_accessed=10**6, transcendentals=0),
         name="place_mid",
     )(vis_count, rows, cells, pos, token, gain)
 
@@ -612,7 +612,7 @@
         out_specs=vmem,
         scratch_shapes=[pltpu.VMEM(((planes + 2) * pitch, 3 * channels), BF16)],
         compiler_params=pltpu.CompilerParams(vmem_limit_bytes=24 * 2**20),
-        cost_estimate=pl.CostEstimate(flops=25 * 10**8, bytes_accessed=10**7, transcendentals=0),
+        cost_estimate=pl.CostEstimate(flops=3 * 10**8, bytes_accessed=10**6, transcendentals=0),
         name="conv_first",
     )(mid, edge0, edge1, mid_dec, weight, bias)
 

time: 105 us -> 104 us (level)
  waiting for transfers between devices: 2.28 us -> 0.81 us
    ppermute x1, waiting for transfers between devices: 1.32 us -> 0.01 us  [body(): rad_low = lax.ppermute(edge1, 'blk', outward)]
  transfers between devices with their start and end apart: 4 -> 4, of which waited for: 2 -> 1; matrix products, arithmetic and copies ran while one was open for 0% -> 0% of each run, Pallas kernels for 10% -> 12%
where the time goes in v8:
time: 104 us; the launch traced here: 103 us
  blocking collectives  58.7 us (56%)
  Pallas kernels  38.1 us (37%)
  starting transfers between devices  4.39 us (4%)
  between operations  1.12 us (1%)
    all_to_all x2, blocking collectives, exchange(): lax.all_to_all(values, ('sector', 'blk'), split_axis=0, concat_axis=0, ti...  58.7 us
    pallas_call x1, Pallas kernels, owner_encode(): pl.pallas_call(owner_kernel, out_shape=jax.ShapeDtypeStruct((owners, MSG,...  13.8 us
    pallas_call x1, Pallas kernels, send_rows(): pl.pallas_call(send_kernel, out_shape=(jax.ShapeDtypeStruct((owners, MSG,...  7.09 us
    pallas_call x1, Pallas kernels, conv_inner(): pl.pallas_call(conv_kernel, out_shape=(jax.ShapeDtypeStruct((az * plane,...  7.03 us
    pallas_call x1, Pallas kernels, conv_first(): pl.pallas_call(first_kernel, out_shape=jax.ShapeDtypeStruct((planes, size...  3.02 us
    pallas_call x1, Pallas kernels, place_mid(): pl.pallas_call(mid_kernel, out_shape=(mid, mid), in_specs=[smem] + [vmem]...  2.75 us
    ppermute x1, starting transfers between devices, body(): rad_high = lax.ppermute(edge0, 'blk', inward)  2.66 us
    pallas_call x1, Pallas kernels, conv_edges(): pl.pallas_call(conv_edge_kernel, out_shape=jax.ShapeDtypeStruct(given.sha...  2.22 us
  transfers between devices with their start and end apart: 4, of which 1 were waited for; matrix products, arithmetic and copies ran while one was open for 0% of the time, Pallas kernels for 12%

profile of v8, /device:TPU:0, one launch (start us, length us, event | category | flops | bytes accessed | tf_op | source)
XLA Modules:
  0.0 103.3 jit_solution(14766646551417564993)
XLA Ops:
  0.7 7.1 %send_rows.1 = (bf16[128,40,128]{2,1,0:T(8,128)(2,1)}, s32[1,128]{1,0:T(1,128)}) custom-call(s32[1]{0:T(128)S(6)} %copy.20.count_ref, s32[1,2048]{1,0:T(1,128)} %bitcast.15, s32[1,2048]{1,0:T(1,128)} %bitcast.26, s32[1,2048]{1,0:T(1,128)} %bitcast.27, bf16[2048,256]{1,0:T(8,128)(2,1)} %vis_ref.1, bf16[2560,256]{1,0:T(8,128)(2,1)} %bitcast.14), custom_call_target="tpu_custom_call" | custom-call | tf_op jit(solution)/shard_map/send_rows/pallas_call | solution.py:148
  7.8 0.0 copy-start.2
  7.8 0.0 copy-start.3
  7.8 0.0 copy-start.4
  7.8 0.0 copy-start.5
  7.8 0.0 copy-start.7
  7.8 0.0 copy-start.10
  7.8 0.0 copy-start.11
  7.8 32.9 %all_to_all.10.msg_ref = bf16[128,40,128]{2,1,0:T(8,128)(2,1)S(1)} all-to-all(bf16[128,40,128]{2,1,0:T(8,128)(2,1)} %get-tuple-element.18), channel_id=1, replica_groups=mesh['sector'=32,'blk'=4] {'sector','blk'}, dimensions={0} | all-to-all | bytes 2621440 | tf_op jit(solution)/shard_map/all_to_all | solution.py:800
  40.7 0.0 copy-done.2
  40.7 0.0 copy-done.3
  40.8 13.8 %owner_encode.1 = bf16[128,40,128]{2,1,0:T(8,128)(2,1)S(1)} custom-call(bf16[128,40,128]{2,1,0:T(8,128)(2,1)S(1)} %all_to_all.10.msg_ref, s32[1,1024]{1,0:T(1,128)S(1)} %copy-done.7, f32[1,256]{1,0:T(1,128)S(1)} %bitcast.22, bf16[256,768]{1,0:T(8,128)(2,1)S(1)} %copy-done.4, bf16[256,256]{1,0:T(8,128)(2,1)S(1)} %copy-done.5, f32[1,256]{1,0:T(1,128)S(1)} %bitcast.23, ...), custom_call_target="tpu_custom_call" | custom-call | tf_op jit(solution)/shard_map/owner_encode/pallas_call | solution.py:374
  54.6 0.0 copy-start.1
  54.6 0.0 copy-start.6
  54.6 0.0 copy-start.8
  54.6 0.0 copy-start.9
  54.6 25.9 %all_to_all.11.back_ref = bf16[128,40,128]{2,1,0:T(8,128)(2,1)S(1)} all-to-all(bf16[128,40,128]{2,1,0:T(8,128)(2,1)S(1)} %owner_encode.1), channel_id=1, replica_groups=mesh['sector'=32,'blk'=4] {'sector','blk'}, dimensions={0} | all-to-all | bytes 2621440 | tf_op jit(solution)/shard_map/all_to_all | solution.py:800
  80.5 0.0 copy-start
  80.5 2.2 %place_edges.1 = (bf16[2048,256]{1,0:T(8,128)(2,1)S(1)}, bf16[2,320,256]{2,1,0:T(8,128)(2,1)S(1)}, bf16[320,256]{1,0:T(8,128)(2,1)S(1)}, bf16[320,256]{1,0:T(8,128)(2,1)S(1)}) custom-call(s32[1]{0:T(128)S(6)} %copy.20.count_ref, s32[1,128]{1,0:T(1,128)S(1)} %copy-done.13, bf16[128,40,128]{2,1,0:T(8,128)(2,1)S(1)} %all_to_all.11.back_ref, ...), custom_call_target="tpu_custom_call" | custom-call | flops 600000000 | bytes 4000000 | tf_op jit(solution)/shard_map/place_edges/pallas_call | solution.py:448
  82.7 0.0 copy-start.12
  82.7 0.6 collective-permute-start
  83.4 2.7 %collective-permute-start.1 = (bf16[320,256]{1,0:T(8,128)(2,1)S(1)}, bf16[320,256]{1,0:T(8,128)(2,1)S(1)}, u32[]{:S(2)}, u32[]{:S(2)}) collective-permute-start(bf16[320,256]{1,0:T(8,128)(2,1)S(1)} %get-tuple-element.21.edge0_ref), channel_id=1, source_target_pairs={{1,0},{2,1},{3,2},{0,3},{5,4},{6,5},{7,6},{4,7},{9,8},{10,9},{11,1... | collective-permute-start | bytes 491528 | tf_op jit(solution)/shard_map/ppermute | solution.py:829
  86.0 2.8 %place_mid.1 = (bf16[8,240,256]{2,1,0:T(8,128)(2,1)S(1)}, bf16[8,240,256]{2,1,0:T(8,128)(2,1)S(1)}) custom-call(s32[1]{0:T(128)S(6)} %copy.20.count_ref, bf16[2048,256]{1,0:T(8,128)(2,1)S(1)} %get-tuple-element.19.rows_ref, s32[1,2048]{1,0:T(1,128)S(1)} %bitcast.17, bf16[8,8,40,256]{3,2,1,0:T(8,128)(2,1)S(1)} %copy-done.1, f32[1,256]{1,0:T(1,128)S(1)} %bitcast.19, ...), custom_call_target="tpu_custom_call" | custom-call | flops 300000000 | bytes 1000000 | tf_op jit(solution)/shard_map/place_mid/pallas_call | solution.py:497
  88.8 3.0 %conv_first.1.after_ref.first_ref = bf16[3,240,256]{2,1,0:T(8,128)(2,1)S(1)} custom-call(bf16[8,240,256]{2,1,0:T(8,128)(2,1)S(1)} %get-tuple-element.20.mid_ref, bf16[320,256]{1,0:T(8,128)(2,1)S(1)} %get-tuple-element.21.edge0_ref, bf16[320,256]{1,0:T(8,128)(2,1)S(1)} %get-tuple-element.22.edge1_ref, bf16[8,240,256]{2,1,0:T(8,128)(2,1)S(1)} %get-tuple-element.23.mid_dec_ref, ...), custom_call_target="tpu_custom_call" | custom-call | flops 300000000 | bytes 1000000 | tf_op jit(solution)/shard_map/conv_first/pallas_call | solution.py:608
  91.9 0.0 collective-permute-done.low_ref
  91.9 0.0 collective-permute-done.1.high_ref
  91.9 0.1 collective-permute-start.2
  92.0 1.0 collective-permute-start.3
  93.0 7.0 %conv_inner.1 = (bf16[2560,256]{1,0:T(8,128)(2,1)}, f32[2,320,256]{2,1,0:T(8,128)S(1)}) custom-call(bf16[8,240,256]{2,1,0:T(8,128)(2,1)S(1)} %get-tuple-element.20.mid_ref, bf16[320,256]{1,0:T(8,128)(2,1)S(1)} %get-tuple-element.21.edge0_ref, bf16[320,256]{1,0:T(8,128)(2,1)S(1)} %get-tuple-element.22.edge1_ref, ...), custom_call_target="tpu_custom_call" | custom-call | flops 6000000000 | bytes 10000000 | tf_op jit(solution)/shard_map/conv_inner/pallas_call | solution.py:720
  100.1 0.0 collective-permute-done.2.near_ref
  100.1 0.8 collective-permute-done.3.far_ref
  100.9 2.2 %conv_edges.1 = bf16[2560,256]{1,0:T(8,128)(2,1)} custom-call(bf16[400,256]{1,0:T(8,128)(2,1)S(1)} %collective-permute-done.2.near_ref, bf16[400,256]{1,0:T(8,128)(2,1)S(1)} %collective-permute-done.3.far_ref, f32[2,320,256]{2,1,0:T(8,128)S(1)} %get-tuple-element.27.partial_ref, ...), custom_call_target="tpu_custom_call", output_to_operand_aliasing={{}: (6, {})} | custom-call | tf_op jit(solution)/shard_map/conv_edges/pallas_call | solution.py:783
  (14 shorter events, 0.1 us)
Async XLA Ops:
  7.8 33.0 %copy-start.2 = (bf16[256,1024]{1,0:T(8,128)(2,1)S(1)}, bf16[256,1024]{1,0:T(8,128)(2,1)}, u32[]{:S(2)}) copy-start(bf16[256,1024]{1,0:T(8,128)(2,1)} %mlp_in_ref.1) | copy-start | bytes 1572868
  7.8 33.0 %copy-start.3 = (bf16[1024,256]{1,0:T(8,128)(2,1)S(1)}, bf16[1024,256]{1,0:T(8,128)(2,1)}, u32[]{:S(2)}) copy-start(bf16[1024,256]{1,0:T(8,128)(2,1)} %mlp_out_ref.1) | copy-start | bytes 1572868
  7.8 33.0 %copy-start.4 = (bf16[256,768]{1,0:T(8,128)(2,1)S(1)}, bf16[256,768]{1,0:T(8,128)(2,1)}, u32[]{:S(2)}) copy-start(bf16[256,768]{1,0:T(8,128)(2,1)} %attn_in_ref.1) | copy-start | bytes 1179652
  7.8 33.0 %copy-start.5 = (bf16[256,256]{1,0:T(8,128)(2,1)S(1)}, bf16[256,256]{1,0:T(8,128)(2,1)}, u32[]{:S(2)}) copy-start(bf16[256,256]{1,0:T(8,128)(2,1)} %attn_out_ref.1) | copy-start | bytes 393220
  7.8 32.9 %copy-start.7 = (s32[1,1024]{1,0:T(1,128)S(1)}, s32[1,1024]{1,0:T(1,128)}, u32[]{:S(2)}) copy-start(s32[1,1024]{1,0:T(1,128)} %window_ref.1) | copy-start | bytes 12292
  7.8 32.9 %copy-start.10 = (f32[256]{0:T(256)S(1)}, f32[256]{0:T(256)}, u32[]{:S(2)}) copy-start(f32[256]{0:T(256)} %param.24) | copy-start | bytes 3076
  7.8 32.9 %copy-start.11 = (f32[256]{0:T(256)S(1)}, f32[256]{0:T(256)}, u32[]{:S(2)}) copy-start(f32[256]{0:T(256)} %param.27) | copy-start | bytes 3076
  54.6 25.9 %copy-start.1 = (bf16[8,8,40,256]{3,2,1,0:T(8,128)(2,1)S(1)}, bf16[8,8,40,256]{3,2,1,0:T(8,128)(2,1)}, u32[]{:S(2)}) copy-start(bf16[8,8,40,256]{3,2,1,0:T(8,128)(2,1)} %pos_ref.3) | copy-start | bytes 3932164
  54.6 25.9 %copy-start.6 = (s32[2048]{0:T(1024)S(1)}, s32[2048]{0:T(1024)}, u32[]{:S(2)}) copy-start(s32[2048]{0:T(1024)} %param.19) | copy-start | bytes 24580
  54.6 25.9 %copy-start.8 = (f32[256]{0:T(256)S(1)}, f32[256]{0:T(256)}, u32[]{:S(2)}) copy-start(f32[256]{0:T(256)} %param.30) | copy-start | bytes 3076
  54.6 25.9 %copy-start.9 = (f32[256]{0:T(256)S(1)}, f32[256]{0:T(256)}, u32[]{:S(2)}) copy-start(f32[256]{0:T(256)} %param.31) | copy-start | bytes 3076
  54.6 25.9 %copy-start.13 = (s32[1,128]{1,0:T(1,128)S(1)}, s32[1,128]{1,0:T(1,128)}, u32[]{:S(2)}) copy-start(s32[1,128]{1,0:T(1,128)} %get-tuple-element.17.starts_ref) | copy-start | bytes 1540
  80.5 8.3 %copy-start = (bf16[27,256,256]{2,1,0:T(8,128)(2,1)S(1)}, bf16[27,256,256]{2,1,0:T(8,128)(2,1)}, u32[]{:S(2)}) copy-start(bf16[27,256,256]{2,1,0:T(8,128)(2,1)} %param.32) | copy-start | bytes 10616836
  82.7 6.1 %copy-start.12 = (f32[256]{0:T(256)S(1)}, f32[256]{0:T(256)}, u32[]{:S(2)}) copy-start(f32[256]{0:T(256)} %param.33) | copy-start | bytes 3076
  82.7 9.1 %collective-permute-start = (bf16[320,256]{1,0:T(8,128)(2,1)S(1)}, bf16[320,256]{1,0:T(8,128)(2,1)S(1)}, u32[]{:S(2)}, u32[]{:S(2)}) collective-permute-start(bf16[320,256]{1,0:T(8,128)(2,1)S(1)} %get-tuple-element.22.edge1_ref), channel_id=1, source_target_pairs={{0,1},{1,2},{2,3},{3,0},{4,5},{5,6},{6,7},{7,4},{8,9},{9,10},{10,1... | collective-permute-start | bytes 491528 | tf_op jit(solution)/shard_map/ppermute | solution.py:828
  83.4 8.5 %collective-permute-start.1 = (bf16[320,256]{1,0:T(8,128)(2,1)S(1)}, bf16[320,256]{1,0:T(8,128)(2,1)S(1)}, u32[]{:S(2)}, u32[]{:S(2)}) collective-permute-start(bf16[320,256]{1,0:T(8,128)(2,1)S(1)} %get-tuple-element.21.edge0_ref), channel_id=1, source_target_pairs={{1,0},{2,1},{3,2},{0,3},{5,4},{6,5},{7,6},{4,7},{9,8},{10,9},{11,1... | collective-permute-start | bytes 491528 | tf_op jit(solution)/shard_map/ppermute | solution.py:829
  91.9 8.1 %collective-permute-start.2 = (bf16[400,256]{1,0:T(8,128)(2,1)S(1)}, bf16[400,256]{1,0:T(8,128)(2,1)S(1)}, u32[]{:S(2)}, u32[]{:S(2)}) collective-permute-start(bf16[400,256]{1,0:T(8,128)(2,1)S(1)} %get-tuple-element.24), channel_id=1, source_target_pairs={{0,4},{8,12},{16,20},{24,28},{32,36},{40,44},{48,52},{56,60},{64,6... | collective-permute-start | bytes 614408 | tf_op jit(solution)/shard_map/ppermute | solution.py:837
  92.0 8.8 %collective-permute-start.3 = (bf16[400,256]{1,0:T(8,128)(2,1)S(1)}, bf16[400,256]{1,0:T(8,128)(2,1)S(1)}, u32[]{:S(2)}, u32[]{:S(2)}) collective-permute-start(bf16[400,256]{1,0:T(8,128)(2,1)S(1)} %get-tuple-element.25), channel_id=1, source_target_pairs={{4,8},{12,16},{20,24},{28,32},{36,40},{44,48},{52,56},{60,64},{68,... | collective-permute-start | bytes 614408 | tf_op jit(solution)/shard_map/ppermute | solution.py:838

commit v9 on v8

--- a/solution.py
+++ b/solution.py
@@ -12,7 +12,7 @@
 I16 = jnp.int16
 I32 = jnp.int32
 CAP = 18
-PLANES_FIRST = 3
+PLANES_FIRST = 2
 MSG = 40
 
 
@@ -825,8 +825,8 @@
     rows, edge_dec, edge0, edge1 = place_edges(vis_count, starts, back, cells, grid_pos, token, gain)
     outward = [(i, (i + 1) % n_blk) for i in range(n_blk)]
     inward = [(t, s) for s, t in outward]
+    rad_high = lax.ppermute(edge0, "blk", inward)
     rad_low = lax.ppermute(edge1, "blk", outward)
-    rad_high = lax.ppermute(edge0, "blk", inward)
     mid_dec, mid = place_mid(vis_count, rows, cells, grid_pos, token, gain)
     weight = conv_weight.reshape(9, 3 * channels, channels)
     bias = conv_bias.reshape(1, -1)

time: 104 us -> 104 us (level)
  starting transfers between devices: 4.39 us -> 3.18 us
    ppermute x1, waiting for transfers between devices: 0.01 us -> 1.26 us  [body(): rad_low = lax.ppermute(edge1, 'blk', outward)]
where the time goes in v9:
time: 104 us; the launch traced here: 102 us
  blocking collectives  58.7 us (56%)
  Pallas kernels  38.1 us (37%)
  starting transfers between devices  3.18 us (3%)
  waiting for transfers between devices  1.26 us (1%)
  between operations  1.12 us (1%)
    all_to_all x2, blocking collectives, exchange(): lax.all_to_all(values, ('sector', 'blk'), split_axis=0, concat_axis=0, ti...  58.7 us
    pallas_call x1, Pallas kernels, owner_encode(): pl.pallas_call(owner_kernel, out_shape=jax.ShapeDtypeStruct((owners, MSG,...  13.8 us
    pallas_call x1, Pallas kernels, conv_inner(): pl.pallas_call(conv_kernel, out_shape=(jax.ShapeDtypeStruct((az * plane,...  7.91 us
    pallas_call x1, Pallas kernels, send_rows(): pl.pallas_call(send_kernel, out_shape=(jax.ShapeDtypeStruct((owners, MSG,...  7.09 us
    pallas_call x1, Pallas kernels, place_mid(): pl.pallas_call(mid_kernel, out_shape=(mid, mid), in_specs=[smem] + [vmem]...  2.75 us
    pallas_call x1, Pallas kernels, conv_edges(): pl.pallas_call(conv_edge_kernel, out_shape=jax.ShapeDtypeStruct(given.sha...  2.24 us
    pallas_call x1, Pallas kernels, place_edges(): pl.pallas_call(edge_kernel, out_shape=(jax.ShapeDtypeStruct((entries, cha...  2.19 us
    pallas_call x1, Pallas kernels, conv_first(): pl.pallas_call(first_kernel, out_shape=jax.ShapeDtypeStruct((planes, size...  2.08 us
  transfers between devices with their start and end apart: 4, of which 1 were waited for; matrix products, arithmetic and copies ran while one was open for 0% of the time, Pallas kernels for 12%

profile of v9, /device:TPU:0, one launch (start us, length us, event | category | flops | bytes accessed | tf_op | source)
XLA Modules:
  0.0 102.5 jit_solution(7558733783697057816)
XLA Ops:
  0.7 7.1 %send_rows.1 = (bf16[128,40,128]{2,1,0:T(8,128)(2,1)}, s32[1,128]{1,0:T(1,128)}) custom-call(s32[1]{0:T(128)S(6)} %copy.20.count_ref, s32[1,2048]{1,0:T(1,128)} %bitcast.15, s32[1,2048]{1,0:T(1,128)} %bitcast.26, s32[1,2048]{1,0:T(1,128)} %bitcast.27, bf16[2048,256]{1,0:T(8,128)(2,1)} %vis_ref.1, bf16[2560,256]{1,0:T(8,128)(2,1)} %bitcast.14), custom_call_target="tpu_custom_call" | custom-call | tf_op jit(solution)/shard_map/send_rows/pallas_call | solution.py:148
  7.8 0.0 copy-start.2
  7.8 0.0 copy-start.3
  7.8 0.0 copy-start.4
  7.8 0.0 copy-start.5
  7.8 0.0 copy-start.7
  7.8 0.0 copy-start.10
  7.8 0.0 copy-start.11
  7.8 32.9 %all_to_all.10.msg_ref = bf16[128,40,128]{2,1,0:T(8,128)(2,1)S(1)} all-to-all(bf16[128,40,128]{2,1,0:T(8,128)(2,1)} %get-tuple-element.18), channel_id=1, replica_groups=mesh['sector'=32,'blk'=4] {'sector','blk'}, dimensions={0} | all-to-all | bytes 2621440 | tf_op jit(solution)/shard_map/all_to_all | solution.py:800
  40.7 0.0 copy-done.2
  40.7 0.0 copy-done.4
  40.8 13.8 %owner_encode.1 = bf16[128,40,128]{2,1,0:T(8,128)(2,1)S(1)} custom-call(bf16[128,40,128]{2,1,0:T(8,128)(2,1)S(1)} %all_to_all.10.msg_ref, s32[1,1024]{1,0:T(1,128)S(1)} %copy-done.7, f32[1,256]{1,0:T(1,128)S(1)} %bitcast.22, bf16[256,768]{1,0:T(8,128)(2,1)S(1)} %copy-done.4, bf16[256,256]{1,0:T(8,128)(2,1)S(1)} %copy-done.5, f32[1,256]{1,0:T(1,128)S(1)} %bitcast.23, ...), custom_call_target="tpu_custom_call" | custom-call | tf_op jit(solution)/shard_map/owner_encode/pallas_call | solution.py:374
  54.6 0.0 copy-start.1
  54.6 0.0 copy-start.6
  54.6 0.0 copy-start.8
  54.6 0.0 copy-start.9
  54.6 25.9 %all_to_all.11.back_ref = bf16[128,40,128]{2,1,0:T(8,128)(2,1)S(1)} all-to-all(bf16[128,40,128]{2,1,0:T(8,128)(2,1)S(1)} %owner_encode.1), channel_id=1, replica_groups=mesh['sector'=32,'blk'=4] {'sector','blk'}, dimensions={0} | all-to-all | bytes 2621440 | tf_op jit(solution)/shard_map/all_to_all | solution.py:800
  80.5 0.0 copy-start
  80.5 2.2 %place_edges.1 = (bf16[2048,256]{1,0:T(8,128)(2,1)S(1)}, bf16[2,320,256]{2,1,0:T(8,128)(2,1)S(1)}, bf16[320,256]{1,0:T(8,128)(2,1)S(1)}, bf16[320,256]{1,0:T(8,128)(2,1)S(1)}) custom-call(s32[1]{0:T(128)S(6)} %copy.20.count_ref, s32[1,128]{1,0:T(1,128)S(1)} %copy-done.13, bf16[128,40,128]{2,1,0:T(8,128)(2,1)S(1)} %all_to_all.11.back_ref, ...), custom_call_target="tpu_custom_call" | custom-call | flops 600000000 | bytes 4000000 | tf_op jit(solution)/shard_map/place_edges/pallas_call | solution.py:448
  82.7 0.0 copy-start.12
  82.7 1.7 %collective-permute-start.1 = (bf16[320,256]{1,0:T(8,128)(2,1)S(1)}, bf16[320,256]{1,0:T(8,128)(2,1)S(1)}, u32[]{:S(2)}, u32[]{:S(2)}) collective-permute-start(bf16[320,256]{1,0:T(8,128)(2,1)S(1)} %get-tuple-element.21.edge0_ref), channel_id=1, source_target_pairs={{1,0},{2,1},{3,2},{0,3},{5,4},{6,5},{7,6},{4,7},{9,8},{10,9},{11,1... | collective-permute-start | bytes 491528 | tf_op jit(solution)/shard_map/ppermute | solution.py:828
  84.4 0.4 collective-permute-start
  84.8 2.7 %place_mid.1 = (bf16[8,240,256]{2,1,0:T(8,128)(2,1)S(1)}, bf16[8,240,256]{2,1,0:T(8,128)(2,1)S(1)}) custom-call(s32[1]{0:T(128)S(6)} %copy.20.count_ref, bf16[2048,256]{1,0:T(8,128)(2,1)S(1)} %get-tuple-element.19.rows_ref, s32[1,2048]{1,0:T(1,128)S(1)} %bitcast.17, bf16[8,8,40,256]{3,2,1,0:T(8,128)(2,1)S(1)} %copy-done.1, f32[1,256]{1,0:T(1,128)S(1)} %bitcast.19, ...), custom_call_target="tpu_custom_call" | custom-call | flops 300000000 | bytes 1000000 | tf_op jit(solution)/shard_map/place_mid/pallas_call | solution.py:497
  87.6 2.1 %conv_first.1.after_ref.first_ref = bf16[2,240,256]{2,1,0:T(8,128)(2,1)S(1)} custom-call(bf16[8,240,256]{2,1,0:T(8,128)(2,1)S(1)} %get-tuple-element.20.mid_ref, bf16[320,256]{1,0:T(8,128)(2,1)S(1)} %get-tuple-element.21.edge0_ref, bf16[320,256]{1,0:T(8,128)(2,1)S(1)} %get-tuple-element.22.edge1_ref, bf16[8,240,256]{2,1,0:T(8,128)(2,1)S(1)} %get-tuple-element.23.mid_dec_ref, ...), custom_call_target="tpu_custom_call" | custom-call | flops 300000000 | bytes 1000000 | tf_op jit(solution)/shard_map/conv_first/pallas_call | solution.py:608
  89.7 0.0 collective-permute-done.1.high_ref
  89.7 1.3 %collective-permute-done.low_ref = bf16[320,256]{1,0:T(8,128)(2,1)S(1)} collective-permute-done((bf16[320,256]{1,0:T(8,128)(2,1)S(1)}, bf16[320,256]{1,0:T(8,128)(2,1)S(1)}, u32[]{:S(2)}, u32[]{:S(2)}) %collective-permute-start) | collective-permute-done | bytes 163872 | tf_op jit(solution)/shard_map/ppermute | solution.py:829
  91.0 0.1 collective-permute-start.2
  91.1 1.0 collective-permute-start.3
  92.1 7.9 %conv_inner.1 = (bf16[2560,256]{1,0:T(8,128)(2,1)}, f32[2,320,256]{2,1,0:T(8,128)S(1)}) custom-call(bf16[8,240,256]{2,1,0:T(8,128)(2,1)S(1)} %get-tuple-element.20.mid_ref, bf16[320,256]{1,0:T(8,128)(2,1)S(1)} %get-tuple-element.21.edge0_ref, bf16[320,256]{1,0:T(8,128)(2,1)S(1)} %get-tuple-element.22.edge1_ref, ...), custom_call_target="tpu_custom_call" | custom-call | flops 6000000000 | bytes 10000000 | tf_op jit(solution)/shard_map/conv_inner/pallas_call | solution.py:720
  100.0 0.0 collective-permute-done.2.near_ref
  100.0 0.0 collective-permute-done.3.far_ref
  100.0 2.2 %conv_edges.1 = bf16[2560,256]{1,0:T(8,128)(2,1)} custom-call(bf16[400,256]{1,0:T(8,128)(2,1)S(1)} %collective-permute-done.2.near_ref, bf16[400,256]{1,0:T(8,128)(2,1)S(1)} %collective-permute-done.3.far_ref, f32[2,320,256]{2,1,0:T(8,128)S(1)} %get-tuple-element.27.partial_ref, ...), custom_call_target="tpu_custom_call", output_to_operand_aliasing={{}: (6, {})} | custom-call | tf_op jit(solution)/shard_map/conv_edges/pallas_call | solution.py:783
  (14 shorter events, 0.1 us)
Async XLA Ops:
  7.8 33.0 %copy-start.2 = (bf16[256,1024]{1,0:T(8,128)(2,1)S(1)}, bf16[256,1024]{1,0:T(8,128)(2,1)}, u32[]{:S(2)}) copy-start(bf16[256,1024]{1,0:T(8,128)(2,1)} %mlp_in_ref.1) | copy-start | bytes 1572868
  7.8 33.0 %copy-start.3 = (bf16[1024,256]{1,0:T(8,128)(2,1)S(1)}, bf16[1024,256]{1,0:T(8,128)(2,1)}, u32[]{:S(2)}) copy-start(bf16[1024,256]{1,0:T(8,128)(2,1)} %mlp_out_ref.1) | copy-start | bytes 1572868
  7.8 33.0 %copy-start.4 = (bf16[256,768]{1,0:T(8,128)(2,1)S(1)}, bf16[256,768]{1,0:T(8,128)(2,1)}, u32[]{:S(2)}) copy-start(bf16[256,768]{1,0:T(8,128)(2,1)} %attn_in_ref.1) | copy-start | bytes 1179652
  7.8 33.0 %copy-start.5 = (bf16[256,256]{1,0:T(8,128)(2,1)S(1)}, bf16[256,256]{1,0:T(8,128)(2,1)}, u32[]{:S(2)}) copy-start(bf16[256,256]{1,0:T(8,128)(2,1)} %attn_out_ref.1) | copy-start | bytes 393220
  7.8 32.9 %copy-start.7 = (s32[1,1024]{1,0:T(1,128)S(1)}, s32[1,1024]{1,0:T(1,128)}, u32[]{:S(2)}) copy-start(s32[1,1024]{1,0:T(1,128)} %window_ref.1) | copy-start | bytes 12292
  7.8 32.9 %copy-start.10 = (f32[256]{0:T(256)S(1)}, f32[256]{0:T(256)}, u32[]{:S(2)}) copy-start(f32[256]{0:T(256)} %param.24) | copy-start | bytes 3076
  7.8 32.9 %copy-start.11 = (f32[256]{0:T(256)S(1)}, f32[256]{0:T(256)}, u32[]{:S(2)}) copy-start(f32[256]{0:T(256)} %param.27) | copy-start | bytes 3076
  54.6 25.9 %copy-start.1 = (bf16[8,8,40,256]{3,2,1,0:T(8,128)(2,1)S(1)}, bf16[8,8,40,256]{3,2,1,0:T(8,128)(2,1)}, u32[]{:S(2)}) copy-start(bf16[8,8,40,256]{3,2,1,0:T(8,128)(2,1)} %pos_ref.3) | copy-start | bytes 3932164
  54.6 25.9 %copy-start.6 = (s32[2048]{0:T(1024)S(1)}, s32[2048]{0:T(1024)}, u32[]{:S(2)}) copy-start(s32[2048]{0:T(1024)} %param.19) | copy-start | bytes 24580
  54.6 25.9 %copy-start.8 = (f32[256]{0:T(256)S(1)}, f32[256]{0:T(256)}, u32[]{:S(2)}) copy-start(f32[256]{0:T(256)} %param.30) | copy-start | bytes 3076
  54.6 25.9 %copy-start.9 = (f32[256]{0:T(256)S(1)}, f32[256]{0:T(256)}, u32[]{:S(2)}) copy-start(f32[256]{0:T(256)} %param.31) | copy-start | bytes 3076
  54.6 25.9 %copy-start.13 = (s32[1,128]{1,0:T(1,128)S(1)}, s32[1,128]{1,0:T(1,128)}, u32[]{:S(2)}) copy-start(s32[1,128]{1,0:T(1,128)} %get-tuple-element.17.starts_ref) | copy-start | bytes 1540
  80.5 7.1 %copy-start = (bf16[27,256,256]{2,1,0:T(8,128)(2,1)S(1)}, bf16[27,256,256]{2,1,0:T(8,128)(2,1)}, u32[]{:S(2)}) copy-start(bf16[27,256,256]{2,1,0:T(8,128)(2,1)} %param.32) | copy-start | bytes 10616836
  82.7 4.9 %copy-start.12 = (f32[256]{0:T(256)S(1)}, f32[256]{0:T(256)}, u32[]{:S(2)}) copy-start(f32[256]{0:T(256)} %param.33) | copy-start | bytes 3076
  82.7 7.0 %collective-permute-start.1 = (bf16[320,256]{1,0:T(8,128)(2,1)S(1)}, bf16[320,256]{1,0:T(8,128)(2,1)S(1)}, u32[]{:S(2)}, u32[]{:S(2)}) collective-permute-start(bf16[320,256]{1,0:T(8,128)(2,1)S(1)} %get-tuple-element.21.edge0_ref), channel_id=1, source_target_pairs={{1,0},{2,1},{3,2},{0,3},{5,4},{6,5},{7,6},{4,7},{9,8},{10,9},{11,1... | collective-permute-start | bytes 491528 | tf_op jit(solution)/shard_map/ppermute | solution.py:828
  84.4 6.6 %collective-permute-start = (bf16[320,256]{1,0:T(8,128)(2,1)S(1)}, bf16[320,256]{1,0:T(8,128)(2,1)S(1)}, u32[]{:S(2)}, u32[]{:S(2)}) collective-permute-start(bf16[320,256]{1,0:T(8,128)(2,1)S(1)} %get-tuple-element.22.edge1_ref), channel_id=1, source_target_pairs={{0,1},{1,2},{2,3},{3,0},{4,5},{5,6},{6,7},{7,4},{8,9},{9,10},{10,1... | collective-permute-start | bytes 491528 | tf_op jit(solution)/shard_map/ppermute | solution.py:829
  91.0 9.0 %collective-permute-start.2 = (bf16[400,256]{1,0:T(8,128)(2,1)S(1)}, bf16[400,256]{1,0:T(8,128)(2,1)S(1)}, u32[]{:S(2)}, u32[]{:S(2)}) collective-permute-start(bf16[400,256]{1,0:T(8,128)(2,1)S(1)} %get-tuple-element.24), channel_id=1, source_target_pairs={{0,4},{8,12},{16,20},{24,28},{32,36},{40,44},{48,52},{56,60},{64,6... | collective-permute-start | bytes 614408 | tf_op jit(solution)/shard_map/ppermute | solution.py:837
  91.1 8.9 %collective-permute-start.3 = (bf16[400,256]{1,0:T(8,128)(2,1)S(1)}, bf16[400,256]{1,0:T(8,128)(2,1)S(1)}, u32[]{:S(2)}, u32[]{:S(2)}) collective-permute-start(bf16[400,256]{1,0:T(8,128)(2,1)S(1)} %get-tuple-element.25), channel_id=1, source_target_pairs={{4,8},{12,16},{20,24},{28,32},{36,40},{44,48},{52,56},{60,64},{68,... | collective-permute-start | bytes 614408 | tf_op jit(solution)/shard_map/ppermute | solution.py:838
